TPU v7x, 32 devices: a whole 2x2x4 slice. The times are simulated.
32 devices in a mesh: dp: 4 (over z), fsdp: 8 (over y, x, core).
Axes of the slice: x: 2, y: 2, z: 4, core: 2. Of those that a mesh axis runs over, the one named last changes fastest.
Arguments:
- features: float32 [98304, 512], P(('dp', 'fsdp')), may hold values from -6 to 6
- cotangent: float32 [3, 98304, 256], P(None, ('dp', 'fsdp')), may hold values from -6 to 6
- counts: int32 [32], P(('dp', 'fsdp')), may hold values from 1536 to 3072, as said below
- keep: int32 [98304], P(('dp', 'fsdp')), may hold values 0 or 1
- w_in: float32 [6, 512, 256], P(None, 'fsdp'), may hold values from -0.25 to 0.25
- in_bias: float32 [6, 256], P(None, 'fsdp'), may hold values from -3 to 3
- norm_gain: float32 [6, 256], P(None, 'fsdp'), may hold values from 0.1 to 1.9
- norm_bias: float32 [6, 256], P(None, 'fsdp'), may hold values from -3 to 3
- w_out: float32 [6, 256, 256], P(None, 'fsdp'), may hold values from -0.375 to 0.375
- out_bias: float32 [6, 256], P(None, 'fsdp'), may hold values from -3 to 3
- task_gate: float32 [2, 512, 4], P(None, 'fsdp'), may hold values from -0.125 to 0.125
- shared_gate: float32 [512, 6], P('fsdp'), may hold values from -0.125 to 0.125
Outputs:
- outputs: float32 [3, 98304, 256], P(None, ('dp', 'fsdp'))
- grad_features: float32 [98304, 512], P(('dp', 'fsdp'))
- grad_w_in: float32 [6, 512, 256], P(None, 'fsdp')
- grad_in_bias: float32 [6, 256], P(None, 'fsdp')
- grad_norm_gain: float32 [6, 256], P(None, 'fsdp')
- grad_norm_bias: float32 [6, 256], P(None, 'fsdp')
- grad_w_out: float32 [6, 256, 256], P(None, 'fsdp')
- grad_out_bias: float32 [6, 256], P(None, 'fsdp')
- grad_task_gate: float32 [2, 512, 4], P(None, 'fsdp')
- grad_shared_gate: float32 [512, 6], P('fsdp')
Inputs may be any that keep to these rules, and one draw needn't show every extreme that they name: `counts`: each device's count is at least half of its 3072 slots; in every draw some device uses all of them.
All inputs are finite; a program needn't handle non-finite values. No bound on the sum of `keep` on one device may be relied on, other than what follows from the above.
Results may differ from a plain program's by a relative error of at most 0.0003.
Values sent between devices are 32-bit elements; how exact they have to be, the bound alone decides.
No kernel may reach another device: no remote copies, remote signals or barrier semaphores. Data moves between devices by JAX's collectives and lax.ppermute only.
A program may use at most 320 MiB of HBM per device.

v0:
```python
import jax
import jax.numpy as jnp
from jax import lax
from jax.sharding import PartitionSpec as P

TASKS = 2
SPEC = 2
MICRO = 3


EPSILON = 1e-05


def forward(features, w_in, in_bias, norm_gain, norm_bias, w_out, out_bias, task_gate, shared_gate):
    highest = lax.Precision.HIGHEST
    preact = jnp.einsum("bd,edh->ebh", features, w_in, precision=highest) + in_bias[:, None, :]
    active = jax.nn.silu(preact)
    centred = active - jnp.mean(active, -1, keepdims=True)
    spread = jnp.mean(centred * centred, -1, keepdims=True)
    normed = centred * lax.rsqrt(spread + EPSILON) * norm_gain[:, None, :] + norm_bias[:, None, :]
    expert = jax.nn.silu(
        jnp.einsum("ebh,ehk->ebk", normed, w_out, precision=highest) + out_bias[:, None, :]
    )
    results = []
    for index_task in range(TASKS):
        weights = jax.nn.softmax(
            jnp.dot(features, task_gate[index_task], precision=highest), axis=-1
        )
        chosen = jnp.concatenate(
            [expert[index_task * SPEC : (index_task + 1) * SPEC], expert[TASKS * SPEC :]], 0
        )
        results.append(jnp.einsum("be,ebh->bh", weights, chosen, precision=highest))
    shared_weights = jax.nn.softmax(jnp.dot(features, shared_gate, precision=highest), axis=-1)
    results.append(jnp.einsum("be,ebh->bh", shared_weights, expert, precision=highest))
    return jnp.stack(results)


def on_device(
    features,
    cotangent,
    counts,
    keep,
    w_in,
    in_bias,
    norm_gain,
    norm_bias,
    w_out,
    out_bias,
    task_gate,
    shared_gate,
):
    rows_here = features.shape[0]
    block = rows_here // MICRO
    valid = ((jnp.arange(rows_here, dtype=jnp.int32) < counts[0]) & (keep > 0)).astype(jnp.float32)
    results = []
    grad_parts = []
    totals = None
    for micro_index in range(MICRO):
        whole = (
            lax.all_gather(w_in, "fsdp", axis=1, tiled=True),
            lax.all_gather(in_bias, "fsdp", axis=1, tiled=True),
            lax.all_gather(norm_gain, "fsdp", axis=1, tiled=True),
            lax.all_gather(norm_bias, "fsdp", axis=1, tiled=True),
            lax.all_gather(w_out, "fsdp", axis=1, tiled=True),
            lax.all_gather(out_bias, "fsdp", axis=1, tiled=True),
            lax.all_gather(task_gate, "fsdp", axis=1, tiled=True),
            lax.all_gather(shared_gate, "fsdp", axis=0, tiled=True),
        )
        lower = micro_index * block
        feat = features[lower : lower + block]
        cot = cotangent[:, lower : lower + block] * valid[None, lower : lower + block, None]
        result, pull = jax.vjp(forward, feat, *whole)
        pulled = pull(cot)
        results.append(result)
        grad_parts.append(pulled[0])
        grads = tuple(pulled[1:])
        owned = (
            lax.psum_scatter(grads[0], "fsdp", scatter_dimension=1, tiled=True),
            lax.psum_scatter(grads[1], "fsdp", scatter_dimension=1, tiled=True),
            lax.psum_scatter(grads[2], "fsdp", scatter_dimension=1, tiled=True),
            lax.psum_scatter(grads[3], "fsdp", scatter_dimension=1, tiled=True),
            lax.psum_scatter(grads[4], "fsdp", scatter_dimension=1, tiled=True),
            lax.psum_scatter(grads[5], "fsdp", scatter_dimension=1, tiled=True),
            lax.psum_scatter(grads[6], "fsdp", scatter_dimension=1, tiled=True),
            lax.psum_scatter(grads[7], "fsdp", scatter_dimension=0, tiled=True),
        )
        totals = owned if micro_index == 0 else jax.tree.map(jnp.add, totals, owned)
    summed = lax.psum(
        (totals[0], totals[1], totals[2], totals[3], totals[4], totals[5], totals[6], totals[7]),
        "dp",
    )
    outputs = jnp.concatenate(results, 1)
    grad_features = jnp.concatenate(grad_parts, 0)
    return (
        outputs,
        grad_features,
        summed[0],
        summed[1],
        summed[2],
        summed[3],
        summed[4],
        summed[5],
        summed[6],
        summed[7],
    )


def solution(mesh):
    placed = (
        P(("dp", "fsdp"), None),
        P(None, ("dp", "fsdp"), None),
        P(("dp", "fsdp")),
        P(("dp", "fsdp")),
        P(None, "fsdp", None),
        P(None, "fsdp"),
        P(None, "fsdp"),
        P(None, "fsdp"),
        P(None, "fsdp", None),
        P(None, "fsdp"),
        P(None, "fsdp", None),
        P("fsdp", None),
    )
    return jax.shard_map(
        on_device,
        mesh=mesh,
        in_specs=placed,
        out_specs=(
            P(None, ("dp", "fsdp"), None),
            P(("dp", "fsdp"), None),
            P(None, "fsdp", None),
            P(None, "fsdp"),
            P(None, "fsdp"),
            P(None, "fsdp"),
            P(None, "fsdp", None),
            P(None, "fsdp"),
            P(None, "fsdp", None),
            P("fsdp", None),
        ),
        check_vma=False,
    )
```

profile of v0, /device:TPU:0, one launch (start us, length us, event | category | flops | bytes accessed | tf_op | source)
XLA Modules:
  0.0 858.2 jit_solution(3420362101305559828)
XLA Ops:
  124.7 22.5 %fusion.83 = f32[6,256,1024]{2,1,0:T(8,128)S(1)} fusion(f32[6,512,256]{2,1,0:T(8,128)} %all-gather.8.cloned.1.call-done, f32[3072,512]{1,0:T(8,128)} %param.12), kind=kOutput, calls=%fused_computation.161 | convolution fusion | flops 9663676416 | bytes 11534336 | tf_op jit(solution)/shard_map/jvp(bd,edh->ebh)/dot_general | solution.py:16
  147.3 25.7 %fusion.196 = (f32[6,1024]{1,0:T(8,128)S(1)}, f32[6,1024]{1,0:T(8,128)S(1)}, f32[6,256,1024]{2,1,0:T(8,128)S(1)}) fusion(f32[6,256]{1,0:T(8,128)S(1)} %bitcast.418, f32[6,256,1024]{2,1,0:T(8,128)S(1)} %fusion.83, f32[6,512,256]{2,1,0:T(8,128)S(1)} %copy-done.6, f32[3072,512]{1,0:T(8,128)} %param.12), kind=kOutput, calls=%fused_computation.322 | convolution fusion | flops 9682538496 | bytes 17881088 | tf_op jit(solution)/shard_map/jvp(bd,edh->ebh)/dot_general | solution.py:16
  173.0 29.1 %fusion.195 = (f32[6,1024]{1,0:T(8,128)S(1)}, f32[6,1024]{1,0:T(8,128)S(1)}, f32[6,1024]{1,0:T(8,128)S(1)}, f32[6,256,1024]{2,1,0:T(8,128)}) fusion(f32[6,256]{1,0:T(8,128)S(1)} %bitcast.419, f32[6,1024]{1,0:T(8,128)S(1)} %broadcast_multiply_fusion, f32[6,256,1024]{2,1,0:T(8,128)S(1)} %fusion.83, f32[6,1024]{1,0:T(8,128)S(1)} %broadcast_multiply_fusion.1, ...), kind=kOutput, calls=%fused_computation.321 | convolution fusion | flops 9698260992 | bytes 24246272 | tf_op jit(solution)/shard_map/jvp(bd,edh->ebh)/dot_general | solution.py:16
  202.3 14.3 %fusion.50 = f32[6,1024,256]{1,2,0:T(8,128)} fusion(f32[6,256,256]{2,1,0:T(8,128)} %all-gather.10.cloned.1.call-done, f32[6,1024]{1,0:T(8,128)S(1)} %fusion.169, f32[6,1024]{1,0:T(8,128)S(1)} %broadcast_multiply_fusion, f32[6,256]{1,0:T(8,128)S(1)} %bitcast.455, f32[6,256]{1,0:T(8,128)S(1)} %bitcast.433, f32[6,256,1024]{2,1,0:T(8,128)} %copy-done, ...), kind=kOutput, calls=%fused_computation.100 | convolution fusion | flops 4845993984 | bytes 14223360 | tf_op jit(solution)/shard_map/jvp(ebh,ehk->ebk)/dot_general | solution.py:22
  216.6 16.0 %multiply_reduce_fusion.1 = (f32[1024,6]{0,1:T(8,128)S(1)}, f32[6,1024,256]{1,2,0:T(8,128)}, f32[1024,6]{0,1:T(8,128)S(1)}, f32[6,1024,256]{1,2,0:T(8,128)}, f32[6,1024,256]{1,2,0:T(8,128)}) fusion(f32[1024,256]{0,1:T(8,128)S(1)} %copy-done.29, f32[6,256]{1,0:T(8,128)S(1)} %bitcast.447, f32[6,1024,256]{1,2,0:T(8,128)} %fusion.50, ...), kind=kOutput, calls=%fused_computation.72 | convolution fusion | flops 4868001792 | bytes 35250176 | tf_op jit(solution)/shard_map/jvp(ebh,ehk->ebk)/dot_general | solution.py:22
  257.2 13.9 %fusion.202 = (f32[6,256]{1,0:T(8,128)}, f32[6,1024,256]{1,2,0:T(8,128)}, f32[6,256]{1,0:T(8,128)}, f32[6,1024,256]{1,2,0:T(8,128)S(1)}) fusion(f32[6,1024,256]{1,2,0:T(8,128)} %fusion.50, f32[6,256]{1,0:T(8,128)S(1)} %bitcast.448, f32[2,1024,256]{1,2,0:T(8,128)S(1)} %get-tuple-element.96, f32[2,1024,256]{1,2,0:T(8,128)S(1)} %get-tuple-element.95, ...), kind=kLoop, calls=%fused_computation.326 | loop fusion | flops 50328576 | bytes 44107776 | tf_op jit(solution)/shard_map/transpose(jvp())/reduce_sum | solution.py:22
  280.5 13.1 %fusion.229 = (f32[6,256]{1,0:T(8,128)}, f32[6,1024,256]{2,1,0:T(8,128)}) fusion(f32[6,1024,256]{1,2,0:T(8,128)S(1)} %get-tuple-element.136, f32[6,256,256]{2,1,0:T(8,128)S(1)} %copy-done.14), kind=kOutput, calls=%fused_computation.349 | convolution fusion | flops 4833409536 | bytes 14161920 | tf_op jit(solution)/shard_map/transpose(jvp(ebh,ehk->ebk))/dot_general | solution.py:22
  300.3 14.3 %fusion.227 = (f32[6,256]{1,0:T(8,128)}, f32[6,1024,256]{2,1,0:T(8,128)}) fusion(f32[6,1024,256]{1,2,0:T(8,128)} %get-tuple-element.73, f32[6,256,256]{2,1,0:T(8,128)S(1)} %copy-done.14), kind=kOutput, calls=%fused_computation.347 | convolution fusion | flops 4833409536 | bytes 14161920 | tf_op jit(solution)/shard_map/transpose(jvp(ebh,ehk->ebk))/dot_general | solution.py:22
  321.3 16.6 %multiply_reduce_fusion.10 = (f32[6,1024]{1,0:T(8,128)}, f32[6,1024]{1,0:T(8,128)S(1)}, f32[6,1024]{1,0:T(8,128)S(1)}) fusion(f32[6,1024,256]{1,2,0:T(8,128)} %copy.111, f32[6,1024]{1,0:T(8,128)S(1)} %broadcast_multiply_fusion.1, f32[6,256]{1,0:T(8,128)S(1)} %bitcast.436, f32[6,256,1024]{2,1,0:T(8,128)} %copy-done.1, f32[6,256]{1,0:T(8,128)S(1)} %bitcast.423, ...), kind=kLoop, calls=%fused_computation.81 | loop fusion | flops 40876032 | bytes 31617024 | tf_op jit(solution)/shard_map/transpose(jvp())/reduce_sum | solution.py:20
  338.6 11.6 %multiply_reduce_fusion.2 = (f32[1024,6]{0,1:T(8,128)S(1)}, f32[6,1024,256]{1,2,0:T(8,128)S(1)}, f32[6,1024,256]{1,2,0:T(8,128)}) fusion(f32[1024,256]{0,1:T(8,128)S(1)} %copy-done.26, f32[6,256]{1,0:T(8,128)S(1)} %bitcast.449, f32[6,256,256]{2,1,0:T(8,128)S(1)} %copy-done.15, f32[6,256]{1,0:T(8,128)S(1)} %bitcast.458, f32[6,256]{1,0:T(8,128)S(1)} %bitcast.437, ...), kind=kOutput, calls=%fused_computation.73 | convolution fusion | flops 4856997888 | bytes 21594112 | tf_op jit(solution)/shard_map/jvp(ebh,ehk->ebk)/dot_general | solution.py:22
  375.3 12.9 %fusion.228 = (f32[6,256]{1,0:T(8,128)}, f32[6,1024,256]{2,1,0:T(8,128)}) fusion(f32[6,1024,256]{1,2,0:T(8,128)S(1)} %get-tuple-element.71, f32[6,256,256]{2,1,0:T(8,128)S(1)} %copy-done.15), kind=kOutput, calls=%fused_computation.348 | convolution fusion | flops 4833409536 | bytes 14161920 | tf_op jit(solution)/shard_map/transpose(jvp(ebh,ehk->ebk))/dot_general | solution.py:22
  395.1 18.3 %multiply_reduce_fusion.11 = (f32[6,1024]{1,0:T(8,128)S(1)}, f32[6,1024]{1,0:T(8,128)S(1)}, f32[6,1024]{1,0:T(8,128)S(1)}) fusion(f32[6,1024,256]{1,2,0:T(8,128)} %copy.105, f32[6,256]{1,0:T(8,128)S(1)} %bitcast.439, f32[6,1024]{1,0:T(8,128)S(1)} %broadcast_multiply_fusion.2, f32[6,256,1024]{2,1,0:T(8,128)} %get-tuple-element.140, ...), kind=kLoop, calls=%fused_computation.82 | loop fusion | flops 51886080 | bytes 38006784 | tf_op jit(solution)/shard_map/transpose(jvp())/reduce_sum | solution.py:20
  413.5 16.3 %fusion.9 = (f32[6,256,1024]{2,1,0:T(8,128)}, f32[6,256,1024]{2,1,0:T(8,128)}) fusion(f32[6,1024,256]{1,2,0:T(8,128)S(1)} %bitcast.371, f32[6,256,1024]{2,1,0:T(8,128)} %copy-done.1, f32[6,1024]{1,0:T(8,128)S(1)} %negate_multiply_fusion.1, f32[6,1024]{1,0:T(8,128)S(1)} %multiply_multiply_fusion.1, f32[6,1024]{1,0:T(8,128)S(1)} %broadcast_multiply_fusion.1, ...), kind=kLoop, calls=%fused_computation.25 | loop fusion | flops 56623104 | bytes 37957632 | tf_op jit(solution)/shard_map/transpose(jvp(jit(silu)))/add_any | solution.py:17
  429.9 17.0 %multiply_reduce_fusion.6 = (f32[6,256]{1,0:T(8,128)}, f32[6,256]{1,0:T(8,128)}, f32[6,256]{1,0:T(8,128)}, f32[6,256]{1,0:T(8,128)}, f32[6,1024]{1,0:T(8,128)S(1)}) fusion(f32[6,1024,256]{1,2,0:T(8,128)S(1)} %bitcast.373, f32[6,1024]{1,0:T(8,128)S(1)} %copy-done.71, f32[6,1024]{1,0:T(8,128)S(1)} %broadcast_multiply_fusion, f32[6,256,1024]{2,1,0:T(8,128)S(1)} %bitcast.375, ...), kind=kLoop, calls=%fused_computation.77 | loop fusion | flops 88068096 | bytes 38080512 | tf_op jit(solution)/shard_map/transpose(jvp())/reduce_sum | solution.py:20
  457.2 12.0 %fusion.85 = f32[6,256,512]{2,1,0:T(8,128)} fusion(f32[6,256,1024]{2,1,0:T(8,128)S(1)} %bitcast.389, f32[3072,512]{1,0:T(8,128)S(1)} %bitcast.369), kind=kOutput, calls=%fused_computation.163 | convolution fusion | flops 9663676416 | bytes 11534336 | tf_op jit(solution)/shard_map/transpose(jvp(bd,edh->ebh))/dot_general | solution.py:16
  488.2 19.7 %add_bitcast_fusion = f32[6,512,256]{1,2,0:T(8,128)} fusion(f32[6,256,512]{2,1,0:T(8,128)S(1)} %fusion.81, f32[6,256,512]{2,1,0:T(8,128)} %fusion.85, f32[3072,512]{1,0:T(8,128)} %param.12, f32[6,1024,256]{1,2,0:T(8,128)} %copy.105, f32[6,256,1024]{2,1,0:T(8,128)} %get-tuple-element.140, f32[6,1024]{1,0:T(8,128)S(1)} %negate_multiply_fusion.2, ...), kind=kOutput, calls=%fused_computation.128 | convolution fusion | flops 9693560832 | bytes 24227840 | tf_op jit(solution)/shard_map/transpose(jvp(bd,edh->ebh))/dot_general | solution.py:16
  634.8 23.2 %bitcast_add_fusion.3 = f32[1024,512]{1,0:T(8,128)} fusion(f32[1024,512]{1,0:T(8,128)S(1)} %copy-done.22, f32[1024,512]{1,0:T(8,128)S(1)} %copy-done.21, f32[1024,512]{1,0:T(8,128)S(1)} %copy-done.23, f32[6,256,1024]{2,1,0:T(8,128)} %get-tuple-element.131, f32[6,512,256]{2,1,0:T(8,128)S(1)} %copy-done.7), kind=kOutput, calls=%fused_computation.156 | convolution fusion | flops 9665249280 | bytes 17825792 | tf_op jit(solution)/shard_map/transpose(jvp(bd,edh->ebh))/dot_general | solution.py:16
  658.1 26.9 %bitcast_add_fusion.5 = f32[1024,512]{1,0:T(8,128)} fusion(f32[1024,512]{1,0:T(8,128)S(1)} %copy-done.41, f32[1024,512]{1,0:T(8,128)S(1)} %copy-done.43, f32[1024,512]{1,0:T(8,128)S(1)} %copy-done.42, f32[6,512,256]{2,1,0:T(8,128)S(1)} %copy-done.7, f32[6,1024,256]{1,2,0:T(8,128)} %copy.105, f32[6,256,1024]{2,1,0:T(8,128)S(1)} %bitcast.379, ...), kind=kOutput, calls=%fused_computation.158 | convolution fusion | flops 9693560832 | bytes 24227840 | tf_op jit(solution)/shard_map/transpose(jvp(bd,edh->ebh))/dot_general | solution.py:16
  687.1 23.9 %bitcast_add_fusion.4 = f32[1024,512]{1,0:T(8,128)S(1)} fusion(f32[1024,512]{1,0:T(8,128)} %fusion.190, f32[1024,512]{1,0:T(8,128)S(1)} %fusion.185, f32[1024,512]{1,0:T(8,128)} %fusion.189, f32[6,256,1024]{2,1,0:T(8,128)} %get-tuple-element.130, f32[6,512,256]{2,1,0:T(8,128)} %all-gather.8.cloned.1.call-done), kind=kOutput, calls=%fused_computation.157 | convolution fusion | flops 9665249280 | bytes 17825792 | tf_op jit(solution)/shard_map/transpose(jvp(bd,edh->ebh))/dot_general | solution.py:16
  716.8 11.9 %reduce-scatter.31.cloned.1.call-done = f32[32,6]{1,0:T(8,128)} async-done(((f32[256,6]{1,0:T(8,128)}), f32[32,6]{1,0:T(8,128)}) %reduce-scatter.31.cloned.1.call-update) | async-done | bytes 784
  729.5 36.2 %reduce-scatter.35.cloned.1.call-done = f32[64,6]{1,0:T(8,128)} async-done(((f32[512,6]{1,0:T(8,128)}), f32[64,6]{1,0:T(8,128)}) %reduce-scatter.35.cloned.1.call-update) | async-done | bytes 1552
  766.5 36.3 %reduce-scatter.33.cloned.1.call-done = f32[64,8]{1,0:T(8,128)} async-done(((f32[512,8]{1,0:T(8,128)}), f32[64,8]{1,0:T(8,128)}) %reduce-scatter.33.cloned.1.call-update) | async-done | bytes 2064
  803.7 19.8 %all-reduce.18 = (f32[6,32]{1,0:T(8,128)}, f32[6,32]{1,0:T(8,128)}, f32[6,32]{1,0:T(8,128)}, f32[6,32]{1,0:T(8,128)}, f32[2,64,4]{1,2,0:T(4,128)}, /*index=5*/f32[64,6]{0,1:T(8,128)}) all-reduce(f32[6,32]{1,0:T(8,128)S(1)} %copy.251, f32[6,32]{1,0:T(8,128)S(1)} %copy.253, ...), channel_id=1, replica_groups=mesh['dp'=4,'fsdp'=8] {'dp'}, use_global_device_ids=true, to_apply=%region_49.50 | all-reduce | flops 1664 | bytes 13312 | tf_op jit(solution)/shard_map/psum | solution.py:88
  823.6 24.3 %all-reduce.22.cloned.1.call-done = (f32[6,64,256]{2,0,1:T(8,128)}, f32[6,32,256]{2,1,0:T(8,128)}) async-done(((f32[6,64,256]{2,0,1:T(8,128)}, f32[6,32,256]{2,1,0:T(8,128)}), (f32[6,64,256]{2,0,1:T(8,128)}, f32[6,32,256]{2,1,0:T(8,128)})) %all-reduce.22.cloned.1.call-update) | async-done | bytes 589840 | tf_op jit(solution)/shard_map/psum | solution.py:88
  (725 shorter events, 364.3 us)
Async XLA Ops:
  7.2 117.5 %all-gather.8.cloned.1.call-start = ((), (), s32[]{:S(2)}) async-start(), calls=%async_computation.8 | async-start | bytes 3538944 | tf_op jit(solution)/shard_map/all_gather | solution.py:60
  7.9 194.3 %all-gather.10.cloned.1.call-start = ((), (), s32[]{:S(2)}) async-start(), calls=%async_computation.9 | async-start | bytes 1769472 | tf_op jit(solution)/shard_map/all_gather | solution.py:64
  8.7 678.3 %reduce-scatter.23.cloned.1.call-start = ((), (), s32[]{:S(2)}) async-start(), calls=%async_computation.11 | async-start | bytes 1769472 | tf_op jit(solution)/shard_map/reduce_scatter | solution.py:82
  41.4 214.5 %copy-start.49 = (f32[1024,6]{0,1:T(8,128)}, f32[1024,6]{0,1:T(8,128)S(1)}, u32[]{:S(2)}) copy-start(f32[1024,6]{0,1:T(8,128)S(1)} %get-tuple-element.143) | copy-start | bytes 73732
  41.4 214.5 %copy-start.159 = (f32[1024]{0:T(1024)}, f32[1024]{0:T(1024)S(1)}, u32[]{:S(2)}) copy-start(f32[1024]{0:T(1024)S(1)} %get-tuple-element.142) | copy-start | bytes 12292
  44.9 211.6 %copy-start.45 = (f32[1024,6]{0,1:T(8,128)}, f32[1024,6]{0,1:T(8,128)S(1)}, u32[]{:S(2)}) copy-start(f32[1024,6]{0,1:T(8,128)S(1)} %get-tuple-element.149) | copy-start | bytes 73732
  45.0 211.6 %copy-start.152 = (f32[1024]{0:T(1024)}, f32[1024]{0:T(1024)S(1)}, u32[]{:S(2)}) copy-start(f32[1024]{0:T(1024)S(1)} %get-tuple-element.148) | copy-start | bytes 12292
  58.7 186.3 %copy-start.114 = (f32[1024,4]{0,1:T(4,128)}, f32[1024,4]{0,1:T(4,128)S(1)}, u32[]{:S(2)}) copy-start(f32[1024,4]{0,1:T(4,128)S(1)} %broadcast_divide_fusion) | copy-start | bytes 49156
  59.4 188.9 %copy-start.121 = (f32[1024,4]{0,1:T(4,128)}, f32[1024,4]{0,1:T(4,128)S(1)}, u32[]{:S(2)}) copy-start(f32[1024,4]{0,1:T(4,128)S(1)} %broadcast_divide_fusion.3) | copy-start | bytes 49156
  60.0 192.3 %copy-start.116 = (f32[1024,4]{0,1:T(4,128)}, f32[1024,4]{0,1:T(4,128)S(1)}, u32[]{:S(2)}) copy-start(f32[1024,4]{0,1:T(4,128)S(1)} %broadcast_divide_fusion.2) | copy-start | bytes 49156
  87.5 431.8 %copy-start.72 = (f32[256,6]{0,1:T(8,128)}, f32[256,6]{0,1:T(8,128)S(1)}, u32[]{:S(2)}) copy-start(f32[256,6]{0,1:T(8,128)S(1)} %reshape.244) | copy-start | bytes 18436
  95.9 269.9 %copy-start.218 = (f32[256,6]{0,1:T(8,128)}, f32[256,6]{0,1:T(8,128)S(1)}, u32[]{:S(2)}) copy-start(f32[256,6]{0,1:T(8,128)S(1)} %reshape.248) | copy-start | bytes 18436
  105.3 414.0 %copy-start.74 = (f32[256,6]{0,1:T(8,128)}, f32[256,6]{0,1:T(8,128)S(1)}, u32[]{:S(2)}) copy-start(f32[256,6]{0,1:T(8,128)S(1)} %reshape.246) | copy-start | bytes 18436
  107.9 148.0 %copy-start.178 = (f32[1024]{0:T(1024)}, f32[1024]{0:T(1024)S(1)}, u32[]{:S(2)}) copy-start(f32[1024]{0:T(1024)S(1)} %fusion.175) | copy-start | bytes 12292
  107.9 148.6 %copy-start.161 = (f32[1024]{0:T(1024)}, f32[1024]{0:T(1024)S(1)}, u32[]{:S(2)}) copy-start(f32[1024]{0:T(1024)S(1)} %fusion.173) | copy-start | bytes 12292
  241.7 237.2 %copy-start.106 = (f32[1024,4]{0,1:T(4,128)}, f32[1024,4]{0,1:T(4,128)S(1)}, u32[]{:S(2)}) copy-start(f32[1024,4]{0,1:T(4,128)S(1)} %get-tuple-element.120) | copy-start | bytes 49156
  478.9 208.1 %reduce-scatter.21.cloned.1.call-start = ((), (), s32[]{:S(2)}) async-start(), calls=%async_computation.10 | async-start | bytes 4718592 | tf_op jit(solution)/shard_map/reduce_scatter | solution.py:78
  528.7 185.7 %reduce-scatter.25.cloned.1.call-start = ((), (), s32[]{:S(2)}) async-start(), calls=%async_computation.12 | async-start | bytes 147456
  585.8 129.4 %reduce-scatter.27.cloned.1.call-start = ((), (), s32[]{:S(2)}) async-start(), calls=%async_computation.13 | async-start | bytes 147456
  589.4 126.6 %reduce-scatter.29.cloned.1.call-start = ((), (), s32[]{:S(2)}) async-start(), calls=%async_computation.14 | async-start | bytes 147456
  593.0 135.7 %reduce-scatter.31.cloned.1.call-start = ((), (), s32[]{:S(2)}) async-start(), calls=%async_computation.15 | async-start | bytes 147456
  596.7 169.0 %reduce-scatter.35.cloned.1.call-start = ((), (), s32[]{:S(2)}) async-start(), calls=%async_computation.17 | async-start | bytes 294912
  603.5 199.2 %reduce-scatter.33.cloned.1.call-start = ((), (), s32[]{:S(2)}) async-start(), calls=%async_computation.16 | async-start | bytes 294912
  625.1 222.8 %all-reduce.22.cloned.1.call-start = ((), (), s32[]{:S(2)}) async-start(), calls=%async_computation.18 | async-start | bytes 1441792 | tf_op jit(solution)/shard_map/psum | solution.py:88
  (240 other events, 3593.4 us)
Sparse Core Ops, SparseCore 0:
  9.9 35.0 all-gather.7
  46.9 25.6 all-gather.9
  479.0 38.7 reduce-scatter.22
  528.8 51.6 reduce-scatter.20
  585.9 33.4 reduce-scatter.24
  622.2 33.3 reduce-scatter.26
  658.9 33.3 reduce-scatter.28
  695.3 33.3 reduce-scatter.30
  732.1 33.5 reduce-scatter.34
  769.1 33.6 reduce-scatter.32
  805.4 42.4 all-reduce.21
where the time goes:
time: 864 us; the launch traced here: 858 us
  matrix products  388 us (45%)
  other arithmetic  157 us (18%)
  waiting for transfers between devices  110 us (13%)
  local copies, waits for them, and re-layouts  108 us (12%)
  blocking collectives  75.1 us (9%)
  between operations  18 us (2%)
    dot_general x9, matrix products, forward(): jnp.einsum('bd,edh->ebh', features, w_in, precision=highest)  193 us
    dot_general x9, matrix products, forward(): jnp.einsum('ebh,ehk->ebk', normed, w_out, precision=highest)  111 us
    unnamed x17, waiting for transfers between devices  85.9 us
    reduce_sum x4, other arithmetic, forward(): centred * lax.rsqrt(spread + EPSILON) * norm_gain[:, None, :]  61.2 us
    dot_general x18, matrix products, forward(): jnp.dot(features, task_gate[index_task], precision=highest)  57.2 us
    unnamed x537, local copies, waits for them, and re-layouts  43.8 us
    dot_general x9, matrix products, forward(): jnp.dot(features, shared_gate, precision=highest)  27.1 us
    psum x1, waiting for transfers between devices, on_device(): lax.psum((totals[0], totals[1], totals[2], totals[3], totals[4], totals[5...  24.3 us
  transfers between devices with their start and end apart: 11, of which 4 were waited for; matrix products, arithmetic and copies ran while one was open for 43% of the time, Pallas kernels for 0%

commit v1 on v0

v1 whole, which is shorter than its diff:
```python
import functools

import jax
import jax.numpy as jnp
from jax import lax
from jax.experimental import pallas as pl
from jax.experimental.pallas import tpu as pltpu
from jax.sharding import PartitionSpec as P

TASKS = 2
SPEC = 2
SHARED = 2
EXPERTS = 6
EPSILON = 1e-05
GROUPS = ((0, 1), (2, 3), (4, 5))
TILE = 512
STEP = 16
LANES = 128
GATES = 16
F32 = jnp.float32
BF16 = jnp.bfloat16
VMEM_BYTES = 58 << 20

NN = (((1,), (0,)), ((), ()))
NT = (((1,), (1,)), ((), ()))
TN = (((0,), (0,)), ((), ()))


def uses(expert):
    if expert >= TASKS * SPEC:
        shared = expert - TASKS * SPEC
        first = [(t, t * (SPEC + SHARED) + SPEC + shared) for t in range(TASKS)]
    else:
        t = expert // SPEC
        first = [(t, t * (SPEC + SHARED) + expert % SPEC)]
    return first + [(TASKS, TASKS * (SPEC + SHARED) + expert)]


def halves(v):
    high = v.astype(BF16)
    return high, (v - high.astype(F32)).astype(BF16)


def dot(a, b, dims):
    return lax.dot_general(a, b, dims, preferred_element_type=F32)


def dot3(a_high, a_low, b_high, b_low, dims):
    return dot(a_high, b_high, dims) + dot(a_low, b_high, dims) + dot(a_high, b_low, dims)


def column(row):
    return jnp.broadcast_to(row, (LANES, row.shape[1])).T


def wide(block, width):
    return jnp.concatenate([block] * (width // LANES), axis=1)


def prep_kernel(x_ref, c_ref, valid_ref, xh_ref, xl_ref, ct_ref):
    depth = x_ref.shape[1]
    high, low = halves(x_ref[...].T)
    xh_ref[0:depth] = high
    xh_ref[depth:] = jnp.ones((xh_ref.shape[0] - depth, xh_ref.shape[1]), BF16)
    xl_ref[...] = low
    valid = valid_ref[...]
    for o in range(c_ref.shape[0]):
        ct_ref[o] = c_ref[o].T * valid


def prep(features, cotangent, valid):
    rows, depth = features.shape
    outs, _, units = cotangent.shape
    return pl.pallas_call(
        prep_kernel,
        grid=(rows // TILE,),
        in_specs=[
            pl.BlockSpec((TILE, depth), lambda i: (i, 0)),
            pl.BlockSpec((outs, TILE, units), lambda i: (0, i, 0)),
            pl.BlockSpec((1, TILE), lambda i: (0, i)),
        ],
        out_specs=[
            pl.BlockSpec((depth + STEP, TILE), lambda i: (0, i)),
            pl.BlockSpec((depth, TILE), lambda i: (0, i)),
            pl.BlockSpec((outs, units, TILE), lambda i: (0, 0, i)),
        ],
        out_shape=[
            jax.ShapeDtypeStruct((depth + STEP, rows), BF16),
            jax.ShapeDtypeStruct((depth, rows), BF16),
            jax.ShapeDtypeStruct((outs, units, rows), F32),
        ],
        compiler_params=pltpu.CompilerParams(vmem_limit_bytes=VMEM_BYTES),
        cost_estimate=pl.CostEstimate(flops=0, bytes_accessed=32000000, transcendentals=0),
    )(features, cotangent, valid)


def softmax_rows(v):
    e = jnp.exp(v - jnp.max(v, axis=0, keepdims=True))
    return e / jnp.sum(e, axis=0, keepdims=True)


def expert_kernel(group, first, last, n_in, *refs):
    names = ["core", "own", "other", "small", "xh", "xl", "ct"]
    names += ["gates"] if first else ["prob"]
    if last:
        names += [f"dp{k}" for k in range(len(GROUPS) - 1)]
    names += ["dah", "dal", "ex", "keep", "send", "wih", "wil"]
    if first:
        names += ["prob"]
    names += ["dl", "gate_keep", "gate_send"] if last else ["dp"]
    names += ["win_t", "win_t_low", "wp", "wp_low", "wp_t", "wp_t_low", "b_in", "b_out", "acc_w", "acc_g"]
    names += ["h", "u", "a", "xhat", "h2", "g", "xhh", "xhl", "dzh", "dzl"]
    if last:
        names += ["all_dp", "acc_gate"]
    r = dict(zip(names, refs, strict=True))
    step = pl.program_id(0)
    count = len(group)
    units = r["acc_w"].shape[2]
    depth = r["xl"].shape[0]
    pairs = r["own"].shape[0]
    devices = 2 * pairs
    rows_in, rows_out = depth // devices, units // devices
    rows_all = rows_in + rows_out
    core = r["core"][0]
    tile = r["xl"].shape[1]
    chunks = [slice(k, k + STEP) for k in range(0, units, STEP)]

    @pl.when(step == 0)
    def _():
        for l, e in enumerate(group):
            base = l * rows_all
            for q in range(pairs):
                for src, at in ((r["own"], core), (r["other"], 1 - core)):
                    place = q * 2 + at
                    r["acc_w"][l, pl.ds(place * rows_in, rows_in)] = src[q, base : base + rows_in]
                    r["acc_g"][l, pl.ds(place * rows_out, rows_out)] = src[
                        q, base + rows_in : base + rows_all
                    ]
            w_in = r["acc_w"][l, 0:depth]
            high, low = halves(w_in)
            r["wih"][l] = high
            r["wil"][l] = low
            high, low = halves((0.5 * w_in).T)
            r["win_t"][l, 0:units] = high
            r["win_t_low"][l, 0:units] = low
            w_out = r["acc_g"][l, 0:units]
            b_in, gain, shift, b_out = (r["small"][k * EXPERTS + e : k * EXPERTS + e + 1] for k in range(4))
            scaled = w_out * wide(column(gain), units)
            high, low = halves(scaled)
            r["wp"][l] = high
            r["wp_low"][l] = low
            high, low = halves((0.5 * scaled).T)
            r["wp_t"][l] = high
            r["wp_t_low"][l] = low
            b_out = b_out + jnp.sum(w_out * wide(column(shift), units), axis=0, keepdims=True)
            r["b_in"][l] = column(0.5 * b_in)
            r["b_out"][l] = column(0.5 * b_out)
            r["xhh"][l, units:] = jnp.ones((STEP, tile), BF16)
        if first:
            high, low = halves(r["gates"][...])
            r["win_t"][0, units:] = high
            r["win_t_low"][0, units:] = low
        r["acc_w"][...] = jnp.zeros_like(r["acc_w"])
        r["acc_g"][...] = jnp.zeros_like(r["acc_g"])
        if last:
            r["acc_gate"][...] = jnp.zeros_like(r["acc_gate"])

    stats = {}

    def project_in(l):
        top = units + (GATES if first and l == 0 else 0)
        r["h"][l, 0:top] = dot3(
            r["win_t"][l, 0:top], r["win_t_low"][l, 0:top], r["xh"][0:depth], r["xl"][...], NN
        )

    def gate_weights():
        z = r["h"][0, units:]
        for lower, upper in ((0, 4), (4, 8), (8, 14)):
            r["prob"][lower:upper] = softmax_rows(z[lower:upper])
        r["prob"][14:16] = jnp.zeros((2, tile), F32)

    def normalise(l):
        total = jnp.zeros((STEP, tile), F32)
        for c in chunks:
            h = r["h"][l, c] + wide(r["b_in"][l, c], tile)
            u = 1.0 + jnp.tanh(h)
            a = h * u
            r["u"][l, c] = u
            r["a"][l, c] = a
            total = total + a
        mean = jnp.sum(total, axis=0, keepdims=True) * (1.0 / units)
        total = jnp.zeros((STEP, tile), F32)
        for c in chunks:
            d = r["a"][l, c] - mean
            total = total + d * d
        scale = lax.rsqrt(jnp.sum(total, axis=0, keepdims=True) * (1.0 / units) + EPSILON)
        stats[l] = scale
        for c in chunks:
            x = (r["a"][l, c] - mean) * scale
            r["xhat"][l, c] = x
            r["xhh"][l, c], r["xhl"][l, c] = halves(x)

    def project_out(l):
        r["h2"][l] = dot3(r["wp_t"][l], r["wp_t_low"][l], r["xhh"][l, 0:units], r["xhl"][l], NN)

    def combine(l):
        taken = uses(group[l])
        prob = [0.5 * r["prob"][row : row + 1] for _, row in taken]
        sums = [jnp.zeros((STEP, tile), F32) for _ in taken]
        for c in chunks:
            h = r["h2"][l, c] + wide(r["b_out"][l, c], tile)
            u = 1.0 + jnp.tanh(h)
            ex = h * u
            r["ex"][l * units + c.start : l * units + c.stop] = ex
            slope = u + ex * (2.0 - u)
            d = None
            for k, (o, _) in enumerate(taken):
                cot = r["ct"][o, c]
                sums[k] = sums[k] + cot * ex
                term = prob[k] * cot
                d = term if d is None else d + term
            r["dzh"][l, c], r["dzl"][l, c] = halves(d * slope)
        for k, (_, row) in enumerate(taken):
            value = jnp.sum(sums[k], axis=0, keepdims=True)
            if last:
                r["all_dp"][row : row + 1] = value
            else:
                at = l * len(taken) + k
                r["dp"][at : at + 1] = value

    def back_out(l):
        r["g"][l] = dot3(r["wp"][l], r["wp_low"][l], r["dzh"][l], r["dzl"][l], NN)

    def grad_out(l):
        r["acc_g"][l] += dot(r["xhh"][l], r["dzh"][l], NT) + dot(r["xhh"][l], r["dzl"][l], NT)
        r["acc_g"][l, 0:units] += dot(r["xhl"][l], r["dzh"][l], NT)

    def back_norm(l):
        total, along = jnp.zeros((STEP, tile), F32), jnp.zeros((STEP, tile), F32)
        for c in chunks:
            g = r["g"][l, c]
            total = total + g
            along = along + g * r["xhat"][l, c]
        mean = jnp.sum(total, axis=0, keepdims=True) * (1.0 / units)
        along = jnp.sum(along, axis=0, keepdims=True) * (1.0 / units)
        scale = 0.5 * stats[l]
        for c in chunks:
            u, a = r["u"][l, c], r["a"][l, c]
            slope = (u + a * (2.0 - u)) * scale
            da = (r["g"][l, c] - mean - r["xhat"][l, c] * along) * slope
            at = slice(l * units + c.start, l * units + c.stop)
            r["dah"][at], r["dal"][at] = halves(da)

    def grad_in(l):
        at = slice(l * units, (l + 1) * units)
        r["acc_w"][l] += dot(r["xh"][...], r["dah"][at], NT) + dot(r["xh"][...], r["dal"][at], NT)
        r["acc_w"][l, 0:depth] += dot(r["xl"][...], r["dah"][at], NT)

    project_in(0)
    if first:
        gate_weights()
    for l in range(count):
        if l + 1 < count:
            project_in(l + 1)
        normalise(l)
    for l in range(count):
        project_out(l)
        combine(l)
    for l in range(count):
        back_out(l)
        grad_out(l)
        back_norm(l)
    for l in range(count):
        grad_in(l)

    if last:
        for k, g in enumerate(GROUPS[:-1]):
            at = 0
            for e in g:
                for _, row in uses(e):
                    r["all_dp"][row : row + 1] = r[f"dp{k}"][at : at + 1]
                    at += 1
        for lower, upper in ((0, 4), (4, 8), (8, 14)):
            p, d = r["prob"][lower:upper], r["all_dp"][lower:upper]
            r["dl"][lower:upper] = p * (d - jnp.sum(p * d, axis=0, keepdims=True))
        r["dl"][14:16] = jnp.zeros((2, tile), F32)
        high, low = halves(r["dl"][...])
        r["acc_gate"][...] += (
            dot(r["xh"][0:depth], high, NT) + dot(r["xh"][0:depth], low, NT) + dot(r["xl"][...], high, NT)
        )

    @pl.when(step == pl.num_programs(0) - 1)
    def _():
        for l in range(count):
            base = l * (rows_all + 8)
            tail = jnp.concatenate([r["acc_g"][l, units : units + 1], r["acc_w"][l, depth : depth + 1]], 0)
            tail = jnp.concatenate([tail] * 4, 0)
            for q in range(pairs):
                for dst, at in ((r["keep"], core), (r["send"], 1 - core)):
                    place = q * 2 + at
                    dst[q, base : base + rows_in] = r["acc_w"][l, pl.ds(place * rows_in, rows_in)]
                    dst[q, base + rows_in : base + rows_all] = r["acc_g"][l, pl.ds(place * rows_out, rows_out)]
                    dst[q, base + rows_all : base + rows_all + 8] = tail
        if last:
            for q in range(pairs):
                for dst, at in ((r["gate_keep"], core), (r["gate_send"], 1 - core)):
                    dst[q] = r["acc_gate"][pl.ds((q * 2 + at) * rows_in, rows_in)]


def expert_call(group, core, own, other, small, xh, xl, ct, prob, gates, dps, last):
    first = gates is not None
    pairs, _, units = own.shape
    depth, rows = xl.shape
    devices = 2 * pairs
    rows_in, rows_out = depth // devices, units // devices
    count = len(group)
    whole = lambda shape: pl.BlockSpec(shape, lambda i: (0,) * len(shape))
    along = lambda n: pl.BlockSpec((n, TILE), lambda i: (0, i))
    ins = [core, own, other, small, xh, xl, ct]
    in_specs = [
        pl.BlockSpec(memory_space=pltpu.SMEM),
        whole(own.shape),
        whole(other.shape),
        whole(small.shape),
        along(xh.shape[0]),
        along(depth),
        pl.BlockSpec((ct.shape[0], units, TILE), lambda i: (0, 0, i)),
    ]
    if first:
        ins.append(gates)
        in_specs.append(whole(gates.shape))
    else:
        ins.append(prob)
        in_specs.append(along(GATES))
    if last:
        ins += dps
        in_specs += [along(8)] * len(dps)
    packed = count * (rows_in + rows_out + 8)
    shape = jax.ShapeDtypeStruct
    outs = [
        (along(count * units), shape((count * units, rows), BF16)),
        (along(count * units), shape((count * units, rows), BF16)),
        (along(count * units), shape((count * units, rows), F32)),
        (whole((pairs, packed, units)), shape((pairs, packed, units), F32)),
        (whole((pairs, packed, units)), shape((pairs, packed, units), F32)),
        (whole((count, depth, units)), shape((count, depth, units), BF16)),
        (whole((count, depth, units)), shape((count, depth, units), BF16)),
    ]
    if first:
        outs.append((along(GATES), shape((GATES, rows), F32)))
    if last:
        outs.append((along(GATES), shape((GATES, rows), F32)))
        outs += [(whole((pairs, rows_in, GATES)), shape((pairs, rows_in, GATES), F32))] * 2
    else:
        outs.append((along(8), shape((8, rows), F32)))
    top = units + (GATES if first else 0)
    full = lambda n, t: pltpu.VMEM((count, n, TILE), t)
    scratch = [
        pltpu.VMEM((count, top, depth), BF16),
        pltpu.VMEM((count, top, depth), BF16),
        pltpu.VMEM((count, units, units), BF16),
        pltpu.VMEM((count, units, units), BF16),
        pltpu.VMEM((count, units, units), BF16),
        pltpu.VMEM((count, units, units), BF16),
        pltpu.VMEM((count, units, LANES), F32),
        pltpu.VMEM((count, units, LANES), F32),
        pltpu.VMEM((count, depth + STEP, units), F32),
        pltpu.VMEM((count, units + STEP, units), F32),
        full(top, F32),
        full(units, F32),
        full(units, F32),
        full(units, F32),
        full(units, F32),
        full(units, F32),
        full(units + STEP, BF16),
        full(units, BF16),
        full(units, BF16),
        full(units, BF16),
    ]
    if last:
        scratch += [pltpu.VMEM((GATES, TILE), F32), pltpu.VMEM((depth, GATES), F32)]
    return pl.pallas_call(
        functools.partial(expert_kernel, group, first, last, len(ins)),
        grid=(rows // TILE,),
        in_specs=in_specs,
        out_specs=[o[0] for o in outs],
        out_shape=[o[1] for o in outs],
        scratch_shapes=scratch,
        compiler_params=pltpu.CompilerParams(vmem_limit_bytes=VMEM_BYTES),
        cost_estimate=pl.CostEstimate(
            flops=20000000000 * count // 2, bytes_accessed=30000000, transcendentals=0
        ),
    )(*ins)


def final_kernel(*refs):
    n = len(GROUPS)
    dahs, dals, exs, wihs, wils = (refs[k * n : (k + 1) * n] for k in range(5))
    prob_ref, dl_ref, gates_ref, out_ref, gf_ref, gate_ref = refs[5 * n :]
    units = out_ref.shape[2]

    @pl.when(pl.program_id(0) == 0)
    def _():
        high, low = halves(gates_ref[...])
        gate_ref[0:GATES] = high
        gate_ref[GATES : 2 * GATES] = low
        gate_ref[2 * GATES :] = high

    high, low = halves(dl_ref[...])
    total = dot(gate_ref[...], jnp.concatenate([high, high, low], 0), TN)
    for k, group in enumerate(GROUPS):
        for l in range(len(group)):
            at = slice(l * units, (l + 1) * units)
            total = total + dot3(wihs[k][l], wils[k][l], dahs[k][at], dals[k][at], NN)
    gf_ref[...] = total.T
    sums = [None] * (TASKS + 1)
    for k, group in enumerate(GROUPS):
        for l, e in enumerate(group):
            ex = exs[k][l * units : (l + 1) * units]
            for o, row in uses(e):
                term = prob_ref[row : row + 1] * ex
                sums[o] = term if sums[o] is None else sums[o] + term
    for o in range(TASKS + 1):
        out_ref[o] = sums[o].T


def final_call(dahs, dals, exs, wihs, wils, prob, dl, gates):
    rows = prob.shape[1]
    _, depth, units = wihs[0].shape
    whole = lambda a: pl.BlockSpec(a.shape, lambda i: (0,) * a.ndim)
    along = lambda a: pl.BlockSpec((a.shape[0], TILE), lambda i: (0, i))
    return pl.pallas_call(
        final_kernel,
        grid=(rows // TILE,),
        in_specs=[along(a) for a in (*dahs, *dals, *exs)]
        + [whole(a) for a in (*wihs, *wils)]
        + [along(prob), along(dl), whole(gates)],
        out_specs=[
            pl.BlockSpec((TASKS + 1, TILE, units), lambda i: (0, i, 0)),
            pl.BlockSpec((TILE, depth), lambda i: (i, 0)),
        ],
        out_shape=[
            jax.ShapeDtypeStruct((TASKS + 1, rows, units), F32),
            jax.ShapeDtypeStruct((rows, depth), F32),
        ],
        scratch_shapes=[pltpu.VMEM((3 * GATES, depth), BF16)],
        compiler_params=pltpu.CompilerParams(vmem_limit_bytes=VMEM_BYTES),
        cost_estimate=pl.CostEstimate(flops=15000000000, bytes_accessed=50000000, transcendentals=0),
    )(*dahs, *dals, *exs, *wihs, *wils, prob, dl, gates)


def local(features, cotangent, valid, core, owns, others, small, gates):
    xh, xl, ct = prep(features, cotangent, valid)
    prob, dps = None, []
    kept, sent, dahs, dals, exs, wihs, wils = [], [], [], [], [], [], []
    for k, group in enumerate(GROUPS):
        last = k == len(GROUPS) - 1
        got = expert_call(
            group, core, owns[k], others[k], small, xh, xl, ct, prob, None if k else gates, dps, last
        )
        dah, dal, ex, keep, send, wih, wil = got[:7]
        rest = list(got[7:])
        if k == 0:
            prob = rest.pop(0)
        kept.append([keep])
        sent.append([send])
        if last:
            dl = rest[0]
            kept[-1].append(rest[1])
            sent[-1].append(rest[2])
        else:
            dps.append(rest[0])
        for to, what in ((dahs, dah), (dals, dal), (exs, ex), (wihs, wih), (wils, wil)):
            to.append(what)
    outputs, grad_features = final_call(dahs, dals, exs, wihs, wils, prob, dl, gates)
    return outputs, grad_features, kept, sent


def make(mesh):
    n_fsdp, n_dp = mesh.shape["fsdp"], mesh.shape["dp"]
    pairs = n_fsdp // 2
    across = [[q * 2 + c for q in range(pairs)] for c in range(2)]
    twin = [(i, i ^ 1) for i in range(n_fsdp)]

    def gather(x):
        spread = jnp.broadcast_to(x[None], (pairs, *x.shape))
        own = lax.all_to_all(spread, "fsdp", 0, 0, axis_index_groups=across)
        return own, lax.ppermute(own, "fsdp", twin)

    def scatter(keep, send):
        got = keep + lax.ppermute(send, "fsdp", twin)
        return jnp.sum(lax.all_to_all(got, "fsdp", 0, 0, axis_index_groups=across), 0)

    def replicas(x):
        bit = 1
        while bit < n_dp:
            x = x + lax.ppermute(x, "dp", [(i, i ^ bit) for i in range(n_dp)])
            bit *= 2
        return x

    def on_device(
        features, cotangent, counts, keep, w_in, in_bias, norm_gain, norm_bias, w_out, out_bias, task_gate, shared_gate
    ):
        rows = features.shape[0]
        depth = features.shape[1]
        experts, rows_in, units = w_in.shape
        rows_out = w_out.shape[1]
        valid = (lax.broadcasted_iota(jnp.int32, (1, rows), 1) < counts[0]) & (keep.reshape(1, rows) > 0)
        me = lax.axis_index("fsdp")
        core = (me % 2).astype(jnp.int32).reshape(1)
        biases = jnp.concatenate([in_bias, norm_gain, norm_bias, out_bias], 0)
        gate = jnp.concatenate([task_gate[0].T, task_gate[1].T, shared_gate.T], 0)
        gate = jnp.pad(gate, ((0, GATES - gate.shape[0]), (0, units - rows_in)))
        extra = jnp.concatenate([jnp.pad(biases, ((0, 0), (0, units - rows_out))), gate], 0)
        owns, others = [], []
        for k, group in enumerate(GROUPS):
            parts = []
            for e in group:
                parts += [w_in[e], w_out[e]]
            if k == 0:
                parts.append(extra)
            own, other = gather(jnp.concatenate(parts, 0))
            owns.append(own)
            others.append(other)
        begin = len(GROUPS[0]) * (rows_in + rows_out)
        mine, theirs = owns[0][:, begin:], others[0][:, begin:]
        both = jnp.where(core[0] == 0, jnp.stack([mine, theirs], 1), jnp.stack([theirs, mine], 1))
        both = both.reshape(n_fsdp, *both.shape[2:])
        n_bias = biases.shape[0]
        small = both[:, :n_bias, :rows_out].transpose(1, 0, 2).reshape(n_bias, units)
        gates = both[:, n_bias:, :rows_in].transpose(1, 0, 2).reshape(GATES, depth)

        outputs, grad_features, kept, sent = local(
            features, cotangent, valid.astype(F32), core, owns, others, small, gates
        )

        g_in, g_in_bias, g_gain, g_shift, g_out, g_out_bias = [], [], [], [], [], []
        for k, group in enumerate(GROUPS):
            total = replicas(scatter(kept[k][0], sent[k][0]))
            for l, e in enumerate(group):
                base = l * (rows_in + rows_out + 8)
                g_in.append(total[base : base + rows_in])
                raw = total[base + rows_in : base + rows_in + rows_out]
                tail = total[base + rows_in + rows_out :]
                column_sum = tail[0]
                g_in_bias.append(lax.dynamic_slice(tail[1], (me * rows_out,), (rows_out,)))
                g_out_bias.append(lax.dynamic_slice(column_sum, (me * rows_out,), (rows_out,)))
                g_out.append(norm_gain[e][:, None] * raw + norm_bias[e][:, None] * column_sum[None])
                g_gain.append(jnp.sum(w_out[e] * raw, 1))
                g_shift.append(jnp.sum(w_out[e] * column_sum[None], 1))
        gate_sum = replicas(scatter(kept[-1][1], sent[-1][1]))
        n_task = SPEC + SHARED
        g_task = jnp.stack([gate_sum[:, t * n_task : (t + 1) * n_task] for t in range(TASKS)])
        g_shared = gate_sum[:, TASKS * n_task : TASKS * n_task + EXPERTS]
        return (
            outputs,
            grad_features,
            jnp.stack(g_in),
            jnp.stack(g_in_bias),
            jnp.stack(g_gain),
            jnp.stack(g_shift),
            jnp.stack(g_out),
            jnp.stack(g_out_bias),
            g_task,
            g_shared,
        )

    return on_device


def solution(mesh):
    placed = (
        P(("dp", "fsdp"), None),
        P(None, ("dp", "fsdp"), None),
        P(("dp", "fsdp")),
        P(("dp", "fsdp")),
        P(None, "fsdp", None),
        P(None, "fsdp"),
        P(None, "fsdp"),
        P(None, "fsdp"),
        P(None, "fsdp", None),
        P(None, "fsdp"),
        P(None, "fsdp", None),
        P("fsdp", None),
    )
    return jax.shard_map(
        make(mesh),
        mesh=mesh,
        in_specs=placed,
        out_specs=(
            P(None, ("dp", "fsdp"), None),
            P(("dp", "fsdp"), None),
            P(None, "fsdp", None),
            P(None, "fsdp"),
            P(None, "fsdp"),
            P(None, "fsdp"),
            P(None, "fsdp", None),
            P(None, "fsdp"),
            P(None, "fsdp", None),
            P("fsdp", None),
        ),
        check_vma=False,
    )
```

time: 864 us -> 267 us (0.31)
  matrix products: 388 us -> 0 us
  other arithmetic: 157 us -> 10 us
  Pallas kernels: 0 us -> 134 us
  local copies, waits for them, and re-layouts: 108 us -> 17.1 us
  blocking collectives: 75.1 us -> 0 us
  waiting for transfers between devices: 110 us -> 61.9 us
  starting transfers between devices: 1.26 us -> 41.1 us
  between operations: 18 us -> 1.78 us
    dot_general x45 -> x0, matrix products: 388 us -> none  [the longest x9 193 us: forward(): jnp.einsum('bd,edh->ebh', features, w_in, precision=highest)]
    pallas_call x0 -> x5, Pallas kernels: none -> 134 us  [the longest x3 94.3 us: expert_call(): pl.pallas_call(functools.partial(expert_kernel, group, first, last, len(i...]
    reduce_sum x22 -> x6, other arithmetic: 87.9 us -> 0.56 us  [the longest x2 0.38 us: on_device(): g_gain.append(jnp.sum(w_out[e] * raw, 1))]
    unnamed x17 -> x0, waiting for transfers between devices: 85.9 us -> none
    all_gather x6 -> x0, blocking collectives: 55.2 us -> none  [the longest x1 11.3 us: on_device(): lax.all_gather(task_gate, 'fsdp', axis=1, tiled=True)]
    unnamed x537 -> x39, local copies, waits for them, and re-layouts: 43.8 us -> 4.86 us
    dot_general x12 -> x0, local copies, waits for them, and re-layouts: 38.4 us -> none  [the longest x3 20 us: forward(): jnp.einsum('ebh,ehk->ebk', normed, w_out, precision=highest)]
    all_to_all x0 -> x7, waiting for transfers between devices: none -> 33.1 us  [the longest x3 20.9 us: gather(): own = lax.all_to_all(spread, 'fsdp', 0, 0, axis_index_groups=across)]
  transfers between devices with their start and end apart: 11 -> 22, of which waited for: 4 -> 10; matrix products, arithmetic and copies ran while one was open for 43% -> 6% of each run, Pallas kernels for 0% -> 50%
where the time goes in v1:
time: 267 us; the launch traced here: 266 us
  Pallas kernels  134 us (50%)
  waiting for transfers between devices  61.9 us (23%)
  starting transfers between devices  41.1 us (15%)
  local copies, waits for them, and re-layouts  17.1 us (6%)
  other arithmetic  10 us (4%)
    pallas_call x3, Pallas kernels, expert_call(): pl.pallas_call(functools.partial(expert_kernel, group, first, last, len(i...  94.3 us
    ppermute x8, waiting for transfers between devices, replicas(): x = x + lax.ppermute(x, 'dp', [(i, i ^ bit) for i in range(n_dp)])  26.5 us
    pallas_call x1, Pallas kernels, final_call(): pl.pallas_call(final_kernel, grid=(rows // TILE,), in_specs=[along(a) for...  26.2 us
    all_to_all x3, waiting for transfers between devices, gather(): own = lax.all_to_all(spread, 'fsdp', 0, 0, axis_index_groups=across)  20.9 us
    all_to_all x4, starting transfers between devices, scatter(): lax.all_to_all(got, 'fsdp', 0, 0, axis_index_groups=across)  15.1 us
    pallas_call x1, Pallas kernels, prep(): pl.pallas_call(prep_kernel, grid=(rows // TILE,), in_specs=[pl.BlockSpec(...  13.4 us
    ppermute x8, starting transfers between devices, replicas(): x = x + lax.ppermute(x, 'dp', [(i, i ^ bit) for i in range(n_dp)])  12.3 us
    all_to_all x4, waiting for transfers between devices, scatter(): lax.all_to_all(got, 'fsdp', 0, 0, axis_index_groups=across)  12.2 us
  transfers between devices with their start and end apart: 22, of which 10 were waited for; matrix products, arithmetic and copies ran while one was open for 6% of the time, Pallas kernels for 50%

profile of v1, /device:TPU:0, one launch (start us, length us, event | category | flops | bytes accessed | tf_op | source)
XLA Modules:
  0.0 265.8 jit_solution(8259308215493374712)
XLA Ops:
  7.0 5.2 %all-to-all-start = ((f32[4,232,256]{2,1,0:T(8,128)}), f32[4,232,256]{2,1,0:T(8,128)S(1)}, u32[]{:S(2)}, u32[]{:S(2)}) async-start(f32[4,232,256]{2,1,0:T(8,128)} %broadcast_in_dim.6), calls=%async_computation | async-start | bytes 1900544 | tf_op jit(solution)/shard_map/all_to_all | solution.py:487
  14.0 10.8 %all-to-all-done.refs_1_ = f32[4,232,256]{2,1,0:T(8,128)S(1)} async-done(((f32[4,232,256]{2,1,0:T(8,128)}), f32[4,232,256]{2,1,0:T(8,128)S(1)}, u32[]{:S(2)}, u32[]{:S(2)}) %all-to-all-start) | async-done | bytes 950304 | tf_op jit(solution)/shard_map/all_to_all | solution.py:487
  25.8 3.5 %all-to-all-start.2 = ((f32[4,192,256]{2,1,0:T(8,128)}), f32[4,192,256]{2,1,0:T(8,128)S(1)}, u32[]{:S(2)}, u32[]{:S(2)}) async-start(f32[4,192,256]{2,1,0:T(8,128)} %broadcast_in_dim.8), calls=%async_computation.2 | async-start | bytes 1572864 | tf_op jit(solution)/shard_map/all_to_all | solution.py:487
  29.4 10.2 %all-to-all-done.2.refs_1_ = f32[4,192,256]{2,1,0:T(8,128)S(1)} async-done(((f32[4,192,256]{2,1,0:T(8,128)}), f32[4,192,256]{2,1,0:T(8,128)S(1)}, u32[]{:S(2)}, u32[]{:S(2)}) %all-to-all-start.2) | async-done | bytes 786464 | tf_op jit(solution)/shard_map/all_to_all | solution.py:487
  40.6 3.5 %all-to-all-start.1 = ((f32[4,192,256]{2,1,0:T(8,128)}), f32[4,192,256]{2,1,0:T(8,128)S(1)}, u32[]{:S(2)}, u32[]{:S(2)}) async-start(f32[4,192,256]{2,1,0:T(8,128)} %broadcast_in_dim.7), calls=%async_computation.1 | async-start | bytes 1572864 | tf_op jit(solution)/shard_map/all_to_all | solution.py:487
  45.3 13.4 %shard_map.195 = (bf16[528,3072]{1,0:T(8,128)(2,1)}, bf16[512,3072]{1,0:T(8,128)(2,1)}, f32[3,256,3072]{2,1,0:T(8,128)}) custom-call(f32[3072,512]{1,0:T(8,128)} %x_ref.1, f32[3,3072,256]{2,1,0:T(8,128)} %c_ref.1, f32[1,3072]{1,0:T(1,128)} %bitcast.162), custom_call_target="tpu_custom_call" | custom-call | bytes 32000000 | tf_op jit(solution)/shard_map/pallas_call | solution.py:74
  61.7 30.7 %shard_map.196 = (bf16[512,3072]{1,0:T(8,128)(2,1)}, bf16[512,3072]{1,0:T(8,128)(2,1)}, f32[512,3072]{1,0:T(8,128)}, f32[4,208,256]{2,1,0:T(8,128)}, f32[4,208,2...) custom-call(s32[1]{0:T(128)} %bitcast.refs_0_, ...), custom_call_target="tpu_custom_call" | custom-call | flops 20000000000 | bytes 30000000 | tf_op jit(solution)/shard_map/pallas_call | solution.py:382
  92.8 30.1 %shard_map.197 = (bf16[512,3072]{1,0:T(8,128)(2,1)}, bf16[512,3072]{1,0:T(8,128)(2,1)}, f32[512,3072]{1,0:T(8,128)}, f32[4,208,256]{2,1,0:T(8,128)}, f32[4,208,2...) custom-call(s32[1]{0:T(128)} %bitcast.refs_0_, ...), custom_call_target="tpu_custom_call" | custom-call | flops 20000000000 | bytes 30000000 | tf_op jit(solution)/shard_map/pallas_call | solution.py:382
  122.9 33.4 %shard_map.198 = (bf16[512,3072]{1,0:T(8,128)(2,1)}, bf16[512,3072]{1,0:T(8,128)(2,1)}, f32[512,3072]{1,0:T(8,128)}, f32[4,208,256]{2,1,0:T(8,128)}, f32[4,208,2...) custom-call(s32[1]{0:T(128)} %bitcast.refs_0_, ...), custom_call_target="tpu_custom_call" | custom-call | flops 20000000000 | bytes 30000000 | tf_op jit(solution)/shard_map/pallas_call | solution.py:382
  157.0 2.3 collective-permute-done.12
  161.0 4.2 %all-to-all-start.6 = ((f32[4,1,1024]{2,1,0:T(1,128)}), f32[4,1,1024]{2,1,0:T(1,128)S(1)}, u32[]{:S(2)}, u32[]{:S(2)}) async-start(f32[4,1,1024]{2,1,0:T(1,128)} %reshape.84), calls=%async_computation.6 | async-start | bytes 32768 | tf_op jit(solution)/shard_map/all_to_all | solution.py:492
  166.1 3.7 %all-to-all-done.6 = f32[4,1,1024]{2,1,0:T(1,128)S(1)} async-done(((f32[4,1,1024]{2,1,0:T(1,128)}), f32[4,1,1024]{2,1,0:T(1,128)S(1)}, u32[]{:S(2)}, u32[]{:S(2)}) %all-to-all-start.6) | async-done | bytes 16416 | tf_op jit(solution)/shard_map/all_to_all | solution.py:492
  169.8 3.5 %all-to-all-start.3 = ((f32[4,208,256]{2,1,0:T(8,128)}), f32[4,208,256]{2,1,0:T(8,128)S(1)}, u32[]{:S(2)}, u32[]{:S(2)}) async-start(f32[4,208,256]{2,1,0:T(8,128)} %add.77), calls=%async_computation.3 | async-start | bytes 1703936 | tf_op jit(solution)/shard_map/all_to_all | solution.py:492
  173.4 2.4 add.83
  175.8 8.2 %all-to-all-done.3 = f32[4,208,256]{2,1,0:T(8,128)S(1)} async-done(((f32[4,208,256]{2,1,0:T(8,128)}), f32[4,208,256]{2,1,0:T(8,128)S(1)}, u32[]{:S(2)}, u32[]{:S(2)}) %all-to-all-start.3) | async-done | bytes 852000 | tf_op jit(solution)/shard_map/all_to_all | solution.py:492
  184.1 3.5 %all-to-all-start.5 = ((f32[4,208,256]{2,1,0:T(8,128)}), f32[4,208,256]{2,1,0:T(8,128)S(1)}, u32[]{:S(2)}, u32[]{:S(2)}) async-start(f32[4,208,256]{2,1,0:T(8,128)} %add.83), calls=%async_computation.5 | async-start | bytes 1703936 | tf_op jit(solution)/shard_map/all_to_all | solution.py:492
  189.0 1.6 collective-permute-start.13
  191.2 1.8 collective-permute-done.13
  192.9 2.6 collective-permute-start.14
  198.5 3.9 %all-to-all-start.4 = ((f32[4,208,256]{2,1,0:T(8,128)}), f32[4,208,256]{2,1,0:T(8,128)S(1)}, u32[]{:S(2)}, u32[]{:S(2)}) async-start(f32[4,208,256]{2,1,0:T(8,128)} %add.80), calls=%async_computation.4 | async-start | bytes 1703936 | tf_op jit(solution)/shard_map/all_to_all | solution.py:492
  202.5 26.2 %shard_map.199 = (f32[3,3072,256]{2,1,0:T(8,128)}, f32[3072,512]{1,0:T(8,128)}) custom-call(bf16[512,3072]{1,0:T(8,128)(2,1)} %get-tuple-element.45.refs_0_, bf16[512,3072]{1,0:T(8,128)(2,1)} %get-tuple-element.47.refs_1_, bf16[512,3072]{1,0:T(8,128)(2,1)} %get-tuple-element.50.refs_2_, bf16[512,3072]{1,0:T(8,128)(2,1)} %get-tuple-element.51.refs_3_, ...), custom_call_target="tpu_custom_call" | custom-call | flops 15000000512 | bytes 50000000 | tf_op jit(solution)/shard_map/pallas_call | solution.py:432
  231.0 2.3 collective-permute-start.5
  234.9 8.8 %collective-permute-done.10 = f32[208,256]{1,0:T(8,128)S(1)} collective-permute-done((f32[208,256]{1,0:T(8,128)S(1)}, f32[208,256]{1,0:T(8,128)S(1)}, u32[]{:S(2)}, u32[]{:S(2)}) %collective-permute-start.10) | collective-permute-done | bytes 213024 | tf_op jit(solution)/shard_map/ppermute | solution.py:497
  247.2 14.5 %collective-permute-done.8 = f32[208,256]{1,0:T(8,128)S(1)} collective-permute-done((f32[208,256]{1,0:T(8,128)S(1)}, f32[208,256]{1,0:T(8,128)S(1)}, u32[]{:S(2)}, u32[]{:S(2)}) %collective-permute-start.8) | collective-permute-done | bytes 213024 | tf_op jit(solution)/shard_map/ppermute | solution.py:497
  (132 shorter events, 33.7 us)
Async XLA Ops:
  0.6 44.1 %copy-start.8 = (s32[3072]{0:T(1024)S(1)}, s32[3072]{0:T(1024)}, u32[]{:S(2)}) copy-start(s32[3072]{0:T(1024)} %param.15) | copy-start | bytes 36868
  7.0 17.7 %all-to-all-start = ((f32[4,232,256]{2,1,0:T(8,128)}), f32[4,232,256]{2,1,0:T(8,128)S(1)}, u32[]{:S(2)}, u32[]{:S(2)}) async-start(f32[4,232,256]{2,1,0:T(8,128)} %broadcast_in_dim.6), calls=%async_computation | async-start | bytes 1900544 | tf_op jit(solution)/shard_map/all_to_all | solution.py:487
  25.8 13.8 %all-to-all-start.2 = ((f32[4,192,256]{2,1,0:T(8,128)}), f32[4,192,256]{2,1,0:T(8,128)S(1)}, u32[]{:S(2)}, u32[]{:S(2)}) async-start(f32[4,192,256]{2,1,0:T(8,128)} %broadcast_in_dim.8), calls=%async_computation.2 | async-start | bytes 1572864 | tf_op jit(solution)/shard_map/all_to_all | solution.py:487
  29.3 30.0 %collective-permute-start = (f32[4,232,256]{2,1,0:T(8,128)S(1)}, f32[4,232,256]{2,1,0:T(8,128)}, u32[]{:S(2)}, u32[]{:S(2)}) collective-permute-start(f32[4,232,256]{2,1,0:T(8,128)S(1)} %all-to-all-done.refs_1_), channel_id=1, source_target_pairs={{0,1},{1,0},{2,3},{3,2},{4,5},{5,4},{6,7},{7,6},{8,9},{9,8},{10,11... | collective-permute-start | bytes 2850824 | tf_op jit(solution)/shard_map/ppermute | solution.py:488
  40.6 18.2 %all-to-all-start.1 = ((f32[4,192,256]{2,1,0:T(8,128)}), f32[4,192,256]{2,1,0:T(8,128)S(1)}, u32[]{:S(2)}, u32[]{:S(2)}) async-start(f32[4,192,256]{2,1,0:T(8,128)} %broadcast_in_dim.7), calls=%async_computation.1 | async-start | bytes 1572864 | tf_op jit(solution)/shard_map/all_to_all | solution.py:487
  58.7 64.2 %collective-permute-start.2 = (f32[4,192,256]{2,1,0:T(8,128)S(1)}, f32[4,192,256]{2,1,0:T(8,128)}, u32[]{:S(2)}, u32[]{:S(2)}) collective-permute-start(f32[4,192,256]{2,1,0:T(8,128)S(1)} %all-to-all-done.2.refs_1_), channel_id=1, source_target_pairs={{0,1},{1,0},{2,3},{3,2},{4,5},{5,4},{6,7},{7,6},{8,9},{9,8},{10,11... | collective-permute-start | bytes 2359304 | tf_op jit(solution)/shard_map/ppermute | solution.py:488
  58.7 34.0 %collective-permute-start.1 = (f32[4,192,256]{2,1,0:T(8,128)S(1)}, f32[4,192,256]{2,1,0:T(8,128)}, u32[]{:S(2)}, u32[]{:S(2)}) collective-permute-start(f32[4,192,256]{2,1,0:T(8,128)S(1)} %all-to-all-done.1.refs_1_), channel_id=1, source_target_pairs={{0,1},{1,0},{2,3},{3,2},{4,5},{5,4},{6,7},{7,6},{8,9},{9,8},{10,11... | collective-permute-start | bytes 2359304 | tf_op jit(solution)/shard_map/ppermute | solution.py:488
  92.4 72.7 %collective-permute-start.3 = (f32[4,208,256]{2,1,0:T(8,128)}, f32[4,208,256]{2,1,0:T(8,128)S(1)}, u32[]{:S(2)}, u32[]{:S(2)}) collective-permute-start(f32[4,208,256]{2,1,0:T(8,128)} %get-tuple-element.67), channel_id=1, source_target_pairs={{0,1},{1,0},{2,3},{3,2},{4,5},{5,4},{6,7},{7,6},{8,9},{9,8},{10,11... | collective-permute-start | bytes 2555912 | tf_op jit(solution)/shard_map/ppermute | solution.py:491
  156.4 17.0 %collective-permute-start.9 = (f32[4,208,256]{2,1,0:T(8,128)}, f32[4,208,256]{2,1,0:T(8,128)}, u32[]{:S(2)}, u32[]{:S(2)}) collective-permute-start(f32[4,208,256]{2,1,0:T(8,128)} %get-tuple-element.71), channel_id=1, source_target_pairs={{0,1},{1,0},{2,3},{3,2},{4,5},{5,4},{6,7},{7,6},{8,9},{9,8},{10,11... | collective-permute-start | bytes 2555912 | tf_op jit(solution)/shard_map/ppermute | solution.py:491
  156.7 2.5 collective-permute-start.12
  161.0 8.9 %all-to-all-start.6 = ((f32[4,1,1024]{2,1,0:T(1,128)}), f32[4,1,1024]{2,1,0:T(1,128)S(1)}, u32[]{:S(2)}, u32[]{:S(2)}) async-start(f32[4,1,1024]{2,1,0:T(1,128)} %reshape.84), calls=%async_computation.6 | async-start | bytes 32768 | tf_op jit(solution)/shard_map/all_to_all | solution.py:492
  169.8 14.3 %all-to-all-start.3 = ((f32[4,208,256]{2,1,0:T(8,128)}), f32[4,208,256]{2,1,0:T(8,128)S(1)}, u32[]{:S(2)}, u32[]{:S(2)}) async-start(f32[4,208,256]{2,1,0:T(8,128)} %add.77), calls=%async_computation.3 | async-start | bytes 1703936 | tf_op jit(solution)/shard_map/all_to_all | solution.py:492
  173.3 22.2 %collective-permute-start.6 = (f32[4,208,256]{2,1,0:T(8,128)}, f32[4,208,256]{2,1,0:T(8,128)S(1)}, u32[]{:S(2)}, u32[]{:S(2)}) collective-permute-start(f32[4,208,256]{2,1,0:T(8,128)} %get-tuple-element.69), channel_id=1, source_target_pairs={{0,1},{1,0},{2,3},{3,2},{4,5},{5,4},{6,7},{7,6},{8,9},{9,8},{10,11... | collective-permute-start | bytes 2555912 | tf_op jit(solution)/shard_map/ppermute | solution.py:491
  184.1 14.4 %all-to-all-start.5 = ((f32[4,208,256]{2,1,0:T(8,128)}), f32[4,208,256]{2,1,0:T(8,128)S(1)}, u32[]{:S(2)}, u32[]{:S(2)}) async-start(f32[4,208,256]{2,1,0:T(8,128)} %add.83), calls=%async_computation.5 | async-start | bytes 1703936 | tf_op jit(solution)/shard_map/all_to_all | solution.py:492
  189.0 3.9 %collective-permute-start.13 = (f32[64,16]{1,0:T(8,128)S(1)}, f32[64,16]{1,0:T(8,128)S(1)}, u32[]{:S(2)}, u32[]{:S(2)}) collective-permute-start(f32[64,16]{1,0:T(8,128)S(1)} %copy.40), channel_id=1, source_target_pairs={{0,8},{8,0},{16,24},{24,16},{1,9},{9,1},{17,25},{25,17},{2,10},{10... | collective-permute-start | bytes 12296 | tf_op jit(solution)/shard_map/ppermute | solution.py:497
  192.9 35.8 %collective-permute-start.14 = (f32[64,16]{1,0:T(8,128)S(1)}, f32[64,16]{1,0:T(8,128)S(1)}, u32[]{:S(2)}, u32[]{:S(2)}) collective-permute-start(f32[64,16]{1,0:T(8,128)S(1)} %add.94), channel_id=1, source_target_pairs={{0,16},{8,24},{16,0},{24,8},{1,17},{9,25},{17,1},{25,9},{2,18},{10... | collective-permute-start | bytes 12296 | tf_op jit(solution)/shard_map/ppermute | solution.py:497
  196.7 34.3 %collective-permute-start.4 = (f32[208,256]{1,0:T(8,128)S(1)}, f32[208,256]{1,0:T(8,128)S(1)}, u32[]{:S(2)}, u32[]{:S(2)}) collective-permute-start(f32[208,256]{1,0:T(8,128)S(1)} %reduce_sum.144), channel_id=1, source_target_pairs={{0,8},{8,0},{16,24},{24,16},{1,9},{9,1},{17,25},{25,17},{2,10},{10... | collective-permute-start | bytes 638984 | tf_op jit(solution)/shard_map/ppermute | solution.py:497
  198.5 31.5 %all-to-all-start.4 = ((f32[4,208,256]{2,1,0:T(8,128)}), f32[4,208,256]{2,1,0:T(8,128)S(1)}, u32[]{:S(2)}, u32[]{:S(2)}) async-start(f32[4,208,256]{2,1,0:T(8,128)} %add.80), calls=%async_computation.4 | async-start | bytes 1703936 | tf_op jit(solution)/shard_map/all_to_all | solution.py:492
  202.5 59.4 %copy-start = (f32[6,32,256]{2,1,0:T(8,128)S(1)}, f32[6,32,256]{2,1,0:T(8,128)}, u32[]{:S(2)}) copy-start(f32[6,32,256]{2,1,0:T(8,128)} %param.20) | copy-start | bytes 589828
  228.8 15.0 %collective-permute-start.10 = (f32[208,256]{1,0:T(8,128)S(1)}, f32[208,256]{1,0:T(8,128)S(1)}, u32[]{:S(2)}, u32[]{:S(2)}) collective-permute-start(f32[208,256]{1,0:T(8,128)S(1)} %reduce_sum.146), channel_id=1, source_target_pairs={{0,8},{8,0},{16,24},{24,16},{1,9},{9,1},{17,25},{25,17},{2,10},{10... | collective-permute-start | bytes 638984 | tf_op jit(solution)/shard_map/ppermute | solution.py:497
  230.1 15.9 %collective-permute-start.7 = (f32[208,256]{1,0:T(8,128)S(1)}, f32[208,256]{1,0:T(8,128)S(1)}, u32[]{:S(2)}, u32[]{:S(2)}) collective-permute-start(f32[208,256]{1,0:T(8,128)S(1)} %reduce_sum.145), channel_id=1, source_target_pairs={{0,8},{8,0},{16,24},{24,16},{1,9},{9,1},{17,25},{25,17},{2,10},{10... | collective-permute-start | bytes 638984 | tf_op jit(solution)/shard_map/ppermute | solution.py:497
  231.0 16.1 %collective-permute-start.5 = (f32[208,256]{1,0:T(8,128)S(1)}, f32[208,256]{1,0:T(8,128)S(1)}, u32[]{:S(2)}, u32[]{:S(2)}) collective-permute-start(f32[208,256]{1,0:T(8,128)S(1)} %add.78), channel_id=1, source_target_pairs={{0,16},{8,24},{16,0},{24,8},{1,17},{9,25},{17,1},{25,9},{2,18},{10... | collective-permute-start | bytes 638984 | tf_op jit(solution)/shard_map/ppermute | solution.py:497
  243.8 18.2 %collective-permute-start.11 = (f32[208,256]{1,0:T(8,128)S(1)}, f32[208,256]{1,0:T(8,128)S(1)}, u32[]{:S(2)}, u32[]{:S(2)}) collective-permute-start(f32[208,256]{1,0:T(8,128)S(1)} %add.84), channel_id=1, source_target_pairs={{0,16},{8,24},{16,0},{24,8},{1,17},{9,25},{17,1},{25,9},{2,18},{10... | collective-permute-start | bytes 638984 | tf_op jit(solution)/shard_map/ppermute | solution.py:497
  246.1 15.7 %collective-permute-start.8 = (f32[208,256]{1,0:T(8,128)S(1)}, f32[208,256]{1,0:T(8,128)S(1)}, u32[]{:S(2)}, u32[]{:S(2)}) collective-permute-start(f32[208,256]{1,0:T(8,128)S(1)} %add.81), channel_id=1, source_target_pairs={{0,16},{8,24},{16,0},{24,8},{1,17},{9,25},{17,1},{25,9},{2,18},{10... | collective-permute-start | bytes 638984 | tf_op jit(solution)/shard_map/ppermute | solution.py:497
  (11 other events, 311.2 us)

commit v2 on v1

--- a/solution.py
+++ b/solution.py
@@ -57,8 +57,58 @@
     return jnp.concatenate([block] * (width // LANES), axis=1)
 
 
-def prep_kernel(x_ref, c_ref, valid_ref, xh_ref, xl_ref, ct_ref):
+def tie(x, after):
+    return pl.pallas_call(
+        lambda *refs: None,
+        in_specs=[pl.BlockSpec(memory_space=pl.ANY)] * (1 + len(after)),
+        out_specs=pl.BlockSpec(memory_space=pl.ANY),
+        out_shape=jax.ShapeDtypeStruct(x.shape, x.dtype),
+        input_output_aliases={0: 0},
+    )(x, *after)
+
+
+def pack_weights(groups, w_in_ref, w_out_ref, to_ref):
+    rows_in, rows_out = w_in_ref.shape[1], w_out_ref.shape[1]
+    at = 0
+    for e in (e for group in groups for e in group):
+        for q in range(to_ref.shape[0]):
+            to_ref[q, at : at + rows_in] = w_in_ref[e]
+            to_ref[q, at + rows_in : at + rows_in + rows_out] = w_out_ref[e]
+        at += rows_in + rows_out
+    return at
+
+
+def pack_kernel(in_bias, gain, shift, out_bias, task_gate, shared_gate, w_in_ref, w_out_ref, to_ref):
+    rows_in, rows_out = w_in_ref.shape[1], w_out_ref.shape[1]
+    at = pack_weights(GROUPS[:1], w_in_ref, w_out_ref, to_ref)
+    n = SPEC + SHARED
+    for q in range(to_ref.shape[0]):
+        to_ref[q, at:] = jnp.zeros((to_ref.shape[1] - at, to_ref.shape[2]), F32)
+        for k, bias in enumerate((in_bias, gain, shift, out_bias)):
+            to_ref[q, at + k * EXPERTS : at + (k + 1) * EXPERTS, 0:rows_out] = bias[...]
+        base = at + 4 * EXPERTS
+        for t in range(TASKS):
+            to_ref[q, base + t * n : base + (t + 1) * n, 0:rows_in] = task_gate[t]
+        base += TASKS * n
+        to_ref[q, base : base + EXPERTS, 0:rows_in] = shared_gate[...]
+
+
+def pack(pairs, w_in, in_bias, gain, shift, w_out, out_bias, task_gate, shared_gate):
+    rows = len(GROUPS[0]) * (w_in.shape[1] + w_out.shape[1]) + 4 * EXPERTS + GATES
+    return pl.pallas_call(
+        pack_kernel,
+        out_shape=jax.ShapeDtypeStruct((pairs, rows, w_in.shape[2]), F32),
+        compiler_params=pltpu.CompilerParams(vmem_limit_bytes=VMEM_BYTES),
+    )(in_bias, gain, shift, out_bias, task_gate.transpose(0, 2, 1), shared_gate.T, w_in, w_out)
+
+
+def prep_kernel(x_ref, c_ref, valid_ref, w_in_ref, w_out_ref, xh_ref, xl_ref, ct_ref, to_ref):
     depth = x_ref.shape[1]
+
+    @pl.when(pl.program_id(0) == 0)
+    def _():
+        pack_weights(GROUPS[1:], w_in_ref, w_out_ref, to_ref)
+
     high, low = halves(x_ref[...].T)
     xh_ref[0:depth] = high
     xh_ref[depth:] = jnp.ones((xh_ref.shape[0] - depth, xh_ref.shape[1]), BF16)
@@ -68,8 +118,9 @@
         ct_ref[o] = c_ref[o].T * valid
 
 
-def prep(features, cotangent, valid):
+def prep(features, cotangent, valid, w_in, w_out, pairs):
     rows, depth = features.shape
+    packed = sum(len(g) for g in GROUPS[1:]) * (w_in.shape[1] + w_out.shape[1])
     outs, _, units = cotangent.shape
     return pl.pallas_call(
         prep_kernel,
@@ -78,20 +129,24 @@
             pl.BlockSpec((TILE, depth), lambda i: (i, 0)),
             pl.BlockSpec((outs, TILE, units), lambda i: (0, i, 0)),
             pl.BlockSpec((1, TILE), lambda i: (0, i)),
+            pl.BlockSpec(w_in.shape, lambda i: (0, 0, 0)),
+            pl.BlockSpec(w_out.shape, lambda i: (0, 0, 0)),
         ],
         out_specs=[
             pl.BlockSpec((depth + STEP, TILE), lambda i: (0, i)),
             pl.BlockSpec((depth, TILE), lambda i: (0, i)),
             pl.BlockSpec((outs, units, TILE), lambda i: (0, 0, i)),
+            pl.BlockSpec((pairs, packed, units), lambda i: (0, 0, 0)),
         ],
         out_shape=[
             jax.ShapeDtypeStruct((depth + STEP, rows), BF16),
             jax.ShapeDtypeStruct((depth, rows), BF16),
             jax.ShapeDtypeStruct((outs, units, rows), F32),
+            jax.ShapeDtypeStruct((pairs, packed, units), F32),
         ],
         compiler_params=pltpu.CompilerParams(vmem_limit_bytes=VMEM_BYTES),
         cost_estimate=pl.CostEstimate(flops=0, bytes_accessed=32000000, transcendentals=0),
-    )(features, cotangent, valid)
+    )(features, cotangent, valid, w_in, w_out)
 
 
 def softmax_rows(v):
@@ -99,15 +154,17 @@
     return e / jnp.sum(e, axis=0, keepdims=True)
 
 
-def expert_kernel(group, first, last, n_in, *refs):
+def expert_kernel(group, first, last, n_after, skip_rows, *refs):
     names = ["core", "own", "other", "small", "xh", "xl", "ct"]
     names += ["gates"] if first else ["prob"]
     if last:
         names += [f"dp{k}" for k in range(len(GROUPS) - 1)]
-    names += ["dah", "dal", "ex", "keep", "send", "wih", "wil"]
+    names += [f"after{k}" for k in range(n_after)]
+    names += ["dah", "dal", "ex", "wih", "wil"]
+    names += ["keep", "send"] if last else ["grads"]
     if first:
         names += ["prob"]
-    names += ["dl", "gate_keep", "gate_send"] if last else ["dp"]
+    names += ["dl"] if last else ["dp"]
     names += ["win_t", "win_t_low", "wp", "wp_low", "wp_t", "wp_t_low", "b_in", "b_out", "acc_w", "acc_g"]
     names += ["h", "u", "a", "xhat", "h2", "g", "xhh", "xhl", "dzh", "dzl"]
     if last:
@@ -122,13 +179,14 @@
     rows_in, rows_out = depth // devices, units // devices
     rows_all = rows_in + rows_out
     core = r["core"][0]
+    skip = skip_rows * rows_all
     tile = r["xl"].shape[1]
     chunks = [slice(k, k + STEP) for k in range(0, units, STEP)]
 
     @pl.when(step == 0)
     def _():
         for l, e in enumerate(group):
-            base = l * rows_all
+            base = (e - group[0]) * rows_all + skip
             for q in range(pairs):
                 for src, at in ((r["own"], core), (r["other"], 1 - core)):
                     place = q * 2 + at
@@ -285,7 +343,7 @@
             r["dl"][lower:upper] = p * (d - jnp.sum(p * d, axis=0, keepdims=True))
         r["dl"][14:16] = jnp.zeros((2, tile), F32)
         high, low = halves(r["dl"][...])
-        r["acc_gate"][...] += (
+        r["acc_gate"][:, 0:GATES] += (
             dot(r["xh"][0:depth], high, NT) + dot(r["xh"][0:depth], low, NT) + dot(r["xl"][...], high, NT)
         )
 
@@ -295,19 +353,29 @@
             base = l * (rows_all + 8)
             tail = jnp.concatenate([r["acc_g"][l, units : units + 1], r["acc_w"][l, depth : depth + 1]], 0)
             tail = jnp.concatenate([tail] * 4, 0)
+            if last:
+                places = [
+                    (dst, q, q * 2 + at)
+                    for q in range(pairs)
+                    for dst, at in ((r["keep"], core), (r["send"], 1 - core))
+                ]
+            else:
+                places = [(r["grads"], k, k) for k in range(devices)]
+            for dst, q, place in places:
+                dst[q, base : base + rows_in] = r["acc_w"][l, pl.ds(place * rows_in, rows_in)]
+                dst[q, base + rows_in : base + rows_all] = r["acc_g"][l, pl.ds(place * rows_out, rows_out)]
+                dst[q, base + rows_all : base + rows_all + 8] = tail
+        if last:
+            gate = r["acc_gate"][...].T[0:GATES]
+            base = count * (rows_all + 8)
             for q in range(pairs):
+                even = gate[:, 2 * q * rows_in : (2 * q + 1) * rows_in]
+                odd = gate[:, (2 * q + 1) * rows_in : (2 * q + 2) * rows_in]
                 for dst, at in ((r["keep"], core), (r["send"], 1 - core)):
-                    place = q * 2 + at
-                    dst[q, base : base + rows_in] = r["acc_w"][l, pl.ds(place * rows_in, rows_in)]
-                    dst[q, base + rows_in : base + rows_all] = r["acc_g"][l, pl.ds(place * rows_out, rows_out)]
-                    dst[q, base + rows_all : base + rows_all + 8] = tail
-        if last:
-            for q in range(pairs):
-                for dst, at in ((r["gate_keep"], core), (r["gate_send"], 1 - core)):
-                    dst[q] = r["acc_gate"][pl.ds((q * 2 + at) * rows_in, rows_in)]
-
-
-def expert_call(group, core, own, other, small, xh, xl, ct, prob, gates, dps, last):
+                    dst[q, base:, 0:rows_in] = jnp.where(at == 0, even, odd)
+
+
+def expert_call(group, core, own, other, small, xh, xl, ct, prob, gates, dps, last, after, skip):
     first = gates is not None
     pairs, _, units = own.shape
     depth, rows = xl.shape
@@ -335,22 +403,26 @@
     if last:
         ins += dps
         in_specs += [along(8)] * len(dps)
+    ins += after
+    in_specs += [pl.BlockSpec(memory_space=pl.ANY)] * len(after)
     packed = count * (rows_in + rows_out + 8)
     shape = jax.ShapeDtypeStruct
     outs = [
         (along(count * units), shape((count * units, rows), BF16)),
         (along(count * units), shape((count * units, rows), BF16)),
         (along(count * units), shape((count * units, rows), F32)),
-        (whole((pairs, packed, units)), shape((pairs, packed, units), F32)),
-        (whole((pairs, packed, units)), shape((pairs, packed, units), F32)),
         (whole((count, depth, units)), shape((count, depth, units), BF16)),
         (whole((count, depth, units)), shape((count, depth, units), BF16)),
     ]
+    if last:
+        packed += GATES
+        outs += [(whole((pairs, packed, units)), shape((pairs, packed, units), F32))] * 2
+    else:
+        outs.append((whole((devices, packed, units)), shape((devices, packed, units), F32)))
     if first:
         outs.append((along(GATES), shape((GATES, rows), F32)))
     if last:
         outs.append((along(GATES), shape((GATES, rows), F32)))
-        outs += [(whole((pairs, rows_in, GATES)), shape((pairs, rows_in, GATES), F32))] * 2
     else:
         outs.append((along(8), shape((8, rows), F32)))
     top = units + (GATES if first else 0)
@@ -378,9 +450,9 @@
         full(units, BF16),
     ]
     if last:
-        scratch += [pltpu.VMEM((GATES, TILE), F32), pltpu.VMEM((depth, GATES), F32)]
+        scratch += [pltpu.VMEM((GATES, TILE), F32), pltpu.VMEM((depth, LANES), F32)]
     return pl.pallas_call(
-        functools.partial(expert_kernel, group, first, last, len(ins)),
+        functools.partial(expert_kernel, group, first, last, len(after), skip),
         grid=(rows // TILE,),
         in_specs=in_specs,
         out_specs=[o[0] for o in outs],
@@ -396,7 +468,8 @@
 def final_kernel(*refs):
     n = len(GROUPS)
     dahs, dals, exs, wihs, wils = (refs[k * n : (k + 1) * n] for k in range(5))
-    prob_ref, dl_ref, gates_ref, out_ref, gf_ref, gate_ref = refs[5 * n :]
+    prob_ref, dl_ref, gates_ref = refs[5 * n : 5 * n + 3]
+    out_ref, gf_ref, gate_ref = refs[-3:]
     units = out_ref.shape[2]
 
     @pl.when(pl.program_id(0) == 0)
@@ -424,56 +497,107 @@
         out_ref[o] = sums[o].T
 
 
-def final_call(dahs, dals, exs, wihs, wils, prob, dl, gates):
+def final_call(dahs, dals, exs, wihs, wils, prob, dl, gates, part, parts, before, after):
     rows = prob.shape[1]
     _, depth, units = wihs[0].shape
+    steps = rows // TILE // parts
+    skip = part * steps
     whole = lambda a: pl.BlockSpec(a.shape, lambda i: (0,) * a.ndim)
-    along = lambda a: pl.BlockSpec((a.shape[0], TILE), lambda i: (0, i))
+    along = lambda a: pl.BlockSpec((a.shape[0], TILE), lambda i: (0, i + skip))
+    ins = [*dahs, *dals, *exs, *wihs, *wils, prob, dl, gates, *before, *after]
+    n = 5 * len(GROUPS) + 3
     return pl.pallas_call(
         final_kernel,
-        grid=(rows // TILE,),
+        grid=(steps,),
         in_specs=[along(a) for a in (*dahs, *dals, *exs)]
         + [whole(a) for a in (*wihs, *wils)]
-        + [along(prob), along(dl), whole(gates)],
+        + [along(prob), along(dl), whole(gates)]
+        + [pl.BlockSpec(memory_space=pl.ANY)] * (len(before) + len(after)),
         out_specs=[
-            pl.BlockSpec((TASKS + 1, TILE, units), lambda i: (0, i, 0)),
-            pl.BlockSpec((TILE, depth), lambda i: (i, 0)),
+            pl.BlockSpec((TASKS + 1, TILE, units), lambda i: (0, i + skip, 0)),
+            pl.BlockSpec((TILE, depth), lambda i: (i + skip, 0)),
         ],
         out_shape=[
             jax.ShapeDtypeStruct((TASKS + 1, rows, units), F32),
             jax.ShapeDtypeStruct((rows, depth), F32),
         ],
         scratch_shapes=[pltpu.VMEM((3 * GATES, depth), BF16)],
+        input_output_aliases={n + k: k for k in range(len(before))},
         compiler_params=pltpu.CompilerParams(vmem_limit_bytes=VMEM_BYTES),
-        cost_estimate=pl.CostEstimate(flops=15000000000, bytes_accessed=50000000, transcendentals=0),
-    )(*dahs, *dals, *exs, *wihs, *wils, prob, dl, gates)
-
-
-def local(features, cotangent, valid, core, owns, others, small, gates):
-    xh, xl, ct = prep(features, cotangent, valid)
-    prob, dps = None, []
-    kept, sent, dahs, dals, exs, wihs, wils = [], [], [], [], [], [], []
+        cost_estimate=pl.CostEstimate(
+            flops=15000000000 // parts, bytes_accessed=50000000 // parts, transcendentals=0
+        ),
+    )(*ins)
+
+
+def finish_kernel(me_ref, *refs):
+    n = len(GROUPS)
+    halves_of = refs[: 2 * n]
+    w_out_ref, gain_ref, shift_ref = refs[2 * n : 2 * n + 3]
+    g_in, g_in_bias, g_gain, g_shift, g_out, g_out_bias, g_task, g_shared = refs[2 * n + 3 :]
+    rows_in, rows_out, units = g_in.shape[1], g_out.shape[1], g_in.shape[2]
+    me = me_ref[0]
+
+    def own(row):
+        value = row[:, 0:rows_out]
+        for p in range(1, units // rows_out):
+            value = jnp.where(me == p, row[:, p * rows_out : (p + 1) * rows_out], value)
+        return value
+
+    def as_row(col):
+        return jnp.broadcast_to(col, (rows_out, LANES)).T[0:1]
+
     for k, group in enumerate(GROUPS):
-        last = k == len(GROUPS) - 1
-        got = expert_call(
-            group, core, owns[k], others[k], small, xh, xl, ct, prob, None if k else gates, dps, last
-        )
-        dah, dal, ex, keep, send, wih, wil = got[:7]
-        rest = list(got[7:])
-        if k == 0:
-            prob = rest.pop(0)
-        kept.append([keep])
-        sent.append([send])
-        if last:
-            dl = rest[0]
-            kept[-1].append(rest[1])
-            sent[-1].append(rest[2])
-        else:
-            dps.append(rest[0])
-        for to, what in ((dahs, dah), (dals, dal), (exs, ex), (wihs, wih), (wils, wil)):
-            to.append(what)
-    outputs, grad_features = final_call(dahs, dals, exs, wihs, wils, prob, dl, gates)
-    return outputs, grad_features, kept, sent
+        a, b = halves_of[2 * k], halves_of[2 * k + 1]
+        add = lambda lower, upper: a[lower:upper] + b[lower:upper]
+        at = 0
+        for e in group:
+            g_in[e] = add(at, at + rows_in)
+            at += rows_in
+            raw = add(at, at + rows_out)
+            at += rows_out
+            tail = add(at, at + 8)
+            at += 8
+            total = tail[0:1]
+            gain = wide(column(gain_ref[e : e + 1]), units)
+            shift = wide(column(shift_ref[e : e + 1]), units)
+            g_out[e] = gain * raw + shift * total
+            w = w_out_ref[e]
+            g_gain[e : e + 1] = as_row(jnp.sum(w * raw, axis=1, keepdims=True))
+            g_shift[e : e + 1] = as_row(jnp.sum(w * total, axis=1, keepdims=True))
+            g_in_bias[e : e + 1] = own(tail[1:2])
+            g_out_bias[e : e + 1] = own(total)
+    gate = add(at, at + GATES)[:, 0:rows_in]
+    m = SPEC + SHARED
+    for t in range(TASKS):
+        g_task[t] = gate[t * m : (t + 1) * m]
+    g_shared[...] = gate[TASKS * m : TASKS * m + EXPERTS]
+
+
+def finish(me, totals, w_in, w_out, gain, shift):
+    experts, rows_in, units = w_in.shape
+    rows_out = w_out.shape[1]
+    shape = lambda *s: jax.ShapeDtypeStruct(s, F32)
+    vector = shape(experts, rows_out)
+    outs = [
+        shape(*w_in.shape),
+        vector,
+        vector,
+        vector,
+        shape(*w_out.shape),
+        vector,
+        shape(TASKS, SPEC + SHARED, rows_in),
+        shape(EXPERTS, rows_in),
+    ]
+    vmem = pl.BlockSpec(memory_space=pltpu.VMEM)
+    got = pl.pallas_call(
+        finish_kernel,
+        in_specs=[pl.BlockSpec(memory_space=pltpu.SMEM)] + [vmem] * (len(totals) + 3),
+        out_specs=[vmem] * len(outs),
+        out_shape=outs,
+        compiler_params=pltpu.CompilerParams(vmem_limit_bytes=VMEM_BYTES),
+    )(me, *totals, w_out, gain, shift)
+    return (*got[:6], got[6].transpose(0, 2, 1), got[7].T)
 
 
 def make(mesh):
@@ -482,21 +606,18 @@
     across = [[q * 2 + c for q in range(pairs)] for c in range(2)]
     twin = [(i, i ^ 1) for i in range(n_fsdp)]
 
-    def gather(x):
-        spread = jnp.broadcast_to(x[None], (pairs, *x.shape))
-        own = lax.all_to_all(spread, "fsdp", 0, 0, axis_index_groups=across)
-        return own, lax.ppermute(own, "fsdp", twin)
-
-    def scatter(keep, send):
-        got = keep + lax.ppermute(send, "fsdp", twin)
-        return jnp.sum(lax.all_to_all(got, "fsdp", 0, 0, axis_index_groups=across), 0)
-
-    def replicas(x):
-        bit = 1
-        while bit < n_dp:
-            x = x + lax.ppermute(x, "dp", [(i, i ^ bit) for i in range(n_dp)])
-            bit *= 2
+    def spread_out(x):
+        return lax.all_to_all(x, "fsdp", 0, 0, axis_index_groups=across)
+
+    def swap(x, bit):
+        return lax.ppermute(x, "dp", [(i, i ^ bit) for i in range(n_dp)])
+
+    def reduce_some(x, some, beside):
+        for bit in some:
+            x = x + tie(swap(x, bit), beside)
         return x
+
+    bits = [1 << k for k in range(n_dp.bit_length() - 1)]
 
     def on_device(
         features, cotangent, counts, keep, w_in, in_bias, norm_gain, norm_bias, w_out, out_bias, task_gate, shared_gate
@@ -508,62 +629,48 @@
         valid = (lax.broadcasted_iota(jnp.int32, (1, rows), 1) < counts[0]) & (keep.reshape(1, rows) > 0)
         me = lax.axis_index("fsdp")
         core = (me % 2).astype(jnp.int32).reshape(1)
-        biases = jnp.concatenate([in_bias, norm_gain, norm_bias, out_bias], 0)
-        gate = jnp.concatenate([task_gate[0].T, task_gate[1].T, shared_gate.T], 0)
-        gate = jnp.pad(gate, ((0, GATES - gate.shape[0]), (0, units - rows_in)))
-        extra = jnp.concatenate([jnp.pad(biases, ((0, 0), (0, units - rows_out))), gate], 0)
-        owns, others = [], []
-        for k, group in enumerate(GROUPS):
-            parts = []
-            for e in group:
-                parts += [w_in[e], w_out[e]]
-            if k == 0:
-                parts.append(extra)
-            own, other = gather(jnp.concatenate(parts, 0))
-            owns.append(own)
-            others.append(other)
+        xh, xl, ct, spread = prep(features, cotangent, valid.astype(F32), w_in, w_out, pairs)
+        own0 = tie(
+            spread_out(
+                pack(pairs, w_in, in_bias, norm_gain, norm_bias, w_out, out_bias, task_gate, shared_gate)
+            ),
+            [xh],
+        )
+        other0 = lax.ppermute(own0, "fsdp", twin)
         begin = len(GROUPS[0]) * (rows_in + rows_out)
-        mine, theirs = owns[0][:, begin:], others[0][:, begin:]
+        mine, theirs = own0[:, begin:], other0[:, begin:]
         both = jnp.where(core[0] == 0, jnp.stack([mine, theirs], 1), jnp.stack([theirs, mine], 1))
         both = both.reshape(n_fsdp, *both.shape[2:])
-        n_bias = biases.shape[0]
+        n_bias = 4 * EXPERTS
         small = both[:, :n_bias, :rows_out].transpose(1, 0, 2).reshape(n_bias, units)
         gates = both[:, n_bias:, :rows_in].transpose(1, 0, 2).reshape(GATES, depth)
 
-        outputs, grad_features, kept, sent = local(
-            features, cotangent, valid.astype(F32), core, owns, others, small, gates
+        first = expert_call(GROUPS[0], core, own0, other0, small, xh, xl, ct, None, gates, [], False, [], 0)
+        prob = first[6]
+        own1 = tie(spread_out(spread), [first[7]])
+        other1 = lax.ppermute(own1, "fsdp", twin)
+        second = expert_call(GROUPS[1], core, own1, other1, small, xh, xl, ct, prob, None, [], False, [], 0)
+        sum0 = jnp.sum(tie(lax.all_to_all(first[5], "fsdp", 0, 0), [second[6]]), 0)
+        third = expert_call(
+            GROUPS[2], core, own1, other1, small, xh, xl, ct, prob, None, [first[7], second[6]], True, [sum0], len(GROUPS[1])
         )
-
-        g_in, g_in_bias, g_gain, g_shift, g_out, g_out_bias = [], [], [], [], [], []
-        for k, group in enumerate(GROUPS):
-            total = replicas(scatter(kept[k][0], sent[k][0]))
-            for l, e in enumerate(group):
-                base = l * (rows_in + rows_out + 8)
-                g_in.append(total[base : base + rows_in])
-                raw = total[base + rows_in : base + rows_in + rows_out]
-                tail = total[base + rows_in + rows_out :]
-                column_sum = tail[0]
-                g_in_bias.append(lax.dynamic_slice(tail[1], (me * rows_out,), (rows_out,)))
-                g_out_bias.append(lax.dynamic_slice(column_sum, (me * rows_out,), (rows_out,)))
-                g_out.append(norm_gain[e][:, None] * raw + norm_bias[e][:, None] * column_sum[None])
-                g_gain.append(jnp.sum(w_out[e] * raw, 1))
-                g_shift.append(jnp.sum(w_out[e] * column_sum[None], 1))
-        gate_sum = replicas(scatter(kept[-1][1], sent[-1][1]))
-        n_task = SPEC + SHARED
-        g_task = jnp.stack([gate_sum[:, t * n_task : (t + 1) * n_task] for t in range(TASKS)])
-        g_shared = gate_sum[:, TASKS * n_task : TASKS * n_task + EXPERTS]
-        return (
-            outputs,
-            grad_features,
-            jnp.stack(g_in),
-            jnp.stack(g_in_bias),
-            jnp.stack(g_gain),
-            jnp.stack(g_shift),
-            jnp.stack(g_out),
-            jnp.stack(g_out_bias),
-            g_task,
-            g_shared,
+        dl = third[7]
+        sum1 = jnp.sum(tie(lax.all_to_all(second[5], "fsdp", 0, 0), [dl]), 0)
+        sum0 = reduce_some(sum0, bits[:-1], [dl])
+        dahs, dals, exs, wihs, wils = zip(first[:5], second[:5], third[:5])
+        kept = third[5] + lax.ppermute(tie(third[6], [sum0, sum1]), "fsdp", twin)
+        part = final_call(dahs, dals, exs, wihs, wils, prob, dl, gates, 0, 2, [], [])
+        sum2 = jnp.sum(tie(spread_out(kept), [part[1]]), 0)
+        pair0 = (sum0, tie(swap(sum0, bits[-1]), [part[1]]))
+        sum1 = reduce_some(sum1, bits[:-1], [part[1]])
+        outputs, grad_features = final_call(
+            dahs, dals, exs, wihs, wils, prob, dl, gates, 1, 2, part, [pair0[1], sum1, sum2]
         )
+        pair1 = (sum1, tie(swap(sum1, bits[-1]), [grad_features]))
+        sum2 = tie(reduce_some(sum2, bits[:-1], [grad_features]), [pair1[1]])
+        pair2 = (sum2, swap(sum2, bits[-1]))
+        rest = finish(me.astype(jnp.int32).reshape(1), (*pair0, *pair1, *pair2), w_in, w_out, norm_gain, norm_bias)
+        return (outputs, grad_features, *rest)
 
     return on_device
 

time: 267 us -> 216 us (0.81)
  waiting for transfers between devices: 61.9 us -> 11.2 us
  Pallas kernels: 134 us -> 147 us
  starting transfers between devices: 41.1 us -> 31.3 us
  local copies, waits for them, and re-layouts: 17.1 us -> 12.4 us
    all_to_all x7 -> x5, waiting for transfers between devices: 33.1 us -> 0.01 us  [the longest x3 0.01 us: spread_out(): return lax.all_to_all(x, 'fsdp', 0, 0, axis_index_groups=across)]
    ppermute x15 -> x9, waiting for transfers between devices: 28.8 us -> 11.2 us  [the longest x6 11.2 us: swap(): return lax.ppermute(x, 'dp', [(i, i ^ bit) for i in range(n_dp)])]
    pallas_call x4 -> x19, Pallas kernels: 120 us -> 133 us  [the longest x3 94.6 us: expert_call(): pl.pallas_call(functools.partial(expert_kernel, group, first, last, len(a...]
    all_to_all x7 -> x5, starting transfers between devices: 27.2 us -> 21.5 us  [the longest x3 13.2 us: spread_out(): return lax.all_to_all(x, 'fsdp', 0, 0, axis_index_groups=across)]
    reduce_sum x6 -> x3, other arithmetic: 0.56 us -> 5.79 us  [the longest x1 2.26 us: on_device(): sum1 = jnp.sum(tie(lax.all_to_all(second[5], 'fsdp', 0, 0), [dl]), 0)]
    unnamed x39 -> x38, local copies, waits for them, and re-layouts: 4.86 us -> 9.87 us
    ppermute x15 -> x9, starting transfers between devices: 13.9 us -> 9.77 us  [the longest x6 9.35 us: swap(): return lax.ppermute(x, 'dp', [(i, i ^ bit) for i in range(n_dp)])]
    broadcast_in_dim x3 -> x0, local copies, waits for them, and re-layouts: 3.03 us -> none  [gather(): spread = jnp.broadcast_to(x[None], (pairs, *x.shape))]
  transfers between devices with their start and end apart: 22 -> 14, of which waited for: 10 -> 1; matrix products, arithmetic and copies ran while one was open for 6% -> 5% of each run, Pallas kernels for 50% -> 65%
where the time goes in v2:
time: 216 us; the launch traced here: 215 us
  Pallas kernels  147 us (68%)
  starting transfers between devices  31.3 us (14%)
  local copies, waits for them, and re-layouts  12.4 us (6%)
  other arithmetic  12 us (6%)
  waiting for transfers between devices  11.2 us (5%)
    pallas_call x3, Pallas kernels, expert_call(): pl.pallas_call(functools.partial(expert_kernel, group, first, last, len(a...  94.6 us
    pallas_call x2, Pallas kernels, final_call(): pl.pallas_call(final_kernel, grid=(steps,), in_specs=[along(a) for a in (...  31.9 us
    pallas_call x1, Pallas kernels, prep(): pl.pallas_call(prep_kernel, grid=(rows // TILE,), in_specs=[pl.BlockSpec(...  14.1 us
    all_to_all x3, starting transfers between devices, spread_out(): return lax.all_to_all(x, 'fsdp', 0, 0, axis_index_groups=across)  13.2 us
    ppermute x6, waiting for transfers between devices, swap(): return lax.ppermute(x, 'dp', [(i, i ^ bit) for i in range(n_dp)])  11.2 us
    unnamed x38, local copies, waits for them, and re-layouts  9.87 us
    ppermute x6, starting transfers between devices, swap(): return lax.ppermute(x, 'dp', [(i, i ^ bit) for i in range(n_dp)])  9.35 us
    add x3, other arithmetic, reduce_some(): x = x + tie(swap(x, bit), beside)  4.48 us
  transfers between devices with their start and end apart: 14, of which 1 were waited for; matrix products, arithmetic and copies ran while one was open for 5% of the time, Pallas kernels for 65%

profile of v2, /device:TPU:0, one launch (start us, length us, event | category | flops | bytes accessed | tf_op | source)
XLA Modules:
  0.0 215.2 jit_solution(339249459644191146)
XLA Ops:
  0.7 2.2 %shard_map.195 = f32[4,232,256]{2,1,0:T(8,128)} custom-call(f32[6,32]{1,0:T(8,128)} %in_bias.1, f32[6,32]{1,0:T(8,128)} %refs_7_.1, f32[6,32]{1,0:T(8,128)} %refs_8_.1, f32[6,32]{1,0:T(8,128)} %out_bias.1, f32[2,4,64]{2,1,0:T(4,128)} %bitcast.21, f32[6,64]{1,0:T(8,128)} %bitcast.22, f32[6,64,256]{2,1,0:T(8,128)} %w_in_ref.3, f32[6,32,256]{2,1,0:T(8,128)} %refs_6_.1), custom_call_target="tpu_custom_call" | custom-call | tf_op jit(solution)/shard_map/pallas_call | solution.py:98
  2.8 5.2 %all-to-all-start = ((f32[4,232,256]{2,1,0:T(8,128)}), f32[4,232,256]{2,1,0:T(8,128)S(1)}, u32[]{:S(2)}, u32[]{:S(2)}) async-start(f32[4,232,256]{2,1,0:T(8,128)} %shard_map.195), calls=%async_computation | async-start | bytes 1900544 | tf_op jit(solution)/shard_map/all_to_all | solution.py:610
  9.2 14.1 %shard_map.196 = (bf16[528,3072]{1,0:T(8,128)(2,1)}, bf16[512,3072]{1,0:T(8,128)(2,1)}, f32[3,256,3072]{2,1,0:T(8,128)}, f32[4,384,256]{2,1,0:T(8,128)}) custom-call(f32[3072,512]{1,0:T(8,128)} %x_ref.1, f32[3,3072,256]{2,1,0:T(8,128)} %c_ref.1, f32[1,3072]{1,0:T(1,128)} %bitcast.20, f32[6,64,256]{2,1,0:T(8,128)} %w_in_ref.3, f32[6,32,256]{2,1,0:T(8,128)} %refs_6_.1), custom_call_target="tpu_custom_call" | custom-call | bytes 32000000 | tf_op jit(solution)/shard_map/pallas_call | solution.py:125
  24.3 4.2 %all-to-all-start.1 = ((f32[4,384,256]{2,1,0:T(8,128)}), f32[4,384,256]{2,1,0:T(8,128)S(1)}, u32[]{:S(2)}, u32[]{:S(2)}) async-start(f32[4,384,256]{2,1,0:T(8,128)} %get-tuple-element.53), calls=%async_computation.1 | async-start | bytes 3145728 | tf_op jit(solution)/shard_map/all_to_all | solution.py:610
  31.1 30.7 %shard_map.198 = (bf16[512,3072]{1,0:T(8,128)(2,1)}, bf16[512,3072]{1,0:T(8,128)(2,1)}, f32[512,3072]{1,0:T(8,128)}, bf16[2,512,256]{2,1,0:T(8,128)(2,1)}, bf16[...) custom-call(s32[1]{0:T(128)} %bitcast.refs_0_, ...), custom_call_target="tpu_custom_call" | custom-call | flops 20000000000 | bytes 30000000 | tf_op jit(solution)/shard_map/pallas_call | solution.py:454
  63.2 4.1 %all-to-all-start.2 = ((f32[8,208,256]{2,1,0:T(8,128)}), f32[8,208,256]{2,1,0:T(8,128)S(1)}, u32[]{:S(2)}, u32[]{:S(2)}) async-start(f32[8,208,256]{2,1,0:T(8,128)} %get-tuple-element.58), calls=%async_computation.2 | async-start | bytes 3407872 | tf_op jit(solution)/shard_map/all_to_all | solution.py:653
  67.3 1.2 copy-done.18
  68.5 30.7 %shard_map.200 = (bf16[512,3072]{1,0:T(8,128)(2,1)}, bf16[512,3072]{1,0:T(8,128)(2,1)}, f32[512,3072]{1,0:T(8,128)}, bf16[2,512,256]{2,1,0:T(8,128)(2,1)}, bf16[...) custom-call(s32[1]{0:T(128)} %bitcast.refs_0_, f32[4,384,256]{2,1,0:T(8,128)} %shard_map.199.refs_1_, ...), custom_call_target="tpu_custom_call" | custom-call | flops 20000000000 | bytes 30000000 | tf_op jit(solution)/shard_map/pallas_call | solution.py:454
  99.2 4.2 %all-to-all-start.3 = ((f32[8,208,256]{2,1,0:T(8,128)}), f32[8,208,256]{2,1,0:T(8,128)S(1)}, u32[]{:S(2)}, u32[]{:S(2)}) async-start(f32[8,208,256]{2,1,0:T(8,128)} %get-tuple-element.75), calls=%async_computation.3 | async-start | bytes 3407872 | tf_op jit(solution)/shard_map/all_to_all | solution.py:658
  103.4 1.6 reduce_sum.27.refs_10_
  105.0 1.6 collective-permute-start.2
  106.6 33.3 %shard_map.202 = (bf16[512,3072]{1,0:T(8,128)(2,1)}, bf16[512,3072]{1,0:T(8,128)(2,1)}, f32[512,3072]{1,0:T(8,128)}, bf16[2,512,256]{2,1,0:T(8,128)(2,1)}, bf16[...) custom-call(s32[1]{0:T(128)} %bitcast.refs_0_, ...), custom_call_target="tpu_custom_call" | custom-call | flops 20000000000 | bytes 30000000 | tf_op jit(solution)/shard_map/pallas_call | solution.py:454
  140.6 1.7 add.17.refs_1_.refs_0_
  143.6 2.3 %reduce_sum.28.refs_2_ = f32[208,256]{1,0:T(8,128)} reduce(f32[8,208,256]{2,1,0:T(8,128)} %shard_map.206, f32[]{:T(128)} %constant.20.clone.1), dimensions={0}, to_apply=%region_1.2 | reduce | flops 372736 | bytes 1916932 | tf_op jit(solution)/shard_map/reduce_sum | solution.py:658
  146.0 2.6 %collective-permute-start.3 = (f32[208,256]{1,0:T(8,128)S(1)}, f32[208,256]{1,0:T(8,128)S(1)}, u32[]{:S(2)}, u32[]{:S(2)}) collective-permute-start(f32[208,256]{1,0:T(8,128)S(1)} %copy-done.7), channel_id=1, source_target_pairs={{0,16},{8,24},{16,0},{24,8},{1,17},{9,25},{17,1},{25,9},{2,18},{10... | collective-permute-start | bytes 638984 | tf_op jit(solution)/shard_map/ppermute | solution.py:613
  150.6 3.8 %all-to-all-start.4 = ((f32[4,224,256]{2,1,0:T(8,128)}), f32[4,224,256]{2,1,0:T(8,128)S(1)}, u32[]{:S(2)}, u32[]{:S(2)}) async-start(f32[4,224,256]{2,1,0:T(8,128)} %add.19), calls=%async_computation.4 | async-start | bytes 1835008 | tf_op jit(solution)/shard_map/all_to_all | solution.py:610
  154.5 16.0 %shard_map.203 = (f32[3,3072,256]{2,1,0:T(8,128)}, f32[3072,512]{1,0:T(8,128)}) custom-call(bf16[512,3072]{1,0:T(8,128)(2,1)} %get-tuple-element.52.refs_0_, bf16[512,3072]{1,0:T(8,128)(2,1)} %get-tuple-element.56.refs_1_, bf16[512,3072]{1,0:T(8,128)(2,1)} %get-tuple-element.59.refs_2_, bf16[512,3072]{1,0:T(8,128)(2,1)} %get-tuple-element.60.refs_3_, ...), custom_call_target="tpu_custom_call" | custom-call | flops 7500000256 | bytes 25000000 | tf_op jit(solution)/shard_map/pallas_call | solution.py:509
  173.1 2.0 collective-permute-start.6
  176.0 1.9 reduce_sum.29.refs_22_
  178.6 16.0 %shard_map.210 = (f32[3,3072,256]{2,1,0:T(8,128)}, f32[3072,512]{1,0:T(8,128)}) custom-call(bf16[512,3072]{1,0:T(8,128)(2,1)} %get-tuple-element.52.refs_0_, bf16[512,3072]{1,0:T(8,128)(2,1)} %get-tuple-element.56.refs_1_, bf16[512,3072]{1,0:T(8,128)(2,1)} %get-tuple-element.59.refs_2_, ...), custom_call_target="tpu_custom_call", output_to_operand_aliasing={{0}: (18, {}), {1}: (19, {})} | custom-call | flops 7500000256 | bytes 25000000 | tf_op jit(solution)/shard_map/pallas_call | solution.py:509
  196.0 1.8 add.20.refs_0_
  197.7 1.7 collective-permute-start.8
  199.4 11.2 %collective-permute-done.8.refs_5_ = f32[224,256]{1,0:T(8,128)S(1)} collective-permute-done((f32[224,256]{1,0:T(8,128)}, f32[224,256]{1,0:T(8,128)S(1)}, u32[]{:S(2)}, u32[]{:S(2)}) %collective-permute-start.8) | collective-permute-done | bytes 229408 | tf_op jit(solution)/shard_map/ppermute | solution.py:613
  211.3 3.8 %shard_map.214 = (f32[6,64,256]{2,1,0:T(8,128)}, f32[6,32]{1,0:T(8,128)}, f32[6,32]{1,0:T(8,128)}, f32[6,32]{1,0:T(8,128)}, f32[6,32,256]{2,1,0:T(8,128)}, /*ind...) custom-call(s32[1]{0:T(128)} %bitcast.10.me_ref, f32[208,256]{1,0:T(8,128)} %add.17.refs_1_.refs_0_, ...), custom_call_target="tpu_custom_call" | custom-call | tf_op jit(solution)/shard_map/pallas_call | solution.py:593
  (80 shorter events, 15.8 us)
Async XLA Ops:
  0.6 8.0 %copy-start.17 = (s32[3072]{0:T(1024)S(1)}, s32[3072]{0:T(1024)}, u32[]{:S(2)}) copy-start(s32[3072]{0:T(1024)} %param.15) | copy-start | bytes 36868
  2.8 20.5 %all-to-all-start = ((f32[4,232,256]{2,1,0:T(8,128)}), f32[4,232,256]{2,1,0:T(8,128)S(1)}, u32[]{:S(2)}, u32[]{:S(2)}) async-start(f32[4,232,256]{2,1,0:T(8,128)} %shard_map.195), calls=%async_computation | async-start | bytes 1900544 | tf_op jit(solution)/shard_map/all_to_all | solution.py:610
  24.3 5.1 %collective-permute-start = (f32[4,232,256]{2,1,0:T(8,128)}, f32[4,232,256]{2,1,0:T(8,128)S(1)}, u32[]{:S(2)}, u32[]{:S(2)}) collective-permute-start(f32[4,232,256]{2,1,0:T(8,128)} %shard_map.197.refs_1_), channel_id=1, source_target_pairs={{0,1},{1,0},{2,3},{3,2},{4,5},{5,4},{6,7},{7,6},{8,9},{9,8},{10,11... | collective-permute-start | bytes 2850824 | tf_op jit(solution)/shard_map/ppermute | solution.py:639
  24.3 37.5 %all-to-all-start.1 = ((f32[4,384,256]{2,1,0:T(8,128)}), f32[4,384,256]{2,1,0:T(8,128)S(1)}, u32[]{:S(2)}, u32[]{:S(2)}) async-start(f32[4,384,256]{2,1,0:T(8,128)} %get-tuple-element.53), calls=%async_computation.1 | async-start | bytes 3145728 | tf_op jit(solution)/shard_map/all_to_all | solution.py:610
  29.4 1.7 copy-start.16
  61.8 1.2 copy-start.3
  63.0 4.3 %collective-permute-start.1 = (f32[4,384,256]{2,1,0:T(8,128)}, f32[4,384,256]{2,1,0:T(8,128)S(1)}, u32[]{:S(2)}, u32[]{:S(2)}) collective-permute-start(f32[4,384,256]{2,1,0:T(8,128)} %shard_map.199.refs_1_), channel_id=1, source_target_pairs={{0,1},{1,0},{2,3},{3,2},{4,5},{5,4},{6,7},{7,6},{8,9},{9,8},{10,11... | collective-permute-start | bytes 4718600 | tf_op jit(solution)/shard_map/ppermute | solution.py:651
  63.2 36.0 %all-to-all-start.2 = ((f32[8,208,256]{2,1,0:T(8,128)}), f32[8,208,256]{2,1,0:T(8,128)S(1)}, u32[]{:S(2)}, u32[]{:S(2)}) async-start(f32[8,208,256]{2,1,0:T(8,128)} %get-tuple-element.58), calls=%async_computation.2 | async-start | bytes 3407872 | tf_op jit(solution)/shard_map/all_to_all | solution.py:653
  67.3 1.2 copy-start.18
  99.2 4.2 %copy-start.1 = (f32[8,208,256]{2,1,0:T(8,128)}, f32[8,208,256]{2,1,0:T(8,128)S(1)}, u32[]{:S(2)}) copy-start(f32[8,208,256]{2,1,0:T(8,128)S(1)} %all-to-all-done.2.refs_0_) | copy-start | bytes 5111812
  99.2 43.2 %all-to-all-start.3 = ((f32[8,208,256]{2,1,0:T(8,128)}), f32[8,208,256]{2,1,0:T(8,128)S(1)}, u32[]{:S(2)}, u32[]{:S(2)}) async-start(f32[8,208,256]{2,1,0:T(8,128)} %get-tuple-element.75), calls=%async_computation.3 | async-start | bytes 3407872 | tf_op jit(solution)/shard_map/all_to_all | solution.py:658
  105.0 1.6 copy-start.13
  105.0 34.9 %collective-permute-start.2 = (f32[208,256]{1,0:T(8,128)S(1)}, f32[208,256]{1,0:T(8,128)S(1)}, u32[]{:S(2)}, u32[]{:S(2)}) collective-permute-start(f32[208,256]{1,0:T(8,128)S(1)} %reduce_sum.27.refs_10_), channel_id=1, source_target_pairs={{0,8},{8,0},{16,24},{24,16},{1,9},{9,1},{17,25},{25,17},{2,10},{10... | collective-permute-start | bytes 638984 | tf_op jit(solution)/shard_map/ppermute | solution.py:613
  142.4 3.7 %copy-start.7 = (f32[208,256]{1,0:T(8,128)S(1)}, f32[208,256]{1,0:T(8,128)}, u32[]{:S(2)}) copy-start(f32[208,256]{1,0:T(8,128)} %add.17.refs_1_.refs_0_) | copy-start | bytes 638980
  142.4 7.2 %copy-start.10 = (f32[4,224,256]{2,1,0:T(8,128)S(1)}, f32[4,224,256]{2,1,0:T(8,128)}, u32[]{:S(2)}) copy-start(f32[4,224,256]{2,1,0:T(8,128)} %get-tuple-element.76) | copy-start | bytes 2752516
  142.4 1.2 copy-start
  145.8 3.7 %collective-permute-start.5 = (f32[4,224,256]{2,1,0:T(8,128)}, f32[4,224,256]{2,1,0:T(8,128)S(1)}, u32[]{:S(2)}, u32[]{:S(2)}) collective-permute-start(f32[4,224,256]{2,1,0:T(8,128)} %shard_map.208), channel_id=1, source_target_pairs={{0,1},{1,0},{2,3},{3,2},{4,5},{5,4},{6,7},{7,6},{8,9},{9,8},{10,11... | collective-permute-start | bytes 2752520 | tf_op jit(solution)/shard_map/ppermute | solution.py:661
  146.0 24.4 %collective-permute-start.3 = (f32[208,256]{1,0:T(8,128)S(1)}, f32[208,256]{1,0:T(8,128)S(1)}, u32[]{:S(2)}, u32[]{:S(2)}) collective-permute-start(f32[208,256]{1,0:T(8,128)S(1)} %copy-done.7), channel_id=1, source_target_pairs={{0,16},{8,24},{16,0},{24,8},{1,17},{9,25},{17,1},{25,9},{2,18},{10... | collective-permute-start | bytes 638984 | tf_op jit(solution)/shard_map/ppermute | solution.py:613
  148.6 22.5 %collective-permute-start.4 = (f32[208,256]{1,0:T(8,128)}, f32[208,256]{1,0:T(8,128)S(1)}, u32[]{:S(2)}, u32[]{:S(2)}) collective-permute-start(f32[208,256]{1,0:T(8,128)} %reduce_sum.28.refs_2_), channel_id=1, source_target_pairs={{0,8},{8,0},{16,24},{24,16},{1,9},{9,1},{17,25},{25,17},{2,10},{10... | collective-permute-start | bytes 638984 | tf_op jit(solution)/shard_map/ppermute | solution.py:613
  150.6 24.5 %all-to-all-start.4 = ((f32[4,224,256]{2,1,0:T(8,128)}), f32[4,224,256]{2,1,0:T(8,128)S(1)}, u32[]{:S(2)}, u32[]{:S(2)}) async-start(f32[4,224,256]{2,1,0:T(8,128)} %add.19), calls=%async_computation.4 | async-start | bytes 1835008 | tf_op jit(solution)/shard_map/all_to_all | solution.py:610
  173.1 5.5 %copy-start.5 = (f32[208,256]{1,0:T(8,128)}, f32[208,256]{1,0:T(8,128)S(1)}, u32[]{:S(2)}) copy-start(f32[208,256]{1,0:T(8,128)S(1)} %add.18.refs_21_.refs_2_) | copy-start | bytes 638980
  173.1 21.5 %collective-permute-start.6 = (f32[208,256]{1,0:T(8,128)S(1)}, f32[208,256]{1,0:T(8,128)S(1)}, u32[]{:S(2)}, u32[]{:S(2)}) collective-permute-start(f32[208,256]{1,0:T(8,128)S(1)} %add.18.refs_21_.refs_2_), channel_id=1, source_target_pairs={{0,16},{8,24},{16,0},{24,8},{1,17},{9,25},{17,1},{25,9},{2,18},{10... | collective-permute-start | bytes 638984 | tf_op jit(solution)/shard_map/ppermute | solution.py:613
  178.0 17.3 %collective-permute-start.7 = (f32[224,256]{1,0:T(8,128)}, f32[224,256]{1,0:T(8,128)S(1)}, u32[]{:S(2)}, u32[]{:S(2)}) collective-permute-start(f32[224,256]{1,0:T(8,128)} %reduce_sum.29.refs_22_), channel_id=1, source_target_pairs={{0,8},{8,0},{16,24},{24,16},{1,9},{9,1},{17,25},{25,17},{2,10},{10... | collective-permute-start | bytes 688136 | tf_op jit(solution)/shard_map/ppermute | solution.py:613
  197.7 12.8 %collective-permute-start.8 = (f32[224,256]{1,0:T(8,128)}, f32[224,256]{1,0:T(8,128)S(1)}, u32[]{:S(2)}, u32[]{:S(2)}) collective-permute-start(f32[224,256]{1,0:T(8,128)} %shard_map.213.refs_4_), channel_id=1, source_target_pairs={{0,16},{8,24},{16,0},{24,8},{1,17},{9,25},{17,1},{25,9},{2,18},{10... | collective-permute-start | bytes 688136 | tf_op jit(solution)/shard_map/ppermute | solution.py:613
  (9 other events, 7.0 us)

commit v3 on v2

v3 whole, which is shorter than its diff:
```python
import functools

import jax
import jax.numpy as jnp
from jax import lax
from jax.experimental import pallas as pl
from jax.experimental.pallas import tpu as pltpu
from jax.sharding import PartitionSpec as P

TASKS = 2
SPEC = 2
SHARED = 2
EXPERTS = 6
EPSILON = 1e-05
GROUPS = ((0, 1), (2, 3), (4, 5))
TILE = 512
STEP = 16
TOKEN = (8, 128)
SPAN = 256
ORDER = (('in', 0), ('in', 1), ('norm', 0), ('in', 2), ('norm', 1), ('in', 3), ('out', 0), ('norm', 2), ('out', 1), ('norm', 3), ('comb', 0), ('out', 2), ('comb', 1), ('out', 3), ('back', 0), ('comb', 2), ('back', 1), ('comb', 3), ('go', 0), ('bnorm', 0), ('back', 2), ('bnorm', 1), ('back', 3), ('gi', 0), ('bnorm', 2), ('go', 1), ('bnorm', 3), ('gi', 1))
LANES = 128
GATES = 16
F32 = jnp.float32
BF16 = jnp.bfloat16
VMEM_BYTES = 58 << 20

NN = (((1,), (0,)), ((), ()))
NT = (((1,), (1,)), ((), ()))
TN = (((0,), (0,)), ((), ()))


def uses(expert):
    if expert >= TASKS * SPEC:
        shared = expert - TASKS * SPEC
        first = [(t, t * (SPEC + SHARED) + SPEC + shared) for t in range(TASKS)]
    else:
        t = expert // SPEC
        first = [(t, t * (SPEC + SHARED) + expert % SPEC)]
    return first + [(TASKS, TASKS * (SPEC + SHARED) + expert)]


def halves(v):
    high = v.astype(BF16)
    return high, (v - high.astype(F32)).astype(BF16)


def dot(a, b, dims):
    return lax.dot_general(a, b, dims, preferred_element_type=F32)


def dot3(a_high, a_low, b_high, b_low, dims):
    return dot(a_high, b_high, dims) + dot(a_low, b_high, dims) + dot(a_high, b_low, dims)


def column(row):
    return jnp.broadcast_to(row, (LANES, row.shape[1])).T


def wide(block, width):
    return jnp.concatenate([block] * (width // LANES), axis=1)


def tie(x, after):
    return pl.pallas_call(
        lambda *refs: None,
        in_specs=[pl.BlockSpec(memory_space=pl.ANY)] + [pl.BlockSpec(memory_space=pltpu.HBM)] * len(after),
        out_specs=pl.BlockSpec(memory_space=pl.ANY),
        out_shape=jax.ShapeDtypeStruct(x.shape, x.dtype),
        input_output_aliases={0: 0},
    )(x, *after)


def total_kernel(n, *refs):
    value = None
    for ref in refs[:n]:
        for part in [ref[...]] if len(ref.shape) == 2 else [ref[k] for k in range(ref.shape[0])]:
            value = part if value is None else value + part
    refs[-2][...] = value
    refs[-1][...] = jnp.zeros_like(refs[-1])


def total(arrays, after):
    vmem = pl.BlockSpec(memory_space=pltpu.VMEM)
    return pl.pallas_call(
        functools.partial(total_kernel, len(arrays)),
        in_specs=[vmem] * len(arrays) + [pl.BlockSpec(memory_space=pltpu.HBM)] * len(after),
        out_specs=[vmem, vmem],
        out_shape=[jax.ShapeDtypeStruct(arrays[0].shape[-2:], F32), jax.ShapeDtypeStruct(TOKEN, F32)],
        compiler_params=pltpu.CompilerParams(vmem_limit_bytes=16 << 20),
    )(*arrays, *after)


def pack_weights(groups, w_in_ref, w_out_ref, to_ref):
    rows_in, rows_out = w_in_ref.shape[1], w_out_ref.shape[1]
    at = 0
    for e in (e for group in groups for e in group):
        for q in range(to_ref.shape[0]):
            to_ref[q, at : at + rows_in] = w_in_ref[e]
            to_ref[q, at + rows_in : at + rows_in + rows_out] = w_out_ref[e]
        at += rows_in + rows_out
    return at


def pack_kernel(in_bias, gain, shift, out_bias, task_gate, shared_gate, w_in_ref, w_out_ref, to_ref):
    rows_in, rows_out = w_in_ref.shape[1], w_out_ref.shape[1]
    at = pack_weights(GROUPS[:1], w_in_ref, w_out_ref, to_ref)
    n = SPEC + SHARED
    for q in range(to_ref.shape[0]):
        to_ref[q, at:] = jnp.zeros((to_ref.shape[1] - at, to_ref.shape[2]), F32)
        for k, bias in enumerate((in_bias, gain, shift, out_bias)):
            to_ref[q, at + k * EXPERTS : at + (k + 1) * EXPERTS, 0:rows_out] = bias[...]
        base = at + 4 * EXPERTS
        for t in range(TASKS):
            to_ref[q, base + t * n : base + (t + 1) * n, 0:rows_in] = task_gate[t]
        base += TASKS * n
        to_ref[q, base : base + EXPERTS, 0:rows_in] = shared_gate[...]


def pack(pairs, w_in, in_bias, gain, shift, w_out, out_bias, task_gate, shared_gate):
    rows = len(GROUPS[0]) * (w_in.shape[1] + w_out.shape[1]) + 4 * EXPERTS + GATES
    return pl.pallas_call(
        pack_kernel,
        out_shape=jax.ShapeDtypeStruct((pairs, rows, w_in.shape[2]), F32),
        compiler_params=pltpu.CompilerParams(vmem_limit_bytes=VMEM_BYTES),
    )(in_bias, gain, shift, out_bias, task_gate.transpose(0, 2, 1), shared_gate.T, w_in, w_out)


def prep_kernel(x_ref, c_ref, valid_ref, w_in_ref, w_out_ref, xh_ref, xl_ref, ct_ref, to_ref, done_ref):
    depth = x_ref.shape[1]

    @pl.when(pl.program_id(0) == 0)
    def _():
        pack_weights(GROUPS[1:], w_in_ref, w_out_ref, to_ref)
        done_ref[...] = jnp.zeros_like(done_ref)

    high, low = halves(x_ref[...].T)
    xh_ref[0:depth] = high
    xh_ref[depth:] = jnp.ones((xh_ref.shape[0] - depth, xh_ref.shape[1]), BF16)
    xl_ref[...] = low
    valid = valid_ref[...]
    for o in range(c_ref.shape[0]):
        ct_ref[o] = c_ref[o].T * valid


def prep(features, cotangent, valid, w_in, w_out, pairs):
    rows, depth = features.shape
    packed = sum(len(g) for g in GROUPS[1:]) * (w_in.shape[1] + w_out.shape[1])
    outs, _, units = cotangent.shape
    return pl.pallas_call(
        prep_kernel,
        grid=(rows // TILE,),
        in_specs=[
            pl.BlockSpec((TILE, depth), lambda i: (i, 0)),
            pl.BlockSpec((outs, TILE, units), lambda i: (0, i, 0)),
            pl.BlockSpec((1, TILE), lambda i: (0, i)),
            pl.BlockSpec(w_in.shape, lambda i: (0, 0, 0)),
            pl.BlockSpec(w_out.shape, lambda i: (0, 0, 0)),
        ],
        out_specs=[
            pl.BlockSpec((depth + STEP, TILE), lambda i: (0, i)),
            pl.BlockSpec((depth, TILE), lambda i: (0, i)),
            pl.BlockSpec((outs, units, TILE), lambda i: (0, 0, i)),
            pl.BlockSpec((pairs, packed, units), lambda i: (0, 0, 0)),
            pl.BlockSpec(TOKEN, lambda i: (0, 0)),
        ],
        out_shape=[
            jax.ShapeDtypeStruct((depth + STEP, rows), BF16),
            jax.ShapeDtypeStruct((depth, rows), BF16),
            jax.ShapeDtypeStruct((outs, units, rows), F32),
            jax.ShapeDtypeStruct((pairs, packed, units), F32),
            jax.ShapeDtypeStruct(TOKEN, F32),
        ],
        compiler_params=pltpu.CompilerParams(vmem_limit_bytes=VMEM_BYTES),
        cost_estimate=pl.CostEstimate(flops=0, bytes_accessed=32000000, transcendentals=0),
    )(features, cotangent, valid, w_in, w_out)


def softmax_rows(v):
    e = jnp.exp(v - jnp.max(v, axis=0, keepdims=True))
    return e / jnp.sum(e, axis=0, keepdims=True)


def expert_kernel(group, first, last, n_after, partial, *refs):
    used = sorted({o for e in group for o, _ in uses(e)})
    names = ["core", "own", "other", "small", "xh", "xl"]
    names += [f"c{o}" for o in used]
    names += ["gates"] if first else ["prob"]
    if last:
        names += [f"dp{k}" for k in range(len(GROUPS) - 1)]
    names += [f"in{o}" for o in partial]
    names += [f"after{k}" for k in range(n_after)]
    names += [f"{name}{l}" for name in ("dah", "dal") for l in range(len(group))]
    names += ["out"] if last else [f"out{o}" for o in used]
    names += ["wih", "wil"]
    names += ["keep", "send"] if last else ["grads"]
    if first:
        names += ["prob"]
    names += ["dl"] if last else ["dp"]
    names += ["done"]
    each = ["win_t", "win_t_low", "wp", "wp_low", "wp_t", "wp_t_low", "b_in", "b_out", "acc_w", "acc_g"]
    each += ["h", "u", "a", "xhat", "h2", "g", "ex", "xhh", "xhl", "dzh", "dzl"]
    names += [f"{name}{l}" for name in each for l in range(len(group))]
    if last:
        names += ["all_dp", "acc_gate"] + [f"mix{o}" for o in used]
    r = dict(zip(names, refs, strict=True))
    for name in (*each, "dah", "dal"):
        r[name] = [r[f"{name}{l}"] for l in range(len(group))]
    step = pl.program_id(0)
    count = len(group)
    units = r["acc_w"][0].shape[1]
    depth = r["xl"].shape[0]
    pairs = r["own"].shape[0]
    devices = 2 * pairs
    rows_in, rows_out = depth // devices, units // devices
    rows_all = rows_in + rows_out
    core = r["core"][0]
    tile = r["xl"].shape[1]
    chunks = [slice(k, k + STEP) for k in range(0, units, STEP)]

    @pl.when(step == 0)
    def _():
        for l, e in enumerate(group):
            base = l * rows_all
            for q in range(pairs):
                for src, at in ((r["own"], core), (r["other"], 1 - core)):
                    place = q * 2 + at
                    r["acc_w"][l][pl.ds(place * rows_in, rows_in)] = src[q, base : base + rows_in]
                    r["acc_g"][l][pl.ds(place * rows_out, rows_out)] = src[
                        q, base + rows_in : base + rows_all
                    ]
            w_in = r["acc_w"][l][0:depth]
            high, low = halves(w_in)
            r["wih"][l] = high
            r["wil"][l] = low
            high, low = halves((0.5 * w_in).T)
            r["win_t"][l][0:units] = high
            r["win_t_low"][l][0:units] = low
            w_out = r["acc_g"][l][0:units]
            b_in, gain, shift, b_out = (r["small"][k * EXPERTS + e : k * EXPERTS + e + 1] for k in range(4))
            scaled = w_out * wide(column(gain), units)
            high, low = halves(scaled)
            r["wp"][l][...] = high
            r["wp_low"][l][...] = low
            high, low = halves((0.5 * scaled).T)
            r["wp_t"][l][...] = high
            r["wp_t_low"][l][...] = low
            b_out = b_out + jnp.sum(w_out * wide(column(shift), units), axis=0, keepdims=True)
            r["b_in"][l][...] = column(0.5 * b_in)
            r["b_out"][l][...] = column(0.5 * b_out)
            r["xhh"][l][units:] = jnp.ones((STEP, tile), BF16)
        if first:
            high, low = halves(r["gates"][...])
            r["win_t"][0][units:] = high
            r["win_t_low"][0][units:] = low
        for l in range(count):
            r["acc_w"][l][...] = jnp.zeros_like(r["acc_w"][l])
            r["acc_g"][l][...] = jnp.zeros_like(r["acc_g"][l])
        r["done"][...] = jnp.zeros_like(r["done"])
        if last:
            r["acc_gate"][...] = jnp.zeros_like(r["acc_gate"])

    stats = {}

    spans = [slice(k, k + SPAN) for k in range(0, tile, SPAN)]
    zero = jnp.zeros((STEP, SPAN), F32)

    def project_in(l, s):
        top = units + (GATES if first and l == 0 else 0)
        r["h"][l][0:top, s] = dot3(
            r["win_t"][l][0:top], r["win_t_low"][l][0:top], r["xh"][0:depth, s], r["xl"][:, s], NN
        )

    def gate_weights(s):
        z = r["h"][0][units:, s]
        for lower, upper in ((0, 4), (4, 8), (8, 14)):
            r["prob"][lower:upper, s] = softmax_rows(z[lower:upper])
        r["prob"][14:16, s] = jnp.zeros((2, SPAN), F32)

    def normalise(l, s):
        total = zero
        for c in chunks:
            h = r["h"][l][c, s] + wide(r["b_in"][l][c], SPAN)
            u = 1.0 + jnp.tanh(h)
            a = h * u
            r["u"][l][c, s] = u
            r["a"][l][c, s] = a
            total = total + a
        mean = jnp.sum(total, axis=0, keepdims=True) * (1.0 / units)
        total = zero
        for c in chunks:
            d = r["a"][l][c, s] - mean
            total = total + d * d
        scale = lax.rsqrt(jnp.sum(total, axis=0, keepdims=True) * (1.0 / units) + EPSILON)
        stats[l, s.start] = scale
        for c in chunks:
            x = (r["a"][l][c, s] - mean) * scale
            r["xhat"][l][c, s] = x
            r["xhh"][l][c, s], r["xhl"][l][c, s] = halves(x)

    def project_out(l, s):
        r["h2"][l][:, s] = dot3(
            r["wp_t"][l][...], r["wp_t_low"][l][...], r["xhh"][l][0:units, s], r["xhl"][l][:, s], NN
        )

    def combine(l, s):
        taken = uses(group[l])
        prob = [0.5 * r["prob"][row : row + 1, s] for _, row in taken]
        sums = [zero for _ in taken]
        end = l == count - 1
        full = [[r["prob"][row : row + 1, s] for _, row in uses(e)] for e in group] if end else None
        for c in chunks:
            h = r["h2"][l][c, s] + wide(r["b_out"][l][c], SPAN)
            u = 1.0 + jnp.tanh(h)
            ex = h * u
            if not end:
                r["ex"][l][c, s] = ex
            slope = u + ex * (2.0 - u)
            d = None
            for k, (o, _) in enumerate(taken):
                cot = r[f"c{o}"][0, c, s]
                sums[k] = sums[k] + cot * ex
                term = prob[k] * cot
                d = term if d is None else d + term
                if end:
                    mix = full[l][k] * ex
                    for m in range(l):
                        mix = mix + full[m][k] * r["ex"][m][c, s]
                    if o in partial:
                        mix = mix + r[f"in{o}"][c, s]
                    if last:
                        r[f"mix{o}"][c, s] = mix
                    else:
                        r[f"out{o}"][c, s] = mix
            r["dzh"][l][c, s], r["dzl"][l][c, s] = halves(d * slope)
        for k, (_, row) in enumerate(taken):
            value = jnp.sum(sums[k], axis=0, keepdims=True)
            if last:
                r["all_dp"][row : row + 1, s] = value
            else:
                at = l * len(taken) + k
                r["dp"][at : at + 1, s] = value

    def back_out(l, s):
        r["g"][l][:, s] = dot3(
            r["wp"][l][...], r["wp_low"][l][...], r["dzh"][l][:, s], r["dzl"][l][:, s], NN
        )

    def grad_out(l):
        r["acc_g"][l][...] += dot(r["xhh"][l][...], r["dzh"][l][...], NT) + dot(
            r["xhh"][l][...], r["dzl"][l][...], NT
        )
        r["acc_g"][l][0:units] += dot(r["xhl"][l][...], r["dzh"][l][...], NT)

    def back_norm(l, s):
        total, along = zero, zero
        for c in chunks:
            g = r["g"][l][c, s]
            total = total + g
            along = along + g * r["xhat"][l][c, s]
        mean = jnp.sum(total, axis=0, keepdims=True) * (1.0 / units)
        along = jnp.sum(along, axis=0, keepdims=True) * (1.0 / units)
        scale = 0.5 * stats[l, s.start]
        for c in chunks:
            u, a = r["u"][l][c, s], r["a"][l][c, s]
            slope = (u + a * (2.0 - u)) * scale
            da = (r["g"][l][c, s] - mean - r["xhat"][l][c, s] * along) * slope
            r["dah"][l][c, s], r["dal"][l][c, s] = halves(da)

    def grad_in(l):
        high, low = r["dah"][l][...], r["dal"][l][...]
        r["acc_w"][l][...] += dot(r["xh"][...], high, NT) + dot(r["xh"][...], low, NT)
        r["acc_w"][l][0:depth] += dot(r["xl"][...], high, NT)

    chains = [(l, s) for l in range(count) for s in spans]
    for stage in ORDER:
        if isinstance(stage, tuple):
            name, k = stage
            if name == "go":
                grad_out(k)
            elif name == "gi":
                grad_in(k)
            else:
                at = {
                    "in": project_in, "norm": normalise, "out": project_out, "comb": combine, "back": back_out,
                    "bnorm": back_norm,
                }[name]
                at(*chains[k])
                if name == "in" and first and chains[k][0] == 0:
                    gate_weights(chains[k][1])

    if last:
        for o in used:
            r["out"][o] = r[f"mix{o}"][...].T
    if last:
        for k, g in enumerate(GROUPS[:-1]):
            at = 0
            for e in g:
                for _, row in uses(e):
                    r["all_dp"][row : row + 1] = r[f"dp{k}"][at : at + 1]
                    at += 1
        for lower, upper in ((0, 4), (4, 8), (8, 14)):
            p, d = r["prob"][lower:upper], r["all_dp"][lower:upper]
            r["dl"][lower:upper] = p * (d - jnp.sum(p * d, axis=0, keepdims=True))
        r["dl"][14:16] = jnp.zeros((2, tile), F32)
        high, low = halves(r["dl"][...])
        r["acc_gate"][:, 0:GATES] += (
            dot(r["xh"][0:depth], high, NT) + dot(r["xh"][0:depth], low, NT) + dot(r["xl"][...], high, NT)
        )

    @pl.when(step == pl.num_programs(0) - 1)
    def _():
        for l in range(count):
            base = l * (rows_all + 8)
            tail = jnp.concatenate([r["acc_g"][l][units : units + 1], r["acc_w"][l][depth : depth + 1]], 0)
            tail = jnp.concatenate([tail] * 4, 0)
            if last:
                places = [
                    (dst, q, q * 2 + at)
                    for q in range(pairs)
                    for dst, at in ((r["keep"], core), (r["send"], 1 - core))
                ]
            else:
                places = [(r["grads"], k, k) for k in range(devices)]
            for dst, q, place in places:
                dst[q, base : base + rows_in] = r["acc_w"][l][pl.ds(place * rows_in, rows_in)]
                dst[q, base + rows_in : base + rows_all] = r["acc_g"][l][pl.ds(place * rows_out, rows_out)]
                dst[q, base + rows_all : base + rows_all + 8] = tail
        if last:
            gate = r["acc_gate"][...].T[0:GATES]
            base = count * (rows_all + 8)
            for q in range(pairs):
                even = gate[:, 2 * q * rows_in : (2 * q + 1) * rows_in]
                odd = gate[:, (2 * q + 1) * rows_in : (2 * q + 2) * rows_in]
                for dst, at in ((r["keep"], core), (r["send"], 1 - core)):
                    dst[q, base:, 0:rows_in] = jnp.where(at == 0, even, odd)


def expert_call(group, core, own, other, small, xh, xl, ct, prob, gates, dps, last, after, skip, mixed):
    first = gates is not None
    pairs, _, units = own.shape
    depth, rows = xl.shape
    devices = 2 * pairs
    rows_in, rows_out = depth // devices, units // devices
    count = len(group)
    whole = lambda shape: pl.BlockSpec(shape, lambda i: (0,) * len(shape))
    along = lambda n: pl.BlockSpec((n, TILE), lambda i: (0, i))
    used = sorted({o for e in group for o, _ in uses(e)})
    ins = [core, own, other, small, xh, xl] + [ct] * len(used)
    held = own.shape[1] if first else count * (rows_in + rows_out)
    weights = pl.BlockSpec((pairs, held, units), lambda i: (0, skip, 0))
    in_specs = [
        pl.BlockSpec(memory_space=pltpu.SMEM),
        weights,
        weights,
        whole(small.shape),
        along(xh.shape[0]),
        along(depth),
    ]
    in_specs += [pl.BlockSpec((1, units, TILE), lambda i, o=o: (o, 0, i)) for o in used]
    if first:
        ins.append(gates)
        in_specs.append(whole(gates.shape))
    else:
        ins.append(prob)
        in_specs.append(along(GATES))
    if last:
        ins += dps
        in_specs += [along(8)] * len(dps)
    ins += [mixed[o] for o in sorted(mixed)]
    in_specs += [along(units)] * len(mixed)
    ins += after
    in_specs += [pl.BlockSpec(memory_space=pltpu.HBM)] * len(after)
    packed = count * (rows_in + rows_out + 8)
    shape = jax.ShapeDtypeStruct
    if last:
        mixes = [
            (pl.BlockSpec((len(used), TILE, units), lambda i: (0, i, 0)), shape((len(used), rows, units), F32))
        ]
    else:
        mixes = [(along(units), shape((units, rows), F32))] * len(used)
    outs = [
        *[(along(units), shape((units, rows), BF16))] * (2 * count),
        *mixes,
        (whole((count, depth, units)), shape((count, depth, units), BF16)),
        (whole((count, depth, units)), shape((count, depth, units), BF16)),
    ]
    if last:
        packed += GATES
        outs += [(whole((pairs, packed, units)), shape((pairs, packed, units), F32))] * 2
    else:
        outs.append((whole((devices, packed, units)), shape((devices, packed, units), F32)))
    if first:
        outs.append((along(GATES), shape((GATES, rows), F32)))
    if last:
        outs.append((along(GATES), shape((GATES, rows), F32)))
    else:
        outs.append((along(8), shape((8, rows), F32)))
    outs.append((whole(TOKEN), shape(TOKEN, F32)))
    top = units + (GATES if first else 0)
    kinds = [
        ((top, depth), BF16),
        ((top, depth), BF16),
        ((units, units), BF16),
        ((units, units), BF16),
        ((units, units), BF16),
        ((units, units), BF16),
        ((units, LANES), F32),
        ((units, LANES), F32),
        ((depth + STEP, units), F32),
        ((units + STEP, units), F32),
        ((top, TILE), F32),
        ((units, TILE), F32),
        ((units, TILE), F32),
        ((units, TILE), F32),
        ((units, TILE), F32),
        ((units, TILE), F32),
        ((units, TILE), F32),
        ((units + STEP, TILE), BF16),
        ((units, TILE), BF16),
        ((units, TILE), BF16),
        ((units, TILE), BF16),
    ]
    scratch = [pltpu.VMEM(*kind) for kind in kinds for _ in group]
    if last:
        scratch += [pltpu.VMEM((GATES, TILE), F32), pltpu.VMEM((depth, LANES), F32)]
        scratch += [pltpu.VMEM((units, TILE), F32)] * len(used)
    return pl.pallas_call(
        functools.partial(expert_kernel, group, first, last, len(after), tuple(sorted(mixed))),
        grid=(rows // TILE,),
        in_specs=in_specs,
        out_specs=[o[0] for o in outs],
        out_shape=[o[1] for o in outs],
        scratch_shapes=scratch,
        compiler_params=pltpu.CompilerParams(vmem_limit_bytes=VMEM_BYTES),
        cost_estimate=pl.CostEstimate(
            flops=20000000000 * count // 2, bytes_accessed=30000000, transcendentals=0
        ),
    )(*ins)


def final_kernel(steps, *refs):
    n = EXPERTS
    dahs, dals = refs[:n], refs[n : 2 * n]
    wihs, wils = refs[2 * n : 2 * n + len(GROUPS)], refs[2 * n + len(GROUPS) : 2 * n + 2 * len(GROUPS)]
    dl_ref, gates_ref = refs[2 * n + 2 * len(GROUPS) : 2 * n + 2 * len(GROUPS) + 2]
    gf_ref, done_ref, gate_ref = refs[-3:]
    done_ref[...] = jnp.zeros_like(done_ref)

    @pl.when(pl.program_id(0) == 0)
    def _():
        high, low = halves(gates_ref[...])
        gate_ref[0:GATES] = high
        gate_ref[GATES : 2 * GATES] = low
        gate_ref[2 * GATES :] = high

    high, low = halves(dl_ref[...])
    total = dot(gate_ref[...], jnp.concatenate([high, high, low], 0), TN)
    at = 0
    for k, group in enumerate(GROUPS):
        for l in range(len(group)):
            total = total + dot3(wihs[k][l], wils[k][l], dahs[at][...], dals[at][...], NN)
            at += 1
    gf_ref[...] = total.T


def final_call(dahs, dals, wihs, wils, dl, gates, part, parts, before, after):
    rows = dl.shape[1]
    _, depth, units = wihs[0].shape
    steps = rows // TILE // parts
    skip = part * steps
    whole = lambda a: pl.BlockSpec(a.shape, lambda i: (0,) * a.ndim)
    along = lambda a: pl.BlockSpec((a.shape[0], TILE), lambda i: (0, i + skip))
    ins = [*dahs, *dals, *wihs, *wils, dl, gates, *before, *after]
    n = 2 * EXPERTS + 2 * len(GROUPS) + 2
    return pl.pallas_call(
        functools.partial(final_kernel, steps),
        grid=(steps,),
        in_specs=[along(a) for a in (*dahs, *dals)]
        + [whole(a) for a in (*wihs, *wils)]
        + [along(dl), whole(gates)]
        + [pl.BlockSpec(memory_space=pltpu.HBM)] * (len(before) + len(after)),
        out_specs=[pl.BlockSpec((TILE, depth), lambda i: (i + skip, 0)), pl.BlockSpec(TOKEN, lambda i: (0, 0))],
        out_shape=[jax.ShapeDtypeStruct((rows, depth), F32), jax.ShapeDtypeStruct(TOKEN, F32)],
        scratch_shapes=[pltpu.VMEM((3 * GATES, depth), BF16)],
        input_output_aliases={n + k: k for k in range(len(before))},
        compiler_params=pltpu.CompilerParams(vmem_limit_bytes=VMEM_BYTES),
        cost_estimate=pl.CostEstimate(
            flops=15000000000 // parts, bytes_accessed=25000000 // parts, transcendentals=0
        ),
    )(*ins)


def finish_kernel(me_ref, *refs):
    n = len(GROUPS) + 1
    w_out_ref, gain_ref, shift_ref = refs[n : n + 3]
    g_in, g_in_bias, g_gain, g_shift, g_out, g_out_bias, g_task, g_shared = refs[n + 3 :]
    rows_in, rows_out, units = g_in.shape[1], g_out.shape[1], g_in.shape[2]
    me = me_ref[0]

    def own(row):
        value = row[:, 0:rows_out]
        for p in range(1, units // rows_out):
            value = jnp.where(me == p, row[:, p * rows_out : (p + 1) * rows_out], value)
        return value

    def as_row(col):
        return jnp.broadcast_to(col, (rows_out, LANES)).T[0:1]

    for k, group in enumerate(GROUPS):
        if k < len(GROUPS) - 1:
            add = lambda lower, upper, a=refs[k]: a[lower:upper]
        else:
            add = lambda lower, upper, a=refs[k], b=refs[k + 1]: a[lower:upper] + b[lower:upper]
        at = 0
        for e in group:
            g_in[e] = add(at, at + rows_in)
            at += rows_in
            raw = add(at, at + rows_out)
            at += rows_out
            tail = add(at, at + 8)
            at += 8
            total = tail[0:1]
            gain = wide(column(gain_ref[e : e + 1]), units)
            shift = wide(column(shift_ref[e : e + 1]), units)
            g_out[e] = gain * raw + shift * total
            w = w_out_ref[e]
            g_gain[e : e + 1] = as_row(jnp.sum(w * raw, axis=1, keepdims=True))
            g_shift[e : e + 1] = as_row(jnp.sum(w * total, axis=1, keepdims=True))
            g_in_bias[e : e + 1] = own(tail[1:2])
            g_out_bias[e : e + 1] = own(total)
    gate = add(at, at + GATES)[:, 0:rows_in]
    m = SPEC + SHARED
    for t in range(TASKS):
        g_task[t] = gate[t * m : (t + 1) * m]
    g_shared[...] = gate[TASKS * m : TASKS * m + EXPERTS]


def finish(me, totals, w_in, w_out, gain, shift):
    experts, rows_in, units = w_in.shape
    rows_out = w_out.shape[1]
    shape = lambda *s: jax.ShapeDtypeStruct(s, F32)
    vector = shape(experts, rows_out)
    outs = [
        shape(*w_in.shape),
        vector,
        vector,
        vector,
        shape(*w_out.shape),
        vector,
        shape(TASKS, SPEC + SHARED, rows_in),
        shape(EXPERTS, rows_in),
    ]
    vmem = pl.BlockSpec(memory_space=pltpu.VMEM)
    got = pl.pallas_call(
        finish_kernel,
        in_specs=[pl.BlockSpec(memory_space=pltpu.SMEM)] + [vmem] * (len(totals) + 3),
        out_specs=[vmem] * len(outs),
        out_shape=outs,
        compiler_params=pltpu.CompilerParams(vmem_limit_bytes=VMEM_BYTES),
    )(me, *totals, w_out, gain, shift)
    return (*got[:6], got[6].transpose(0, 2, 1), got[7].T)


def make(mesh):
    n_fsdp, n_dp = mesh.shape["fsdp"], mesh.shape["dp"]
    pairs = n_fsdp // 2
    across = [[q * 2 + c for q in range(pairs)] for c in range(2)]
    twin = [(i, i ^ 1) for i in range(n_fsdp)]

    def spread_out(x):
        return lax.all_to_all(x, "fsdp", 0, 0, axis_index_groups=across)

    def swap(x, bit):
        return lax.ppermute(x, "dp", [(i, i ^ bit) for i in range(n_dp)])

    def reduce_some(x, token, some, beside):
        for bit in some:
            x, token = total([x, swap(x, bit)], beside)
        return x, token

    bits = [1 << k for k in range(n_dp.bit_length() - 1)]

    def on_device(
        features, cotangent, counts, keep, w_in, in_bias, norm_gain, norm_bias, w_out, out_bias, task_gate, shared_gate
    ):
        rows = features.shape[0]
        depth = features.shape[1]
        experts, rows_in, units = w_in.shape
        rows_out = w_out.shape[1]
        valid = (lax.broadcasted_iota(jnp.int32, (1, rows), 1) < counts[0]) & (keep.reshape(1, rows) > 0)
        me = lax.axis_index("fsdp")
        core = (me % 2).astype(jnp.int32).reshape(1)
        xh, xl, ct, spread, done = prep(features, cotangent, valid.astype(F32), w_in, w_out, pairs)
        own0 = tie(
            spread_out(
                pack(pairs, w_in, in_bias, norm_gain, norm_bias, w_out, out_bias, task_gate, shared_gate)
            ),
            [done],
        )
        other0 = lax.ppermute(own0, "fsdp", twin)
        begin = len(GROUPS[0]) * (rows_in + rows_out)
        mine, theirs = own0[:, begin:], other0[:, begin:]
        both = jnp.where(core[0] == 0, jnp.stack([mine, theirs], 1), jnp.stack([theirs, mine], 1))
        both = both.reshape(n_fsdp, *both.shape[2:])
        n_bias = 4 * EXPERTS
        small = both[:, :n_bias, :rows_out].transpose(1, 0, 2).reshape(n_bias, units)
        gates = both[:, n_bias:, :rows_in].transpose(1, 0, 2).reshape(GATES, depth)

        def parts_of(got, group):
            n = len(group)
            m = 1 if group == GROUPS[-1] else len({o for e in group for o, _ in uses(e)})
            return got[:n], got[n : 2 * n], got[2 * n : 2 * n + m], got[2 * n + m :]

        got = expert_call(GROUPS[0], core, own0, other0, small, xh, xl, ct, None, gates, [], False, [], 0, {})
        dah0, dal0, mix0, (wih0, wil0, grads0, prob, dp0, done0) = parts_of(got, GROUPS[0])
        own1 = tie(spread_out(spread), [done0])
        other1 = lax.ppermute(own1, "fsdp", twin)
        got = expert_call(
            GROUPS[1], core, own1, other1, small, xh, xl, ct, prob, None, [], False, [], 0, {2: mix0[1]}
        )
        dah1, dal1, mix1, (wih1, wil1, grads1, dp1, done1) = parts_of(got, GROUPS[1])
        sum0, token0 = total([lax.all_to_all(grads0, "fsdp", 0, 0)], [done1])
        got = expert_call(
            GROUPS[2],
            core,
            own1,
            other1,
            small,
            xh,
            xl,
            ct,
            prob,
            None,
            [dp0, dp1],
            True,
            [token0],
            1,
            {0: mix0[0], 1: mix1[0], 2: mix1[1]},
        )
        dah2, dal2, (outputs,), (wih2, wil2, keep2, send2, dl, done2) = parts_of(got, GROUPS[2])
        sum1, token1 = total([lax.all_to_all(grads1, "fsdp", 0, 0)], [done2])
        sum0, token0 = reduce_some(sum0, token0, bits[:-1], [done2])
        kept = keep2 + lax.ppermute(tie(send2, [token0, token1]), "fsdp", twin)
        tail = (
            (*dah0, *dah1, *dah2),
            (*dal0, *dal1, *dal2),
            (wih0, wih1, wih2),
            (wil0, wil1, wil2),
            dl,
            gates,
        )
        part, done3 = final_call(*tail, 0, 2, [], [])
        sum2, token2 = total([spread_out(kept)], [done3])
        sum0, token0 = total([sum0, swap(sum0, bits[-1])], [done3])
        sum1, token1 = reduce_some(sum1, token1, bits[:-1], [done3])
        grad_features, done4 = final_call(*tail, 1, 2, [part], [token0, token1, token2])
        sum1, token1 = total([sum1, swap(sum1, bits[-1])], [done4])
        sum2, token2 = reduce_some(sum2, token2, bits[:-1], [done4, token1])
        pair2 = (sum2, swap(sum2, bits[-1]))
        rest = finish(me.astype(jnp.int32).reshape(1), (sum0, sum1, *pair2), w_in, w_out, norm_gain, norm_bias)
        return (outputs, grad_features, *rest)

    return on_device


def solution(mesh):
    placed = (
        P(("dp", "fsdp"), None),
        P(None, ("dp", "fsdp"), None),
        P(("dp", "fsdp")),
        P(("dp", "fsdp")),
        P(None, "fsdp", None),
        P(None, "fsdp"),
        P(None, "fsdp"),
        P(None, "fsdp"),
        P(None, "fsdp", None),
        P(None, "fsdp"),
        P(None, "fsdp", None),
        P("fsdp", None),
    )
    return jax.shard_map(
        make(mesh),
        mesh=mesh,
        in_specs=placed,
        out_specs=(
            P(None, ("dp", "fsdp"), None),
            P(("dp", "fsdp"), None),
            P(None, "fsdp", None),
            P(None, "fsdp"),
            P(None, "fsdp"),
            P(None, "fsdp"),
            P(None, "fsdp", None),
            P(None, "fsdp"),
            P(None, "fsdp", None),
            P("fsdp", None),
        ),
        check_vma=False,
    )
```

time: 216 us -> 203 us (0.940)
  other arithmetic: 12 us -> 1.74 us
  local copies, waits for them, and re-layouts: 12.4 us -> 10.2 us
    reduce_sum x3 -> x0, other arithmetic: 5.79 us -> none  [the longest x1 2.26 us: on_device(): sum1 = jnp.sum(tie(lax.all_to_all(second[5], 'fsdp', 0, 0), [dl]), 0)]
    pallas_call x2 -> x10, Pallas kernels: 31.9 us -> 26.5 us  [the longest x2 25.6 us: final_call(): pl.pallas_call(functools.partial(final_kernel, steps), grid=(steps,), in_...]
    add x4 -> x1, other arithmetic: 5.57 us -> 1.11 us  [on_device(): kept = keep2 + lax.ppermute(tie(send2, [token0, token1]), 'fsdp', twin)]
    pallas_call x3, Pallas kernels: 94.6 us -> 98.5 us  [expert_call(): pl.pallas_call(functools.partial(expert_kernel, group, first, last, len(a...]
    unnamed x38, local copies, waits for them, and re-layouts: 9.87 us -> 7.66 us
  transfers between devices with their start and end apart: 14 -> 14, of which waited for: 1 -> 1; matrix products, arithmetic and copies ran while one was open for 5% -> 2% of each run, Pallas kernels for 65% -> 69%
where the time goes in v3:
time: 203 us; the launch traced here: 202 us
  Pallas kernels  145 us (71%)
  starting transfers between devices  32.4 us (16%)
  waiting for transfers between devices  10.8 us (5%)
  local copies, waits for them, and re-layouts  10.2 us (5%)
    pallas_call x3, Pallas kernels, expert_call(): pl.pallas_call(functools.partial(expert_kernel, group, first, last, len(a...  98.5 us
    pallas_call x2, Pallas kernels, final_call(): pl.pallas_call(functools.partial(final_kernel, steps), grid=(steps,), in_...  25.6 us
    pallas_call x1, Pallas kernels, prep(): pl.pallas_call(prep_kernel, grid=(rows // TILE,), in_specs=[pl.BlockSpec(...  14.2 us
    all_to_all x3, starting transfers between devices, spread_out(): return lax.all_to_all(x, 'fsdp', 0, 0, axis_index_groups=across)  13.5 us
    ppermute x6, waiting for transfers between devices, swap(): return lax.ppermute(x, 'dp', [(i, i ^ bit) for i in range(n_dp)])  10.8 us
    ppermute x6, starting transfers between devices, swap(): return lax.ppermute(x, 'dp', [(i, i ^ bit) for i in range(n_dp)])  9.64 us
    unnamed x38, local copies, waits for them, and re-layouts  7.66 us
    all_to_all x1, starting transfers between devices, on_device(): sum1, token1 = total([lax.all_to_all(grads1, 'fsdp', 0, 0)], [done2])  4.2 us
  transfers between devices with their start and end apart: 14, of which 1 were waited for; matrix products, arithmetic and copies ran while one was open for 2% of the time, Pallas kernels for 69%

profile of v3, /device:TPU:0, one launch (start us, length us, event | category | flops | bytes accessed | tf_op | source)
XLA Modules:
  0.0 202.0 jit_solution(5052991007210879461)
XLA Ops:
  0.7 2.2 %shard_map.196 = f32[4,232,256]{2,1,0:T(8,128)} custom-call(f32[6,32]{1,0:T(8,128)} %in_bias.1, f32[6,32]{1,0:T(8,128)} %refs_5_.1, f32[6,32]{1,0:T(8,128)} %refs_6_.1, f32[6,32]{1,0:T(8,128)} %out_bias.1, f32[2,4,64]{2,1,0:T(4,128)} %bitcast.21, f32[6,64]{1,0:T(8,128)} %bitcast.22, f32[6,64,256]{2,1,0:T(8,128)} %w_in_ref.3, f32[6,32,256]{2,1,0:T(8,128)} %refs_4_.1), custom_call_target="tpu_custom_call" | custom-call | tf_op jit(solution)/shard_map/pallas_call | solution.py:121
  2.8 5.2 %all-to-all-start.1 = ((f32[4,232,256]{2,1,0:T(8,128)}), f32[4,232,256]{2,1,0:T(8,128)}, u32[]{:S(2)}, u32[]{:S(2)}) async-start(f32[4,232,256]{2,1,0:T(8,128)} %shard_map.196), calls=%async_computation.1 | async-start | bytes 1900544 | tf_op jit(solution)/shard_map/all_to_all | solution.py:671
  9.2 14.2 %shard_map.195 = (bf16[528,3072]{1,0:T(8,128)(2,1)}, bf16[512,3072]{1,0:T(8,128)(2,1)}, f32[3,256,3072]{2,1,0:T(8,128)}, f32[4,384,256]{2,1,0:T(8,128)}, f32[8,128]{1,0:T(8,128)}) custom-call(f32[3072,512]{1,0:T(8,128)} %x_ref.1, f32[3,3072,256]{2,1,0:T(8,128)} %c_ref.1, f32[1,3072]{1,0:T(1,128)} %bitcast.20, f32[6,64,256]{2,1,0:T(8,128)} %w_in_ref.3, ...), custom_call_target="tpu_custom_call" | custom-call | bytes 32000000 | tf_op jit(solution)/shard_map/pallas_call | solution.py:149
  23.6 4.4 %all-to-all-start = ((f32[4,384,256]{2,1,0:T(8,128)}), f32[4,384,256]{2,1,0:T(8,128)}, u32[]{:S(2)}, u32[]{:S(2)}) async-start(f32[4,384,256]{2,1,0:T(8,128)} %get-tuple-element.76), calls=%async_computation | async-start | bytes 3145728 | tf_op jit(solution)/shard_map/all_to_all | solution.py:671
  28.0 0.9 slice_bitcast_fusion.1
  29.1 0.8 reshape.45.refs_3_
  30.6 31.2 %shard_map.198 = (bf16[256,3072]{1,0:T(8,128)(2,1)}, bf16[256,3072]{1,0:T(8,128)(2,1)}, bf16[256,3072]{1,0:T(8,128)(2,1)}, bf16[256,3072]{1,0:T(8,128)(2,1)}, f3...) custom-call(s32[1]{0:T(128)} %bitcast.refs_0_, ...), custom_call_target="tpu_custom_call" | custom-call | flops 20000000000 | bytes 30000000 | tf_op jit(solution)/shard_map/pallas_call | solution.py:527
  62.4 4.1 %all-to-all-start.2 = ((f32[8,208,256]{2,1,0:T(8,128)}), f32[8,208,256]{2,1,0:T(8,128)S(1)}, u32[]{:S(2)}, u32[]{:S(2)}) async-start(f32[8,208,256]{2,1,0:T(8,128)} %get-tuple-element.89), calls=%async_computation.2 | async-start | bytes 3407872 | tf_op jit(solution)/shard_map/all_to_all | solution.py:722
  66.6 1.1 copy-done.18
  67.7 31.2 %shard_map.200 = (bf16[256,3072]{1,0:T(8,128)(2,1)}, bf16[256,3072]{1,0:T(8,128)(2,1)}, bf16[256,3072]{1,0:T(8,128)(2,1)}, bf16[256,3072]{1,0:T(8,128)(2,1)}, f3...) custom-call(s32[1]{0:T(128)} %bitcast.refs_0_, ...), custom_call_target="tpu_custom_call" | custom-call | flops 20000000000 | bytes 30000000 | tf_op jit(solution)/shard_map/pallas_call | solution.py:527
  98.9 4.2 %all-to-all-start.3 = ((f32[8,208,256]{2,1,0:T(8,128)}), f32[8,208,256]{2,1,0:T(8,128)S(1)}, u32[]{:S(2)}, u32[]{:S(2)}) async-start(f32[8,208,256]{2,1,0:T(8,128)} %get-tuple-element.118), calls=%async_computation.3 | async-start | bytes 3407872 | tf_op jit(solution)/shard_map/all_to_all | solution.py:741
  103.8 2.0 %collective-permute-start.2 = (f32[208,256]{1,0:T(8,128)S(1)}, f32[208,256]{1,0:T(8,128)S(1)}, u32[]{:S(2)}, u32[]{:S(2)}) collective-permute-start(f32[208,256]{1,0:T(8,128)S(1)} %get-tuple-element.113.refs_0_), channel_id=1, source_target_pairs={{0,8},{8,0},{16,24},{24,16},{1,9},{9,1},{17,25},{25,17},{2,10},{10... | collective-permute-start | bytes 638984 | tf_op jit(solution)/shard_map/ppermute | solution.py:674
  105.8 36.1 %shard_map.202 = (bf16[256,3072]{1,0:T(8,128)(2,1)}, bf16[256,3072]{1,0:T(8,128)(2,1)}, bf16[256,3072]{1,0:T(8,128)(2,1)}, bf16[256,3072]{1,0:T(8,128)(2,1)}, f3...) custom-call(s32[1]{0:T(128)} %bitcast.refs_0_, ...), custom_call_target="tpu_custom_call" | custom-call | flops 20000000000 | bytes 30000000 | tf_op jit(solution)/shard_map/pallas_call | solution.py:527
  144.9 2.6 %collective-permute-start.3 = (f32[208,256]{1,0:T(8,128)S(1)}, f32[208,256]{1,0:T(8,128)S(1)}, u32[]{:S(2)}, u32[]{:S(2)}) collective-permute-start(f32[208,256]{1,0:T(8,128)S(1)} %get-tuple-element.115.refs_0_), channel_id=1, source_target_pairs={{0,16},{8,24},{16,0},{24,8},{1,17},{9,25},{17,1},{25,9},{2,18},{10... | collective-permute-start | bytes 638984 | tf_op jit(solution)/shard_map/ppermute | solution.py:674
  147.9 1.1 add.8
  149.0 4.0 %all-to-all-start.4 = ((f32[4,224,256]{2,1,0:T(8,128)}), f32[4,224,256]{2,1,0:T(8,128)S(1)}, u32[]{:S(2)}, u32[]{:S(2)}) async-start(f32[4,224,256]{2,1,0:T(8,128)} %add.8), calls=%async_computation.4 | async-start | bytes 1835008 | tf_op jit(solution)/shard_map/all_to_all | solution.py:671
  153.0 12.8 %shard_map.203 = (f32[3072,512]{1,0:T(8,128)}, f32[8,128]{1,0:T(8,128)}) custom-call(bf16[256,3072]{1,0:T(8,128)(2,1)} %get-tuple-element.93.refs_0_, bf16[256,3072]{1,0:T(8,128)(2,1)} %get-tuple-element.94.refs_1_, bf16[256,3072]{1,0:T(8,128)(2,1)} %get-tuple-element.95.refs_2_, bf16[256,3072]{1,0:T(8,128)(2,1)} %get-tuple-element.96.refs_3_, ...), custom_call_target="tpu_custom_call" | custom-call | flops 7500000256 | bytes 12500000 | tf_op jit(solution)/shard_map/pallas_call | solution.py:575
  166.5 0.7 copy-done.1
  167.3 2.3 %collective-permute-start.6 = (f32[208,256]{1,0:T(8,128)S(1)}, f32[208,256]{1,0:T(8,128)S(1)}, u32[]{:S(2)}, u32[]{:S(2)}) collective-permute-start(f32[208,256]{1,0:T(8,128)S(1)} %get-tuple-element.128.refs_0_), channel_id=1, source_target_pairs={{0,16},{8,24},{16,0},{24,8},{1,17},{9,25},{17,1},{25,9},{2,18},{10... | collective-permute-start | bytes 638984 | tf_op jit(solution)/shard_map/ppermute | solution.py:674
  170.7 12.8 %shard_map.210 = (f32[3072,512]{1,0:T(8,128)}, f32[8,128]{1,0:T(8,128)}) custom-call(bf16[256,3072]{1,0:T(8,128)(2,1)} %get-tuple-element.93.refs_0_, bf16[256,3072]{1,0:T(8,128)(2,1)} %get-tuple-element.94.refs_1_, bf16[256,3072]{1,0:T(8,128)(2,1)} %get-tuple-element.95.refs_2_, ...), custom_call_target="tpu_custom_call", output_to_operand_aliasing={{0}: (20, {})} | custom-call | flops 7500000256 | bytes 12500000 | tf_op jit(solution)/shard_map/pallas_call | solution.py:575
  184.9 1.8 collective-permute-start.8
  186.7 10.8 %collective-permute-done.8.refs_3_ = f32[224,256]{1,0:T(8,128)S(1)} collective-permute-done((f32[224,256]{1,0:T(8,128)S(1)}, f32[224,256]{1,0:T(8,128)S(1)}, u32[]{:S(2)}, u32[]{:S(2)}) %collective-permute-start.8) | collective-permute-done | bytes 229408 | tf_op jit(solution)/shard_map/ppermute | solution.py:674
  197.5 0.7 copy-done.15
  198.2 3.7 %shard_map.213 = (f32[6,64,256]{2,1,0:T(8,128)}, f32[6,32]{1,0:T(8,128)}, f32[6,32]{1,0:T(8,128)}, f32[6,32]{1,0:T(8,128)}, f32[6,32,256]{2,1,0:T(8,128)}, /*ind...) custom-call(s32[1]{0:T(128)} %bitcast.10.me_ref, f32[208,256]{1,0:T(8,128)} %copy-done.1, f32[208,256]{1,0:T(8,128)} %copy-done.2, ...), custom_call_target="tpu_custom_call" | custom-call | tf_op jit(solution)/shard_map/pallas_call | solution.py:654
  (73 shorter events, 9.2 us)
Async XLA Ops:
  0.6 8.0 %copy-start.17 = (s32[3072]{0:T(1024)S(1)}, s32[3072]{0:T(1024)}, u32[]{:S(2)}) copy-start(s32[3072]{0:T(1024)} %param.15) | copy-start | bytes 36868
  2.8 20.7 %all-to-all-start.1 = ((f32[4,232,256]{2,1,0:T(8,128)}), f32[4,232,256]{2,1,0:T(8,128)}, u32[]{:S(2)}, u32[]{:S(2)}) async-start(f32[4,232,256]{2,1,0:T(8,128)} %shard_map.196), calls=%async_computation.1 | async-start | bytes 1900544 | tf_op jit(solution)/shard_map/all_to_all | solution.py:671
  23.5 5.4 %collective-permute-start = (f32[4,232,256]{2,1,0:T(8,128)}, f32[4,232,256]{2,1,0:T(8,128)S(1)}, u32[]{:S(2)}, u32[]{:S(2)}) collective-permute-start(f32[4,232,256]{2,1,0:T(8,128)} %shard_map.197.refs_1_), channel_id=1, source_target_pairs={{0,1},{1,0},{2,3},{3,2},{4,5},{5,4},{6,7},{7,6},{8,9},{9,8},{10,11... | collective-permute-start | bytes 2850824 | tf_op jit(solution)/shard_map/ppermute | solution.py:700
  23.6 38.3 %all-to-all-start = ((f32[4,384,256]{2,1,0:T(8,128)}), f32[4,384,256]{2,1,0:T(8,128)}, u32[]{:S(2)}, u32[]{:S(2)}) async-start(f32[4,384,256]{2,1,0:T(8,128)} %get-tuple-element.76), calls=%async_computation | async-start | bytes 3145728 | tf_op jit(solution)/shard_map/all_to_all | solution.py:671
  28.9 1.7 copy-start.16
  61.9 4.7 %collective-permute-start.1 = (f32[4,384,256]{2,1,0:T(8,128)}, f32[4,384,256]{2,1,0:T(8,128)S(1)}, u32[]{:S(2)}, u32[]{:S(2)}) collective-permute-start(f32[4,384,256]{2,1,0:T(8,128)} %shard_map.199.refs_1_), channel_id=1, source_target_pairs={{0,1},{1,0},{2,3},{3,2},{4,5},{5,4},{6,7},{7,6},{8,9},{9,8},{10,11... | collective-permute-start | bytes 4718600 | tf_op jit(solution)/shard_map/ppermute | solution.py:717
  62.4 36.5 %all-to-all-start.2 = ((f32[8,208,256]{2,1,0:T(8,128)}), f32[8,208,256]{2,1,0:T(8,128)S(1)}, u32[]{:S(2)}, u32[]{:S(2)}) async-start(f32[8,208,256]{2,1,0:T(8,128)} %get-tuple-element.89), calls=%async_computation.2 | async-start | bytes 3407872 | tf_op jit(solution)/shard_map/all_to_all | solution.py:722
  66.6 1.1 copy-start.18
  98.9 4.2 %copy-start.10 = (f32[8,128]{1,0:T(8,128)S(1)}, f32[8,128]{1,0:T(8,128)}, u32[]{:S(2)}) copy-start(f32[8,128]{1,0:T(8,128)} %get-tuple-element.90.refs_1_) | copy-start | bytes 12292
  98.9 44.4 %all-to-all-start.3 = ((f32[8,208,256]{2,1,0:T(8,128)}), f32[8,208,256]{2,1,0:T(8,128)S(1)}, u32[]{:S(2)}, u32[]{:S(2)}) async-start(f32[8,208,256]{2,1,0:T(8,128)} %get-tuple-element.118), calls=%async_computation.3 | async-start | bytes 3407872 | tf_op jit(solution)/shard_map/all_to_all | solution.py:741
  103.8 38.1 %collective-permute-start.2 = (f32[208,256]{1,0:T(8,128)S(1)}, f32[208,256]{1,0:T(8,128)S(1)}, u32[]{:S(2)}, u32[]{:S(2)}) collective-permute-start(f32[208,256]{1,0:T(8,128)S(1)} %get-tuple-element.113.refs_0_), channel_id=1, source_target_pairs={{0,8},{8,0},{16,24},{24,16},{1,9},{9,1},{17,25},{25,17},{2,10},{10... | collective-permute-start | bytes 638984 | tf_op jit(solution)/shard_map/ppermute | solution.py:674
  144.0 3.9 %copy-start.14 = (f32[4,224,256]{2,1,0:T(8,128)S(1)}, f32[4,224,256]{2,1,0:T(8,128)}, u32[]{:S(2)}) copy-start(f32[4,224,256]{2,1,0:T(8,128)} %get-tuple-element.121) | copy-start | bytes 2752516
  144.6 3.3 %collective-permute-start.5 = (f32[4,224,256]{2,1,0:T(8,128)}, f32[4,224,256]{2,1,0:T(8,128)S(1)}, u32[]{:S(2)}, u32[]{:S(2)}) collective-permute-start(f32[4,224,256]{2,1,0:T(8,128)} %shard_map.208), channel_id=1, source_target_pairs={{0,1},{1,0},{2,3},{3,2},{4,5},{5,4},{6,7},{7,6},{8,9},{9,8},{10,11... | collective-permute-start | bytes 2752520 | tf_op jit(solution)/shard_map/ppermute | solution.py:743
  144.9 20.9 %collective-permute-start.3 = (f32[208,256]{1,0:T(8,128)S(1)}, f32[208,256]{1,0:T(8,128)S(1)}, u32[]{:S(2)}, u32[]{:S(2)}) collective-permute-start(f32[208,256]{1,0:T(8,128)S(1)} %get-tuple-element.115.refs_0_), channel_id=1, source_target_pairs={{0,16},{8,24},{16,0},{24,8},{1,17},{9,25},{17,1},{25,9},{2,18},{10... | collective-permute-start | bytes 638984 | tf_op jit(solution)/shard_map/ppermute | solution.py:674
  147.5 19.8 %collective-permute-start.4 = (f32[208,256]{1,0:T(8,128)S(1)}, f32[208,256]{1,0:T(8,128)S(1)}, u32[]{:S(2)}, u32[]{:S(2)}) collective-permute-start(f32[208,256]{1,0:T(8,128)S(1)} %get-tuple-element.119.refs_0_), channel_id=1, source_target_pairs={{0,8},{8,0},{16,24},{24,16},{1,9},{9,1},{17,25},{25,17},{2,10},{10... | collective-permute-start | bytes 638984 | tf_op jit(solution)/shard_map/ppermute | solution.py:674
  149.0 20.6 %all-to-all-start.4 = ((f32[4,224,256]{2,1,0:T(8,128)}), f32[4,224,256]{2,1,0:T(8,128)S(1)}, u32[]{:S(2)}, u32[]{:S(2)}) async-start(f32[4,224,256]{2,1,0:T(8,128)} %add.8), calls=%async_computation.4 | async-start | bytes 1835008 | tf_op jit(solution)/shard_map/all_to_all | solution.py:671
  166.5 0.7 copy-start.1
  167.2 3.4 %copy-start.7 = (f32[8,128]{1,0:T(8,128)}, f32[8,128]{1,0:T(8,128)S(1)}, u32[]{:S(2)}) copy-start(f32[8,128]{1,0:T(8,128)S(1)} %get-tuple-element.117.refs_21_) | copy-start | bytes 12292
  167.3 3.4 %copy-start.8 = (f32[8,128]{1,0:T(8,128)}, f32[8,128]{1,0:T(8,128)S(1)}, u32[]{:S(2)}) copy-start(f32[8,128]{1,0:T(8,128)S(1)} %get-tuple-element.120.refs_22_) | copy-start | bytes 12292
  167.3 16.2 %collective-permute-start.6 = (f32[208,256]{1,0:T(8,128)S(1)}, f32[208,256]{1,0:T(8,128)S(1)}, u32[]{:S(2)}, u32[]{:S(2)}) collective-permute-start(f32[208,256]{1,0:T(8,128)S(1)} %get-tuple-element.128.refs_0_), channel_id=1, source_target_pairs={{0,16},{8,24},{16,0},{24,8},{1,17},{9,25},{17,1},{25,9},{2,18},{10... | collective-permute-start | bytes 638984 | tf_op jit(solution)/shard_map/ppermute | solution.py:674
  170.2 14.0 %collective-permute-start.7 = (f32[224,256]{1,0:T(8,128)S(1)}, f32[224,256]{1,0:T(8,128)S(1)}, u32[]{:S(2)}, u32[]{:S(2)}) collective-permute-start(f32[224,256]{1,0:T(8,128)S(1)} %get-tuple-element.131.refs_0_), channel_id=1, source_target_pairs={{0,8},{8,0},{16,24},{24,16},{1,9},{9,1},{17,25},{25,17},{2,10},{10... | collective-permute-start | bytes 688136 | tf_op jit(solution)/shard_map/ppermute | solution.py:674
  184.2 13.3 %copy-start.2 = (f32[208,256]{1,0:T(8,128)}, f32[208,256]{1,0:T(8,128)S(1)}, u32[]{:S(2)}) copy-start(f32[208,256]{1,0:T(8,128)S(1)} %get-tuple-element.130.refs_1_) | copy-start | bytes 638980
  184.9 12.6 %copy-start = (f32[224,256]{1,0:T(8,128)}, f32[224,256]{1,0:T(8,128)S(1)}, u32[]{:S(2)}) copy-start(f32[224,256]{1,0:T(8,128)S(1)} %get-tuple-element.133.refs_2_) | copy-start | bytes 688132
  184.9 12.6 %collective-permute-start.8 = (f32[224,256]{1,0:T(8,128)S(1)}, f32[224,256]{1,0:T(8,128)S(1)}, u32[]{:S(2)}, u32[]{:S(2)}) collective-permute-start(f32[224,256]{1,0:T(8,128)S(1)} %get-tuple-element.133.refs_2_), channel_id=1, source_target_pairs={{0,16},{8,24},{16,0},{24,8},{1,17},{9,25},{17,1},{25,9},{2,18},{10... | collective-permute-start | bytes 688136 | tf_op jit(solution)/shard_map/ppermute | solution.py:674
  (9 other events, 5.8 us)

commit v4 on v3

--- a/solution.py
+++ b/solution.py
@@ -15,6 +15,7 @@
 GROUPS = ((0, 1), (2, 3), (4, 5))
 TILE = 512
 STEP = 16
+PARTS = 3
 TOKEN = (8, 128)
 SPAN = 256
 ORDER = (('in', 0), ('in', 1), ('norm', 0), ('in', 2), ('norm', 1), ('in', 3), ('out', 0), ('norm', 2), ('out', 1), ('norm', 3), ('comb', 0), ('out', 2), ('comb', 1), ('out', 3), ('back', 0), ('comb', 2), ('back', 1), ('comb', 3), ('go', 0), ('bnorm', 0), ('back', 2), ('bnorm', 1), ('back', 3), ('gi', 0), ('bnorm', 2), ('go', 1), ('bnorm', 3), ('gi', 1))
@@ -403,9 +404,8 @@
             r["dl"][lower:upper] = p * (d - jnp.sum(p * d, axis=0, keepdims=True))
         r["dl"][14:16] = jnp.zeros((2, tile), F32)
         high, low = halves(r["dl"][...])
-        r["acc_gate"][:, 0:GATES] += (
-            dot(r["xh"][0:depth], high, NT) + dot(r["xh"][0:depth], low, NT) + dot(r["xl"][...], high, NT)
-        )
+        both = dot(r["xh"][0:depth], jnp.concatenate([high, low], 0), NT)
+        r["acc_gate"][:, 0:GATES] += both[:, 0:GATES] + both[:, GATES:] + dot(r["xl"][...], high, NT)
 
     @pl.when(step == pl.num_programs(0) - 1)
     def _():
@@ -531,7 +531,7 @@
         out_specs=[o[0] for o in outs],
         out_shape=[o[1] for o in outs],
         scratch_shapes=scratch,
-        compiler_params=pltpu.CompilerParams(vmem_limit_bytes=VMEM_BYTES),
+        compiler_params=pltpu.CompilerParams(vmem_limit_bytes=58 << 20),
         cost_estimate=pl.CostEstimate(
             flops=20000000000 * count // 2, bytes_accessed=30000000, transcendentals=0
         ),
@@ -553,21 +553,24 @@
         gate_ref[GATES : 2 * GATES] = low
         gate_ref[2 * GATES :] = high
 
-    high, low = halves(dl_ref[...])
-    total = dot(gate_ref[...], jnp.concatenate([high, high, low], 0), TN)
-    at = 0
-    for k, group in enumerate(GROUPS):
-        for l in range(len(group)):
-            total = total + dot3(wihs[k][l], wils[k][l], dahs[at][...], dals[at][...], NN)
-            at += 1
-    gf_ref[...] = total.T
-
-
-def final_call(dahs, dals, wihs, wils, dl, gates, part, parts, before, after):
+    for k in range(0, TILE, SPAN):
+        span = slice(k, k + SPAN)
+        high, low = halves(dl_ref[:, span])
+        value = dot(gate_ref[...], jnp.concatenate([high, high, low], 0), TN)
+        at = 0
+        for k, group in enumerate(GROUPS):
+            for l in range(len(group)):
+                value = value + dot3(wihs[k][l], wils[k][l], dahs[at][:, span], dals[at][:, span], NN)
+                at += 1
+        gf_ref[span] = value.T
+
+
+def final_call(dahs, dals, wihs, wils, dl, gates, part, before, after):
     rows = dl.shape[1]
     _, depth, units = wihs[0].shape
-    steps = rows // TILE // parts
-    skip = part * steps
+    tiles = rows // TILE
+    skip, end = (tiles * k // PARTS for k in (part, part + 1))
+    steps, parts = end - skip, PARTS
     whole = lambda a: pl.BlockSpec(a.shape, lambda i: (0,) * a.ndim)
     along = lambda a: pl.BlockSpec((a.shape[0], TILE), lambda i: (0, i + skip))
     ins = [*dahs, *dals, *wihs, *wils, dl, gates, *before, *after]
@@ -583,7 +586,7 @@
         out_shape=[jax.ShapeDtypeStruct((rows, depth), F32), jax.ShapeDtypeStruct(TOKEN, F32)],
         scratch_shapes=[pltpu.VMEM((3 * GATES, depth), BF16)],
         input_output_aliases={n + k: k for k in range(len(before))},
-        compiler_params=pltpu.CompilerParams(vmem_limit_bytes=VMEM_BYTES),
+        compiler_params=pltpu.CompilerParams(vmem_limit_bytes=58 << 20),
         cost_estimate=pl.CostEstimate(
             flops=15000000000 // parts, bytes_accessed=25000000 // parts, transcendentals=0
         ),
@@ -656,7 +659,7 @@
         in_specs=[pl.BlockSpec(memory_space=pltpu.SMEM)] + [vmem] * (len(totals) + 3),
         out_specs=[vmem] * len(outs),
         out_shape=outs,
-        compiler_params=pltpu.CompilerParams(vmem_limit_bytes=VMEM_BYTES),
+        compiler_params=pltpu.CompilerParams(vmem_limit_bytes=16 << 20),
     )(me, *totals, w_out, gain, shift)
     return (*got[:6], got[6].transpose(0, 2, 1), got[7].T)
 
@@ -749,13 +752,14 @@
             dl,
             gates,
         )
-        part, done3 = final_call(*tail, 0, 2, [], [])
+        part, done3 = final_call(*tail, 0, [], [])
         sum2, token2 = total([spread_out(kept)], [done3])
-        sum0, token0 = total([sum0, swap(sum0, bits[-1])], [done3])
         sum1, token1 = reduce_some(sum1, token1, bits[:-1], [done3])
-        grad_features, done4 = final_call(*tail, 1, 2, [part], [token0, token1, token2])
-        sum1, token1 = total([sum1, swap(sum1, bits[-1])], [done4])
-        sum2, token2 = reduce_some(sum2, token2, bits[:-1], [done4, token1])
+        part, done4 = final_call(*tail, 1, [part], [token1, token2])
+        sum0, token0 = total([sum0, swap(sum0, bits[-1])], [done4])
+        sum2, token2 = reduce_some(sum2, token2, bits[:-1], [done4])
+        grad_features, done5 = final_call(*tail, 2, [part], [token0, token2])
+        sum1, token1 = total([sum1, swap(sum1, bits[-1])], [done5])
         pair2 = (sum2, swap(sum2, bits[-1]))
         rest = finish(me.astype(jnp.int32).reshape(1), (sum0, sum1, *pair2), w_in, w_out, norm_gain, norm_bias)
         return (outputs, grad_features, *rest)

time: 203 us -> 196 us (0.966)
  waiting for transfers between devices: 10.8 us -> 5.9 us
    ppermute x6, waiting for transfers between devices: 10.8 us -> 3.41 us  [swap(): return lax.ppermute(x, 'dp', [(i, i ^ bit) for i in range(n_dp)])]
    pallas_call x2 -> x3, Pallas kernels: 25.6 us -> 29.3 us  [final_call(): pl.pallas_call(functools.partial(final_kernel, steps), grid=(steps,), in_...]
    ppermute x1, waiting for transfers between devices: 0.01 us -> 2.47 us  [on_device(): kept = keep2 + lax.ppermute(tie(send2, [token0, token1]), 'fsdp', twin)]
    ppermute x6, starting transfers between devices: 9.64 us -> 7.4 us  [swap(): return lax.ppermute(x, 'dp', [(i, i ^ bit) for i in range(n_dp)])]
    unnamed x38 -> x40, local copies, waits for them, and re-layouts: 7.66 us -> 6.72 us
  transfers between devices with their start and end apart: 14 -> 14, of which waited for: 1 -> 3; matrix products, arithmetic and copies ran while one was open for 2% -> 2% of each run, Pallas kernels for 69% -> 73%
where the time goes in v4:
time: 196 us
  Pallas kernels  147 us (75%)
  starting transfers between devices  30.4 us (16%)
  local copies, waits for them, and re-layouts  9.27 us (5%)
  waiting for transfers between devices  5.9 us (3%)
    pallas_call x3, Pallas kernels, expert_call(): pl.pallas_call(functools.partial(expert_kernel, group, first, last, len(a...  97.7 us
    pallas_call x3, Pallas kernels, final_call(): pl.pallas_call(functools.partial(final_kernel, steps), grid=(steps,), in_...  29.3 us
    pallas_call x1, Pallas kernels, prep(): pl.pallas_call(prep_kernel, grid=(rows // TILE,), in_specs=[pl.BlockSpec(...  14.2 us
    all_to_all x3, starting transfers between devices, spread_out(): return lax.all_to_all(x, 'fsdp', 0, 0, axis_index_groups=across)  13.8 us
    ppermute x6, starting transfers between devices, swap(): return lax.ppermute(x, 'dp', [(i, i ^ bit) for i in range(n_dp)])  7.4 us
    unnamed x40, local copies, waits for them, and re-layouts  6.72 us
    all_to_all x1, starting transfers between devices, on_device(): sum1, token1 = total([lax.all_to_all(grads1, 'fsdp', 0, 0)], [done2])  4.21 us
    all_to_all x1, starting transfers between devices, on_device(): sum0, token0 = total([lax.all_to_all(grads0, 'fsdp', 0, 0)], [done1])  4.16 us
  transfers between devices with their start and end apart: 14, of which 3 were waited for; matrix products, arithmetic and copies ran while one was open for 2% of the time, Pallas kernels for 73%

profile of v4, /device:TPU:0, one launch (start us, length us, event | category | flops | bytes accessed | tf_op | source)
XLA Modules:
  0.0 195.7 jit_solution(2211014567075754096)
XLA Ops:
  0.7 2.2 %shard_map.196 = f32[4,232,256]{2,1,0:T(8,128)} custom-call(f32[6,32]{1,0:T(8,128)} %in_bias.1, f32[6,32]{1,0:T(8,128)} %refs_5_.1, f32[6,32]{1,0:T(8,128)} %refs_6_.1, f32[6,32]{1,0:T(8,128)} %out_bias.1, f32[2,4,64]{2,1,0:T(4,128)} %bitcast.21, f32[6,64]{1,0:T(8,128)} %bitcast.22, f32[6,64,256]{2,1,0:T(8,128)} %w_in_ref.3, f32[6,32,256]{2,1,0:T(8,128)} %refs_4_.1), custom_call_target="tpu_custom_call" | custom-call | tf_op jit(solution)/shard_map/pallas_call | solution.py:122
  2.8 5.2 %all-to-all-start.1 = ((f32[4,232,256]{2,1,0:T(8,128)}), f32[4,232,256]{2,1,0:T(8,128)}, u32[]{:S(2)}, u32[]{:S(2)}) async-start(f32[4,232,256]{2,1,0:T(8,128)} %shard_map.196), calls=%async_computation.1 | async-start | bytes 1900544 | tf_op jit(solution)/shard_map/all_to_all | solution.py:674
  9.2 14.2 %shard_map.195 = (bf16[528,3072]{1,0:T(8,128)(2,1)}, bf16[512,3072]{1,0:T(8,128)(2,1)}, f32[3,256,3072]{2,1,0:T(8,128)}, f32[4,384,256]{2,1,0:T(8,128)}, f32[8,128]{1,0:T(8,128)}) custom-call(f32[3072,512]{1,0:T(8,128)} %x_ref.1, f32[3,3072,256]{2,1,0:T(8,128)} %c_ref.1, f32[1,3072]{1,0:T(1,128)} %bitcast.20, f32[6,64,256]{2,1,0:T(8,128)} %w_in_ref.3, ...), custom_call_target="tpu_custom_call" | custom-call | bytes 32000000 | tf_op jit(solution)/shard_map/pallas_call | solution.py:150
  23.5 4.4 %all-to-all-start = ((f32[4,384,256]{2,1,0:T(8,128)}), f32[4,384,256]{2,1,0:T(8,128)}, u32[]{:S(2)}, u32[]{:S(2)}) async-start(f32[4,384,256]{2,1,0:T(8,128)} %get-tuple-element.78), calls=%async_computation | async-start | bytes 3145728 | tf_op jit(solution)/shard_map/all_to_all | solution.py:674
  28.0 0.9 slice_bitcast_fusion.1
  29.1 0.8 reshape.45.refs_3_
  30.6 31.2 %shard_map.198 = (bf16[256,3072]{1,0:T(8,128)(2,1)}, bf16[256,3072]{1,0:T(8,128)(2,1)}, bf16[256,3072]{1,0:T(8,128)(2,1)}, bf16[256,3072]{1,0:T(8,128)(2,1)}, f3...) custom-call(s32[1]{0:T(128)} %bitcast.refs_0_, ...), custom_call_target="tpu_custom_call" | custom-call | flops 20000000000 | bytes 30000000 | tf_op jit(solution)/shard_map/pallas_call | solution.py:527
  62.4 4.2 %all-to-all-start.2 = ((f32[8,208,256]{2,1,0:T(8,128)}), f32[8,208,256]{2,1,0:T(8,128)S(1)}, u32[]{:S(2)}, u32[]{:S(2)}) async-start(f32[8,208,256]{2,1,0:T(8,128)} %get-tuple-element.91), calls=%async_computation.2 | async-start | bytes 3407872 | tf_op jit(solution)/shard_map/all_to_all | solution.py:725
  66.6 1.1 copy-done.19
  67.7 31.2 %shard_map.200 = (bf16[256,3072]{1,0:T(8,128)(2,1)}, bf16[256,3072]{1,0:T(8,128)(2,1)}, bf16[256,3072]{1,0:T(8,128)(2,1)}, bf16[256,3072]{1,0:T(8,128)(2,1)}, f3...) custom-call(s32[1]{0:T(128)} %bitcast.refs_0_, ...), custom_call_target="tpu_custom_call" | custom-call | flops 20000000000 | bytes 30000000 | tf_op jit(solution)/shard_map/pallas_call | solution.py:527
  99.0 4.2 %all-to-all-start.3 = ((f32[8,208,256]{2,1,0:T(8,128)}), f32[8,208,256]{2,1,0:T(8,128)S(1)}, u32[]{:S(2)}, u32[]{:S(2)}) async-start(f32[8,208,256]{2,1,0:T(8,128)} %get-tuple-element.115), calls=%async_computation.3 | async-start | bytes 3407872 | tf_op jit(solution)/shard_map/all_to_all | solution.py:744
  103.9 2.0 %collective-permute-start.3 = (f32[208,256]{1,0:T(8,128)S(1)}, f32[208,256]{1,0:T(8,128)S(1)}, u32[]{:S(2)}, u32[]{:S(2)}) collective-permute-start(f32[208,256]{1,0:T(8,128)S(1)} %get-tuple-element.122.refs_0_), channel_id=1, source_target_pairs={{0,8},{8,0},{16,24},{24,16},{1,9},{9,1},{17,25},{25,17},{2,10},{10... | collective-permute-start | bytes 638984 | tf_op jit(solution)/shard_map/ppermute | solution.py:677
  105.9 35.3 %shard_map.202 = (bf16[256,3072]{1,0:T(8,128)(2,1)}, bf16[256,3072]{1,0:T(8,128)(2,1)}, bf16[256,3072]{1,0:T(8,128)(2,1)}, bf16[256,3072]{1,0:T(8,128)(2,1)}, f3...) custom-call(s32[1]{0:T(128)} %bitcast.refs_0_, ...), custom_call_target="tpu_custom_call" | custom-call | flops 20000000000 | bytes 30000000 | tf_op jit(solution)/shard_map/pallas_call | solution.py:527
  144.1 2.5 %collective-permute-done.4 = f32[4,224,256]{2,1,0:T(8,128)S(1)} collective-permute-done((f32[4,224,256]{2,1,0:T(8,128)}, f32[4,224,256]{2,1,0:T(8,128)S(1)}, u32[]{:S(2)}, u32[]{:S(2)}) %collective-permute-start.4) | collective-permute-done | bytes 917536 | tf_op jit(solution)/shard_map/ppermute | solution.py:746
  146.6 1.1 add.8
  147.7 4.2 %all-to-all-start.4 = ((f32[4,224,256]{2,1,0:T(8,128)}), f32[4,224,256]{2,1,0:T(8,128)S(1)}, u32[]{:S(2)}, u32[]{:S(2)}) async-start(f32[4,224,256]{2,1,0:T(8,128)} %add.8), calls=%async_computation.4 | async-start | bytes 1835008 | tf_op jit(solution)/shard_map/all_to_all | solution.py:674
  151.9 9.8 %shard_map.203 = (f32[3072,512]{1,0:T(8,128)}, f32[8,128]{1,0:T(8,128)}) custom-call(bf16[256,3072]{1,0:T(8,128)(2,1)} %get-tuple-element.95.refs_0_, bf16[256,3072]{1,0:T(8,128)(2,1)} %get-tuple-element.96.refs_1_, bf16[256,3072]{1,0:T(8,128)(2,1)} %get-tuple-element.97.refs_2_, bf16[256,3072]{1,0:T(8,128)(2,1)} %get-tuple-element.98.refs_3_, ...), custom_call_target="tpu_custom_call" | custom-call | flops 5000000000 | bytes 8333333 | tf_op jit(solution)/shard_map/pallas_call | solution.py:578
  161.7 3.1 %collective-permute-start.5 = (f32[208,256]{1,0:T(8,128)S(1)}, f32[208,256]{1,0:T(8,128)S(1)}, u32[]{:S(2)}, u32[]{:S(2)}) collective-permute-start(f32[208,256]{1,0:T(8,128)S(1)} %get-tuple-element.127.refs_0_), channel_id=1, source_target_pairs={{0,16},{8,24},{16,0},{24,8},{1,17},{9,25},{17,1},{25,9},{2,18},{10... | collective-permute-start | bytes 638984 | tf_op jit(solution)/shard_map/ppermute | solution.py:677
  165.7 2.0 collective-permute-start.6
  167.6 9.8 %shard_map.209 = (f32[3072,512]{1,0:T(8,128)}, f32[8,128]{1,0:T(8,128)}) custom-call(bf16[256,3072]{1,0:T(8,128)(2,1)} %get-tuple-element.95.refs_0_, bf16[256,3072]{1,0:T(8,128)(2,1)} %get-tuple-element.96.refs_1_, bf16[256,3072]{1,0:T(8,128)(2,1)} %get-tuple-element.97.refs_2_, ...), custom_call_target="tpu_custom_call", output_to_operand_aliasing={{0}: (20, {})} | custom-call | flops 5000000000 | bytes 8333333 | tf_op jit(solution)/shard_map/pallas_call | solution.py:578
  177.4 2.6 %collective-permute-done.5.refs_1_ = f32[208,256]{1,0:T(8,128)S(1)} collective-permute-done((f32[208,256]{1,0:T(8,128)S(1)}, f32[208,256]{1,0:T(8,128)S(1)}, u32[]{:S(2)}, u32[]{:S(2)}) %collective-permute-start.5) | collective-permute-done | bytes 213024 | tf_op jit(solution)/shard_map/ppermute | solution.py:677
  181.4 9.8 %shard_map.212 = (f32[3072,512]{1,0:T(8,128)}, f32[8,128]{1,0:T(8,128)}) custom-call(bf16[256,3072]{1,0:T(8,128)(2,1)} %get-tuple-element.95.refs_0_, bf16[256,3072]{1,0:T(8,128)(2,1)} %get-tuple-element.96.refs_1_, bf16[256,3072]{1,0:T(8,128)(2,1)} %get-tuple-element.97.refs_2_, ...), custom_call_target="tpu_custom_call", output_to_operand_aliasing={{0}: (20, {})} | custom-call | flops 5000000000 | bytes 8333333 | tf_op jit(solution)/shard_map/pallas_call | solution.py:578
  192.5 0.8 collective-permute-done.8.refs_3_
  193.3 2.4 %shard_map.214 = (f32[6,64,256]{2,1,0:T(8,128)}, f32[6,32]{1,0:T(8,128)}, f32[6,32]{1,0:T(8,128)}, f32[6,32]{1,0:T(8,128)}, f32[6,32,256]{2,1,0:T(8,128)}, /*ind...) custom-call(s32[1]{0:T(128)} %bitcast.10.me_ref, f32[208,256]{1,0:T(8,128)S(1)} %get-tuple-element.133.refs_0_, ...), custom_call_target="tpu_custom_call" | custom-call | tf_op jit(solution)/shard_map/pallas_call | solution.py:657
  (76 shorter events, 9.1 us)
Async XLA Ops:
  0.6 8.0 %copy-start.18 = (s32[3072]{0:T(1024)S(1)}, s32[3072]{0:T(1024)}, u32[]{:S(2)}) copy-start(s32[3072]{0:T(1024)} %param.15) | copy-start | bytes 36868
  2.8 20.6 %all-to-all-start.1 = ((f32[4,232,256]{2,1,0:T(8,128)}), f32[4,232,256]{2,1,0:T(8,128)}, u32[]{:S(2)}, u32[]{:S(2)}) async-start(f32[4,232,256]{2,1,0:T(8,128)} %shard_map.196), calls=%async_computation.1 | async-start | bytes 1900544 | tf_op jit(solution)/shard_map/all_to_all | solution.py:674
  23.5 5.4 %collective-permute-start = (f32[4,232,256]{2,1,0:T(8,128)}, f32[4,232,256]{2,1,0:T(8,128)S(1)}, u32[]{:S(2)}, u32[]{:S(2)}) collective-permute-start(f32[4,232,256]{2,1,0:T(8,128)} %shard_map.197.refs_1_), channel_id=1, source_target_pairs={{0,1},{1,0},{2,3},{3,2},{4,5},{5,4},{6,7},{7,6},{8,9},{9,8},{10,11... | collective-permute-start | bytes 2850824 | tf_op jit(solution)/shard_map/ppermute | solution.py:703
  23.5 38.3 %all-to-all-start = ((f32[4,384,256]{2,1,0:T(8,128)}), f32[4,384,256]{2,1,0:T(8,128)}, u32[]{:S(2)}, u32[]{:S(2)}) async-start(f32[4,384,256]{2,1,0:T(8,128)} %get-tuple-element.78), calls=%async_computation | async-start | bytes 3145728 | tf_op jit(solution)/shard_map/all_to_all | solution.py:674
  28.9 1.7 copy-start.17
  61.9 4.7 %collective-permute-start.1 = (f32[4,384,256]{2,1,0:T(8,128)}, f32[4,384,256]{2,1,0:T(8,128)S(1)}, u32[]{:S(2)}, u32[]{:S(2)}) collective-permute-start(f32[4,384,256]{2,1,0:T(8,128)} %shard_map.199.refs_1_), channel_id=1, source_target_pairs={{0,1},{1,0},{2,3},{3,2},{4,5},{5,4},{6,7},{7,6},{8,9},{9,8},{10,11... | collective-permute-start | bytes 4718600 | tf_op jit(solution)/shard_map/ppermute | solution.py:720
  62.4 36.5 %all-to-all-start.2 = ((f32[8,208,256]{2,1,0:T(8,128)}), f32[8,208,256]{2,1,0:T(8,128)S(1)}, u32[]{:S(2)}, u32[]{:S(2)}) async-start(f32[8,208,256]{2,1,0:T(8,128)} %get-tuple-element.91), calls=%async_computation.2 | async-start | bytes 3407872 | tf_op jit(solution)/shard_map/all_to_all | solution.py:725
  66.6 1.1 copy-start.19
  99.0 4.2 %copy-start.11 = (f32[8,128]{1,0:T(8,128)S(1)}, f32[8,128]{1,0:T(8,128)}, u32[]{:S(2)}) copy-start(f32[8,128]{1,0:T(8,128)} %get-tuple-element.92.refs_1_) | copy-start | bytes 12292
  99.0 43.6 %all-to-all-start.3 = ((f32[8,208,256]{2,1,0:T(8,128)}), f32[8,208,256]{2,1,0:T(8,128)S(1)}, u32[]{:S(2)}, u32[]{:S(2)}) async-start(f32[8,208,256]{2,1,0:T(8,128)} %get-tuple-element.115), calls=%async_computation.3 | async-start | bytes 3407872 | tf_op jit(solution)/shard_map/all_to_all | solution.py:744
  103.9 37.3 %collective-permute-start.3 = (f32[208,256]{1,0:T(8,128)S(1)}, f32[208,256]{1,0:T(8,128)S(1)}, u32[]{:S(2)}, u32[]{:S(2)}) collective-permute-start(f32[208,256]{1,0:T(8,128)S(1)} %get-tuple-element.122.refs_0_), channel_id=1, source_target_pairs={{0,8},{8,0},{16,24},{24,16},{1,9},{9,1},{17,25},{25,17},{2,10},{10... | collective-permute-start | bytes 638984 | tf_op jit(solution)/shard_map/ppermute | solution.py:677
  143.2 3.4 %copy-start.16 = (f32[4,224,256]{2,1,0:T(8,128)S(1)}, f32[4,224,256]{2,1,0:T(8,128)}, u32[]{:S(2)}) copy-start(f32[4,224,256]{2,1,0:T(8,128)} %get-tuple-element.120) | copy-start | bytes 2752516
  143.9 2.7 %collective-permute-start.4 = (f32[4,224,256]{2,1,0:T(8,128)}, f32[4,224,256]{2,1,0:T(8,128)S(1)}, u32[]{:S(2)}, u32[]{:S(2)}) collective-permute-start(f32[4,224,256]{2,1,0:T(8,128)} %shard_map.207), channel_id=1, source_target_pairs={{0,1},{1,0},{2,3},{3,2},{4,5},{5,4},{6,7},{7,6},{8,9},{9,8},{10,11... | collective-permute-start | bytes 2752520 | tf_op jit(solution)/shard_map/ppermute | solution.py:746
  147.7 17.9 %all-to-all-start.4 = ((f32[4,224,256]{2,1,0:T(8,128)}), f32[4,224,256]{2,1,0:T(8,128)S(1)}, u32[]{:S(2)}, u32[]{:S(2)}) async-start(f32[4,224,256]{2,1,0:T(8,128)} %add.8), calls=%async_computation.4 | async-start | bytes 1835008 | tf_op jit(solution)/shard_map/all_to_all | solution.py:674
  151.9 12.9 %collective-permute-start.2 = (f32[208,256]{1,0:T(8,128)S(1)}, f32[208,256]{1,0:T(8,128)S(1)}, u32[]{:S(2)}, u32[]{:S(2)}) collective-permute-start(f32[208,256]{1,0:T(8,128)S(1)} %get-tuple-element.117.refs_0_), channel_id=1, source_target_pairs={{0,8},{8,0},{16,24},{24,16},{1,9},{9,1},{17,25},{25,17},{2,10},{10... | collective-permute-start | bytes 638984 | tf_op jit(solution)/shard_map/ppermute | solution.py:677
  161.7 18.3 %collective-permute-start.5 = (f32[208,256]{1,0:T(8,128)S(1)}, f32[208,256]{1,0:T(8,128)S(1)}, u32[]{:S(2)}, u32[]{:S(2)}) collective-permute-start(f32[208,256]{1,0:T(8,128)S(1)} %get-tuple-element.127.refs_0_), channel_id=1, source_target_pairs={{0,16},{8,24},{16,0},{24,8},{1,17},{9,25},{17,1},{25,9},{2,18},{10... | collective-permute-start | bytes 638984 | tf_op jit(solution)/shard_map/ppermute | solution.py:677
  165.5 2.1 %copy-start.10 = (f32[8,128]{1,0:T(8,128)}, f32[8,128]{1,0:T(8,128)S(1)}, u32[]{:S(2)}) copy-start(f32[8,128]{1,0:T(8,128)S(1)} %get-tuple-element.119.refs_21_) | copy-start | bytes 12292
  165.5 25.7 %collective-permute-start.7 = (f32[208,256]{1,0:T(8,128)S(1)}, f32[208,256]{1,0:T(8,128)S(1)}, u32[]{:S(2)}, u32[]{:S(2)}) collective-permute-start(f32[208,256]{1,0:T(8,128)S(1)} %get-tuple-element.134.refs_0_), channel_id=1, source_target_pairs={{0,16},{8,24},{16,0},{24,8},{1,17},{9,25},{17,1},{25,9},{2,18},{10... | collective-permute-start | bytes 638984 | tf_op jit(solution)/shard_map/ppermute | solution.py:677
  165.6 2.0 %copy-start.13 = (f32[8,128]{1,0:T(8,128)}, f32[8,128]{1,0:T(8,128)S(1)}, u32[]{:S(2)}) copy-start(f32[8,128]{1,0:T(8,128)S(1)} %get-tuple-element.125.refs_22_) | copy-start | bytes 12292
  165.7 15.1 %collective-permute-start.6 = (f32[224,256]{1,0:T(8,128)S(1)}, f32[224,256]{1,0:T(8,128)S(1)}, u32[]{:S(2)}, u32[]{:S(2)}) collective-permute-start(f32[224,256]{1,0:T(8,128)S(1)} %get-tuple-element.130.refs_0_), channel_id=1, source_target_pairs={{0,8},{8,0},{16,24},{24,16},{1,9},{9,1},{17,25},{25,17},{2,10},{10... | collective-permute-start | bytes 688136 | tf_op jit(solution)/shard_map/ppermute | solution.py:677
  180.8 12.5 %collective-permute-start.8 = (f32[224,256]{1,0:T(8,128)S(1)}, f32[224,256]{1,0:T(8,128)S(1)}, u32[]{:S(2)}, u32[]{:S(2)}) collective-permute-start(f32[224,256]{1,0:T(8,128)S(1)} %get-tuple-element.137.refs_2_), channel_id=1, source_target_pairs={{0,16},{8,24},{16,0},{24,8},{1,17},{9,25},{17,1},{25,9},{2,18},{10... | collective-permute-start | bytes 688136 | tf_op jit(solution)/shard_map/ppermute | solution.py:677
  181.4 11.9 %copy-start = (f32[6,32,256]{2,1,0:T(8,128)S(1)}, f32[6,32,256]{2,1,0:T(8,128)}, u32[]{:S(2)}) copy-start(f32[6,32,256]{2,1,0:T(8,128)} %refs_4_.1) | copy-start | bytes 589828
  181.4 11.9 %copy-start.1 = (f32[6,32]{1,0:T(8,128)S(1)}, f32[6,32]{1,0:T(8,128)}, u32[]{:S(2)}) copy-start(f32[6,32]{1,0:T(8,128)} %refs_5_.1) | copy-start | bytes 2308
  181.4 11.9 %copy-start.2 = (f32[6,32]{1,0:T(8,128)S(1)}, f32[6,32]{1,0:T(8,128)}, u32[]{:S(2)}) copy-start(f32[6,32]{1,0:T(8,128)} %refs_6_.1) | copy-start | bytes 2308
  (10 other events, 6.4 us)

commit v5 on v4

--- a/solution.py
+++ b/solution.py
@@ -51,6 +51,12 @@
 
 def dot3(a_high, a_low, b_high, b_low, dims):
     return dot(a_high, b_high, dims) + dot(a_low, b_high, dims) + dot(a_high, b_low, dims)
+
+
+def dot3_stacked(both, b_high, b_low):
+    n = both.shape[0] // 2
+    product = dot(both[...], b_high, NN)
+    return product[0:n] + product[n:] + dot(both[0:n], b_low, NN)
 
 
 def column(row):
@@ -183,9 +189,9 @@
 
 def expert_kernel(group, first, last, n_after, partial, *refs):
     used = sorted({o for e in group for o, _ in uses(e)})
-    names = ["core", "own", "other", "small", "xh", "xl"]
+    names = ["core", "own", "other"] + ([] if first else ["small"]) + ["xh", "xl"]
     names += [f"c{o}" for o in used]
-    names += ["gates"] if first else ["prob"]
+    names += [] if first else ["prob"]
     if last:
         names += [f"dp{k}" for k in range(len(GROUPS) - 1)]
     names += [f"in{o}" for o in partial]
@@ -195,10 +201,10 @@
     names += ["wih", "wil"]
     names += ["keep", "send"] if last else ["grads"]
     if first:
-        names += ["prob"]
+        names += ["prob", "small", "gates"]
     names += ["dl"] if last else ["dp"]
     names += ["done"]
-    each = ["win_t", "win_t_low", "wp", "wp_low", "wp_t", "wp_t_low", "b_in", "b_out", "acc_w", "acc_g"]
+    each = ["win_t", "wp", "wp_t", "b_in", "b_out", "acc_w", "acc_g"]
     each += ["h", "u", "a", "xhat", "h2", "g", "ex", "xhh", "xhl", "dzh", "dzl"]
     names += [f"{name}{l}" for name in each for l in range(len(group))]
     if last:
@@ -220,6 +226,18 @@
 
     @pl.when(step == 0)
     def _():
+        if first:
+            begin = count * rows_all
+            r["small"][...] = jnp.zeros_like(r["small"])
+            r["gates"][...] = jnp.zeros_like(r["gates"])
+            for q in range(pairs):
+                block, offset = divmod(2 * q * rows_in, units)
+                lanes = slice(block * units, (block + 1) * units)
+                for src, at in ((r["own"], core), (r["other"], 1 - core)):
+                    piece = src[q, begin : begin + 4 * EXPERTS]
+                    r["small"][...] += pltpu.roll(piece, (2 * q + at) * rows_out, 1)
+                    piece = src[q, begin + 4 * EXPERTS : begin + 4 * EXPERTS + GATES]
+                    r["gates"][:, lanes] += pltpu.roll(piece, offset + at * rows_in, 1)
         for l, e in enumerate(group):
             base = l * rows_all
             for q in range(pairs):
@@ -234,25 +252,30 @@
             r["wih"][l] = high
             r["wil"][l] = low
             high, low = halves((0.5 * w_in).T)
+            top = r["win_t"][l].shape[0] // 2
             r["win_t"][l][0:units] = high
-            r["win_t_low"][l][0:units] = low
+            r["win_t"][l][top : top + units] = low
             w_out = r["acc_g"][l][0:units]
             b_in, gain, shift, b_out = (r["small"][k * EXPERTS + e : k * EXPERTS + e + 1] for k in range(4))
             scaled = w_out * wide(column(gain), units)
             high, low = halves(scaled)
-            r["wp"][l][...] = high
-            r["wp_low"][l][...] = low
+            r["wp"][l][0:units] = high
+            r["wp"][l][units:] = low
             high, low = halves((0.5 * scaled).T)
-            r["wp_t"][l][...] = high
-            r["wp_t_low"][l][...] = low
+            r["wp_t"][l][0:units] = high
+            r["wp_t"][l][units:] = low
             b_out = b_out + jnp.sum(w_out * wide(column(shift), units), axis=0, keepdims=True)
             r["b_in"][l][...] = column(0.5 * b_in)
             r["b_out"][l][...] = column(0.5 * b_out)
             r["xhh"][l][units:] = jnp.ones((STEP, tile), BF16)
         if first:
             high, low = halves(r["gates"][...])
-            r["win_t"][0][units:] = high
-            r["win_t_low"][0][units:] = low
+            top = r["win_t"][0].shape[0] // 2
+            r["win_t"][0][units:top] = high
+            r["win_t"][0][top + units :] = low
+            for l in range(1, count):
+                r["win_t"][l][units:top] = high
+                r["win_t"][l][top + units :] = low
         for l in range(count):
             r["acc_w"][l][...] = jnp.zeros_like(r["acc_w"][l])
             r["acc_g"][l][...] = jnp.zeros_like(r["acc_g"][l])
@@ -266,10 +289,7 @@
     zero = jnp.zeros((STEP, SPAN), F32)
 
     def project_in(l, s):
-        top = units + (GATES if first and l == 0 else 0)
-        r["h"][l][0:top, s] = dot3(
-            r["win_t"][l][0:top], r["win_t_low"][l][0:top], r["xh"][0:depth, s], r["xl"][:, s], NN
-        )
+        r["h"][l][:, s] = dot3_stacked(r["win_t"][l], r["xh"][0:depth, s], r["xl"][:, s])
 
     def gate_weights(s):
         z = r["h"][0][units:, s]
@@ -299,9 +319,7 @@
             r["xhh"][l][c, s], r["xhl"][l][c, s] = halves(x)
 
     def project_out(l, s):
-        r["h2"][l][:, s] = dot3(
-            r["wp_t"][l][...], r["wp_t_low"][l][...], r["xhh"][l][0:units, s], r["xhl"][l][:, s], NN
-        )
+        r["h2"][l][:, s] = dot3_stacked(r["wp_t"][l], r["xhh"][l][0:units, s], r["xhl"][l][:, s])
 
     def combine(l, s):
         taken = uses(group[l])
@@ -342,9 +360,7 @@
                 r["dp"][at : at + 1, s] = value
 
     def back_out(l, s):
-        r["g"][l][:, s] = dot3(
-            r["wp"][l][...], r["wp_low"][l][...], r["dzh"][l][:, s], r["dzl"][l][:, s], NN
-        )
+        r["g"][l][:, s] = dot3_stacked(r["wp"][l], r["dzh"][l][:, s], r["dzl"][l][:, s])
 
     def grad_out(l):
         r["acc_g"][l][...] += dot(r["xhh"][l][...], r["dzh"][l][...], NT) + dot(
@@ -435,8 +451,8 @@
                     dst[q, base:, 0:rows_in] = jnp.where(at == 0, even, odd)
 
 
-def expert_call(group, core, own, other, small, xh, xl, ct, prob, gates, dps, last, after, skip, mixed):
-    first = gates is not None
+def expert_call(group, core, own, other, small, xh, xl, ct, prob, dps, last, after, skip, mixed):
+    first = small is None
     pairs, _, units = own.shape
     depth, rows = xl.shape
     devices = 2 * pairs
@@ -445,22 +461,19 @@
     whole = lambda shape: pl.BlockSpec(shape, lambda i: (0,) * len(shape))
     along = lambda n: pl.BlockSpec((n, TILE), lambda i: (0, i))
     used = sorted({o for e in group for o, _ in uses(e)})
-    ins = [core, own, other, small, xh, xl] + [ct] * len(used)
+    ins = [core, own, other] + ([] if first else [small]) + [xh, xl] + [ct] * len(used)
     held = own.shape[1] if first else count * (rows_in + rows_out)
     weights = pl.BlockSpec((pairs, held, units), lambda i: (0, skip, 0))
     in_specs = [
         pl.BlockSpec(memory_space=pltpu.SMEM),
         weights,
         weights,
-        whole(small.shape),
+        *([] if first else [whole((4 * EXPERTS, units))]),
         along(xh.shape[0]),
         along(depth),
     ]
     in_specs += [pl.BlockSpec((1, units, TILE), lambda i, o=o: (o, 0, i)) for o in used]
-    if first:
-        ins.append(gates)
-        in_specs.append(whole(gates.shape))
-    else:
+    if not first:
         ins.append(prob)
         in_specs.append(along(GATES))
     if last:
@@ -491,6 +504,9 @@
         outs.append((whole((devices, packed, units)), shape((devices, packed, units), F32)))
     if first:
         outs.append((along(GATES), shape((GATES, rows), F32)))
+        outs += [
+            (whole((n, lanes)), shape((n, lanes), F32)) for n, lanes in ((4 * EXPERTS, units), (GATES, depth))
+        ]
     if last:
         outs.append((along(GATES), shape((GATES, rows), F32)))
     else:
@@ -498,12 +514,9 @@
     outs.append((whole(TOKEN), shape(TOKEN, F32)))
     top = units + (GATES if first else 0)
     kinds = [
-        ((top, depth), BF16),
-        ((top, depth), BF16),
-        ((units, units), BF16),
-        ((units, units), BF16),
-        ((units, units), BF16),
-        ((units, units), BF16),
+        ((2 * top, depth), BF16),
+        ((2 * units, units), BF16),
+        ((2 * units, units), BF16),
         ((units, LANES), F32),
         ((units, LANES), F32),
         ((depth + STEP, units), F32),
@@ -701,25 +714,17 @@
             [done],
         )
         other0 = lax.ppermute(own0, "fsdp", twin)
-        begin = len(GROUPS[0]) * (rows_in + rows_out)
-        mine, theirs = own0[:, begin:], other0[:, begin:]
-        both = jnp.where(core[0] == 0, jnp.stack([mine, theirs], 1), jnp.stack([theirs, mine], 1))
-        both = both.reshape(n_fsdp, *both.shape[2:])
-        n_bias = 4 * EXPERTS
-        small = both[:, :n_bias, :rows_out].transpose(1, 0, 2).reshape(n_bias, units)
-        gates = both[:, n_bias:, :rows_in].transpose(1, 0, 2).reshape(GATES, depth)
-
         def parts_of(got, group):
             n = len(group)
             m = 1 if group == GROUPS[-1] else len({o for e in group for o, _ in uses(e)})
             return got[:n], got[n : 2 * n], got[2 * n : 2 * n + m], got[2 * n + m :]
 
-        got = expert_call(GROUPS[0], core, own0, other0, small, xh, xl, ct, None, gates, [], False, [], 0, {})
-        dah0, dal0, mix0, (wih0, wil0, grads0, prob, dp0, done0) = parts_of(got, GROUPS[0])
+        got = expert_call(GROUPS[0], core, own0, other0, None, xh, xl, ct, None, [], False, [], 0, {})
+        dah0, dal0, mix0, (wih0, wil0, grads0, prob, small, gates, dp0, done0) = parts_of(got, GROUPS[0])
         own1 = tie(spread_out(spread), [done0])
         other1 = lax.ppermute(own1, "fsdp", twin)
         got = expert_call(
-            GROUPS[1], core, own1, other1, small, xh, xl, ct, prob, None, [], False, [], 0, {2: mix0[1]}
+            GROUPS[1], core, own1, other1, small, xh, xl, ct, prob, [], False, [], 0, {2: mix0[1]}
         )
         dah1, dal1, mix1, (wih1, wil1, grads1, dp1, done1) = parts_of(got, GROUPS[1])
         sum0, token0 = total([lax.all_to_all(grads0, "fsdp", 0, 0)], [done1])
@@ -733,7 +738,6 @@
             xl,
             ct,
             prob,
-            None,
             [dp0, dp1],
             True,
             [token0],

time: 196 us -> 192 us (0.980)
  Pallas kernels: 147 us -> 144 us
    pallas_call x3, Pallas kernels: 97.7 us -> 95.3 us  [expert_call(): pl.pallas_call(functools.partial(expert_kernel, group, first, last, len(a...]
  transfers between devices with their start and end apart: 14 -> 14, of which waited for: 3 -> 3; matrix products, arithmetic and copies ran while one was open for 2% -> 0% of each run, Pallas kernels for 73% -> 73%
where the time goes in v5:
time: 192 us
  Pallas kernels  144 us (75%)
  starting transfers between devices  30.4 us (16%)
  local copies, waits for them, and re-layouts  7.7 us (4%)
  waiting for transfers between devices  5.89 us (3%)
    pallas_call x3, Pallas kernels, expert_call(): pl.pallas_call(functools.partial(expert_kernel, group, first, last, len(a...  95.3 us
    pallas_call x3, Pallas kernels, final_call(): pl.pallas_call(functools.partial(final_kernel, steps), grid=(steps,), in_...  29.3 us
    pallas_call x1, Pallas kernels, prep(): pl.pallas_call(prep_kernel, grid=(rows // TILE,), in_specs=[pl.BlockSpec(...  14.2 us
    all_to_all x3, starting transfers between devices, spread_out(): return lax.all_to_all(x, 'fsdp', 0, 0, axis_index_groups=across)  13.8 us
    unnamed x40, local copies, waits for them, and re-layouts  7.7 us
    ppermute x6, starting transfers between devices, swap(): return lax.ppermute(x, 'dp', [(i, i ^ bit) for i in range(n_dp)])  7.42 us
    all_to_all x1, starting transfers between devices, on_device(): sum1, token1 = total([lax.all_to_all(grads1, 'fsdp', 0, 0)], [done2])  4.19 us
    all_to_all x1, starting transfers between devices, on_device(): sum0, token0 = total([lax.all_to_all(grads0, 'fsdp', 0, 0)], [done1])  4.17 us
  transfers between devices with their start and end apart: 14, of which 3 were waited for; matrix products, arithmetic and copies ran while one was open for 0% of the time, Pallas kernels for 73%

profile of v5, /device:TPU:0, one launch (start us, length us, event | category | flops | bytes accessed | tf_op | source)
XLA Modules:
  0.0 191.6 jit_solution(13785635760065602172)
XLA Ops:
  0.7 2.2 %shard_map.196 = f32[4,232,256]{2,1,0:T(8,128)} custom-call(f32[6,32]{1,0:T(8,128)} %in_bias.1, f32[6,32]{1,0:T(8,128)} %refs_5_.1, f32[6,32]{1,0:T(8,128)} %refs_6_.1, f32[6,32]{1,0:T(8,128)} %out_bias.1, f32[2,4,64]{2,1,0:T(4,128)} %bitcast.10, f32[6,64]{1,0:T(8,128)} %bitcast.11, f32[6,64,256]{2,1,0:T(8,128)} %w_in_ref.3, f32[6,32,256]{2,1,0:T(8,128)} %refs_4_.1), custom_call_target="tpu_custom_call" | custom-call | tf_op jit(solution)/shard_map/pallas_call | solution.py:128
  2.8 5.2 %all-to-all-start.1 = ((f32[4,232,256]{2,1,0:T(8,128)}), f32[4,232,256]{2,1,0:T(8,128)}, u32[]{:S(2)}, u32[]{:S(2)}) async-start(f32[4,232,256]{2,1,0:T(8,128)} %shard_map.196), calls=%async_computation.1 | async-start | bytes 1900544 | tf_op jit(solution)/shard_map/all_to_all | solution.py:687
  9.2 14.2 %shard_map.195 = (bf16[528,3072]{1,0:T(8,128)(2,1)}, bf16[512,3072]{1,0:T(8,128)(2,1)}, f32[3,256,3072]{2,1,0:T(8,128)}, f32[4,384,256]{2,1,0:T(8,128)}, f32[8,128]{1,0:T(8,128)}) custom-call(f32[3072,512]{1,0:T(8,128)} %x_ref.1, f32[3,3072,256]{2,1,0:T(8,128)} %c_ref.1, f32[1,3072]{1,0:T(1,128)} %bitcast.9, f32[6,64,256]{2,1,0:T(8,128)} %w_in_ref.3, ...), custom_call_target="tpu_custom_call" | custom-call | bytes 32000000 | tf_op jit(solution)/shard_map/pallas_call | solution.py:156
  23.5 4.4 %all-to-all-start = ((f32[4,384,256]{2,1,0:T(8,128)}), f32[4,384,256]{2,1,0:T(8,128)}, u32[]{:S(2)}, u32[]{:S(2)}) async-start(f32[4,384,256]{2,1,0:T(8,128)} %get-tuple-element.80), calls=%async_computation | async-start | bytes 3145728 | tf_op jit(solution)/shard_map/all_to_all | solution.py:687
  28.0 1.0 copy-done.19
  29.0 30.2 %shard_map.198 = (bf16[256,3072]{1,0:T(8,128)(2,1)}, bf16[256,3072]{1,0:T(8,128)(2,1)}, bf16[256,3072]{1,0:T(8,128)(2,1)}, bf16[256,3072]{1,0:T(8,128)(2,1)}, f3...) custom-call(s32[1]{0:T(128)} %bitcast.refs_0_, ...), custom_call_target="tpu_custom_call" | custom-call | flops 20000000000 | bytes 30000000 | tf_op jit(solution)/shard_map/pallas_call | solution.py:540
  59.8 4.2 %all-to-all-start.2 = ((f32[8,208,256]{2,1,0:T(8,128)}), f32[8,208,256]{2,1,0:T(8,128)S(1)}, u32[]{:S(2)}, u32[]{:S(2)}) async-start(f32[8,208,256]{2,1,0:T(8,128)} %get-tuple-element.94), calls=%async_computation.2 | async-start | bytes 3407872 | tf_op jit(solution)/shard_map/all_to_all | solution.py:730
  63.9 1.1 copy-done.18
  65.1 30.1 %shard_map.200 = (bf16[256,3072]{1,0:T(8,128)(2,1)}, bf16[256,3072]{1,0:T(8,128)(2,1)}, bf16[256,3072]{1,0:T(8,128)(2,1)}, bf16[256,3072]{1,0:T(8,128)(2,1)}, f3...) custom-call(s32[1]{0:T(128)} %bitcast.refs_0_, ...), custom_call_target="tpu_custom_call" | custom-call | flops 20000000000 | bytes 30000000 | tf_op jit(solution)/shard_map/pallas_call | solution.py:540
  95.2 4.2 %all-to-all-start.3 = ((f32[8,208,256]{2,1,0:T(8,128)}), f32[8,208,256]{2,1,0:T(8,128)S(1)}, u32[]{:S(2)}, u32[]{:S(2)}) async-start(f32[8,208,256]{2,1,0:T(8,128)} %get-tuple-element.119), calls=%async_computation.3 | async-start | bytes 3407872 | tf_op jit(solution)/shard_map/all_to_all | solution.py:748
  100.1 2.0 %collective-permute-start.3 = (f32[208,256]{1,0:T(8,128)S(1)}, f32[208,256]{1,0:T(8,128)S(1)}, u32[]{:S(2)}, u32[]{:S(2)}) collective-permute-start(f32[208,256]{1,0:T(8,128)S(1)} %get-tuple-element.126.refs_0_), channel_id=1, source_target_pairs={{0,8},{8,0},{16,24},{24,16},{1,9},{9,1},{17,25},{25,17},{2,10},{10... | collective-permute-start | bytes 638984 | tf_op jit(solution)/shard_map/ppermute | solution.py:690
  102.1 35.0 %shard_map.202 = (bf16[256,3072]{1,0:T(8,128)(2,1)}, bf16[256,3072]{1,0:T(8,128)(2,1)}, bf16[256,3072]{1,0:T(8,128)(2,1)}, bf16[256,3072]{1,0:T(8,128)(2,1)}, f3...) custom-call(s32[1]{0:T(128)} %bitcast.refs_0_, ...), custom_call_target="tpu_custom_call" | custom-call | flops 20000000000 | bytes 30000000 | tf_op jit(solution)/shard_map/pallas_call | solution.py:540
  138.5 0.7 copy-done.4
  140.1 2.5 %collective-permute-done.4 = f32[4,224,256]{2,1,0:T(8,128)S(1)} collective-permute-done((f32[4,224,256]{2,1,0:T(8,128)}, f32[4,224,256]{2,1,0:T(8,128)S(1)}, u32[]{:S(2)}, u32[]{:S(2)}) %collective-permute-start.4) | collective-permute-done | bytes 917536 | tf_op jit(solution)/shard_map/ppermute | solution.py:750
  142.5 1.1 add.8
  143.7 4.2 %all-to-all-start.4 = ((f32[4,224,256]{2,1,0:T(8,128)}), f32[4,224,256]{2,1,0:T(8,128)S(1)}, u32[]{:S(2)}, u32[]{:S(2)}) async-start(f32[4,224,256]{2,1,0:T(8,128)} %add.8), calls=%async_computation.4 | async-start | bytes 1835008 | tf_op jit(solution)/shard_map/all_to_all | solution.py:687
  147.8 9.8 %shard_map.203 = (f32[3072,512]{1,0:T(8,128)}, f32[8,128]{1,0:T(8,128)}) custom-call(bf16[256,3072]{1,0:T(8,128)(2,1)} %get-tuple-element.98.refs_0_, bf16[256,3072]{1,0:T(8,128)(2,1)} %get-tuple-element.99.refs_1_, bf16[256,3072]{1,0:T(8,128)(2,1)} %get-tuple-element.100.refs_2_, bf16[256,3072]{1,0:T(8,128)(2,1)} %get-tuple-element.101.refs_3_, ...), custom_call_target="tpu_custom_call" | custom-call | flops 5000000000 | bytes 8333333 | tf_op jit(solution)/shard_map/pallas_call | solution.py:591
  157.6 3.1 %collective-permute-start.5 = (f32[208,256]{1,0:T(8,128)S(1)}, f32[208,256]{1,0:T(8,128)S(1)}, u32[]{:S(2)}, u32[]{:S(2)}) collective-permute-start(f32[208,256]{1,0:T(8,128)S(1)} %get-tuple-element.131.refs_0_), channel_id=1, source_target_pairs={{0,16},{8,24},{16,0},{24,8},{1,17},{9,25},{17,1},{25,9},{2,18},{10... | collective-permute-start | bytes 638984 | tf_op jit(solution)/shard_map/ppermute | solution.py:690
  161.6 2.0 %collective-permute-start.6 = (f32[224,256]{1,0:T(8,128)S(1)}, f32[224,256]{1,0:T(8,128)S(1)}, u32[]{:S(2)}, u32[]{:S(2)}) collective-permute-start(f32[224,256]{1,0:T(8,128)S(1)} %get-tuple-element.134.refs_0_), channel_id=1, source_target_pairs={{0,8},{8,0},{16,24},{24,16},{1,9},{9,1},{17,25},{25,17},{2,10},{10... | collective-permute-start | bytes 688136 | tf_op jit(solution)/shard_map/ppermute | solution.py:690
  163.6 9.8 %shard_map.209 = (f32[3072,512]{1,0:T(8,128)}, f32[8,128]{1,0:T(8,128)}) custom-call(bf16[256,3072]{1,0:T(8,128)(2,1)} %get-tuple-element.98.refs_0_, bf16[256,3072]{1,0:T(8,128)(2,1)} %get-tuple-element.99.refs_1_, bf16[256,3072]{1,0:T(8,128)(2,1)} %get-tuple-element.100.refs_2_, ...), custom_call_target="tpu_custom_call", output_to_operand_aliasing={{0}: (20, {})} | custom-call | flops 5000000000 | bytes 8333333 | tf_op jit(solution)/shard_map/pallas_call | solution.py:591
  173.3 2.6 %collective-permute-done.5.refs_1_ = f32[208,256]{1,0:T(8,128)S(1)} collective-permute-done((f32[208,256]{1,0:T(8,128)S(1)}, f32[208,256]{1,0:T(8,128)S(1)}, u32[]{:S(2)}, u32[]{:S(2)}) %collective-permute-start.5) | collective-permute-done | bytes 213024 | tf_op jit(solution)/shard_map/ppermute | solution.py:690
  177.3 9.8 %shard_map.212 = (f32[3072,512]{1,0:T(8,128)}, f32[8,128]{1,0:T(8,128)}) custom-call(bf16[256,3072]{1,0:T(8,128)(2,1)} %get-tuple-element.98.refs_0_, bf16[256,3072]{1,0:T(8,128)(2,1)} %get-tuple-element.99.refs_1_, bf16[256,3072]{1,0:T(8,128)(2,1)} %get-tuple-element.100.refs_2_, ...), custom_call_target="tpu_custom_call", output_to_operand_aliasing={{0}: (20, {})} | custom-call | flops 5000000000 | bytes 8333333 | tf_op jit(solution)/shard_map/pallas_call | solution.py:591
  188.4 0.8 collective-permute-done.8.refs_3_
  189.2 2.4 %shard_map.214 = (f32[6,64,256]{2,1,0:T(8,128)}, f32[6,32]{1,0:T(8,128)}, f32[6,32]{1,0:T(8,128)}, f32[6,32]{1,0:T(8,128)}, f32[6,32,256]{2,1,0:T(8,128)}, /*ind...) custom-call(s32[1]{0:T(128)} %bitcast.5.me_ref, f32[208,256]{1,0:T(8,128)S(1)} %get-tuple-element.137.refs_0_, ...), custom_call_target="tpu_custom_call" | custom-call | tf_op jit(solution)/shard_map/pallas_call | solution.py:670
  (66 shorter events, 7.6 us)
Async XLA Ops:
  0.6 8.0 %copy-start.17 = (s32[3072]{0:T(1024)S(1)}, s32[3072]{0:T(1024)}, u32[]{:S(2)}) copy-start(s32[3072]{0:T(1024)} %param.15) | copy-start | bytes 36868
  2.8 20.6 %all-to-all-start.1 = ((f32[4,232,256]{2,1,0:T(8,128)}), f32[4,232,256]{2,1,0:T(8,128)}, u32[]{:S(2)}, u32[]{:S(2)}) async-start(f32[4,232,256]{2,1,0:T(8,128)} %shard_map.196), calls=%async_computation.1 | async-start | bytes 1900544 | tf_op jit(solution)/shard_map/all_to_all | solution.py:687
  23.5 4.5 %collective-permute-start = (f32[4,232,256]{2,1,0:T(8,128)}, f32[4,232,256]{2,1,0:T(8,128)S(1)}, u32[]{:S(2)}, u32[]{:S(2)}) collective-permute-start(f32[4,232,256]{2,1,0:T(8,128)} %shard_map.197.refs_1_), channel_id=1, source_target_pairs={{0,1},{1,0},{2,3},{3,2},{4,5},{5,4},{6,7},{7,6},{8,9},{9,8},{10,11... | collective-permute-start | bytes 2850824 | tf_op jit(solution)/shard_map/ppermute | solution.py:716
  23.5 35.6 %all-to-all-start = ((f32[4,384,256]{2,1,0:T(8,128)}), f32[4,384,256]{2,1,0:T(8,128)}, u32[]{:S(2)}, u32[]{:S(2)}) async-start(f32[4,384,256]{2,1,0:T(8,128)} %get-tuple-element.80), calls=%async_computation | async-start | bytes 3145728 | tf_op jit(solution)/shard_map/all_to_all | solution.py:687
  28.0 1.0 copy-start.19
  59.2 4.7 %collective-permute-start.1 = (f32[4,384,256]{2,1,0:T(8,128)}, f32[4,384,256]{2,1,0:T(8,128)S(1)}, u32[]{:S(2)}, u32[]{:S(2)}) collective-permute-start(f32[4,384,256]{2,1,0:T(8,128)} %shard_map.199.refs_1_), channel_id=1, source_target_pairs={{0,1},{1,0},{2,3},{3,2},{4,5},{5,4},{6,7},{7,6},{8,9},{9,8},{10,11... | collective-permute-start | bytes 4718600 | tf_op jit(solution)/shard_map/ppermute | solution.py:725
  59.8 35.4 %all-to-all-start.2 = ((f32[8,208,256]{2,1,0:T(8,128)}), f32[8,208,256]{2,1,0:T(8,128)S(1)}, u32[]{:S(2)}, u32[]{:S(2)}) async-start(f32[8,208,256]{2,1,0:T(8,128)} %get-tuple-element.94), calls=%async_computation.2 | async-start | bytes 3407872 | tf_op jit(solution)/shard_map/all_to_all | solution.py:730
  63.9 1.1 copy-start.18
  95.2 4.2 %copy-start.11 = (f32[8,128]{1,0:T(8,128)S(1)}, f32[8,128]{1,0:T(8,128)}, u32[]{:S(2)}) copy-start(f32[8,128]{1,0:T(8,128)} %get-tuple-element.95.refs_1_) | copy-start | bytes 12292
  95.2 43.3 %all-to-all-start.3 = ((f32[8,208,256]{2,1,0:T(8,128)}), f32[8,208,256]{2,1,0:T(8,128)S(1)}, u32[]{:S(2)}, u32[]{:S(2)}) async-start(f32[8,208,256]{2,1,0:T(8,128)} %get-tuple-element.119), calls=%async_computation.3 | async-start | bytes 3407872 | tf_op jit(solution)/shard_map/all_to_all | solution.py:748
  100.1 37.1 %collective-permute-start.3 = (f32[208,256]{1,0:T(8,128)S(1)}, f32[208,256]{1,0:T(8,128)S(1)}, u32[]{:S(2)}, u32[]{:S(2)}) collective-permute-start(f32[208,256]{1,0:T(8,128)S(1)} %get-tuple-element.126.refs_0_), channel_id=1, source_target_pairs={{0,8},{8,0},{16,24},{24,16},{1,9},{9,1},{17,25},{25,17},{2,10},{10... | collective-permute-start | bytes 638984 | tf_op jit(solution)/shard_map/ppermute | solution.py:690
  139.2 3.4 %copy-start.16 = (f32[4,224,256]{2,1,0:T(8,128)S(1)}, f32[4,224,256]{2,1,0:T(8,128)}, u32[]{:S(2)}) copy-start(f32[4,224,256]{2,1,0:T(8,128)} %get-tuple-element.124) | copy-start | bytes 2752516
  139.9 2.7 %collective-permute-start.4 = (f32[4,224,256]{2,1,0:T(8,128)}, f32[4,224,256]{2,1,0:T(8,128)S(1)}, u32[]{:S(2)}, u32[]{:S(2)}) collective-permute-start(f32[4,224,256]{2,1,0:T(8,128)} %shard_map.207), channel_id=1, source_target_pairs={{0,1},{1,0},{2,3},{3,2},{4,5},{5,4},{6,7},{7,6},{8,9},{9,8},{10,11... | collective-permute-start | bytes 2752520 | tf_op jit(solution)/shard_map/ppermute | solution.py:750
  143.7 17.9 %all-to-all-start.4 = ((f32[4,224,256]{2,1,0:T(8,128)}), f32[4,224,256]{2,1,0:T(8,128)S(1)}, u32[]{:S(2)}, u32[]{:S(2)}) async-start(f32[4,224,256]{2,1,0:T(8,128)} %add.8), calls=%async_computation.4 | async-start | bytes 1835008 | tf_op jit(solution)/shard_map/all_to_all | solution.py:687
  147.8 12.9 %collective-permute-start.2 = (f32[208,256]{1,0:T(8,128)S(1)}, f32[208,256]{1,0:T(8,128)S(1)}, u32[]{:S(2)}, u32[]{:S(2)}) collective-permute-start(f32[208,256]{1,0:T(8,128)S(1)} %get-tuple-element.121.refs_0_), channel_id=1, source_target_pairs={{0,8},{8,0},{16,24},{24,16},{1,9},{9,1},{17,25},{25,17},{2,10},{10... | collective-permute-start | bytes 638984 | tf_op jit(solution)/shard_map/ppermute | solution.py:690
  157.6 18.3 %collective-permute-start.5 = (f32[208,256]{1,0:T(8,128)S(1)}, f32[208,256]{1,0:T(8,128)S(1)}, u32[]{:S(2)}, u32[]{:S(2)}) collective-permute-start(f32[208,256]{1,0:T(8,128)S(1)} %get-tuple-element.131.refs_0_), channel_id=1, source_target_pairs={{0,16},{8,24},{16,0},{24,8},{1,17},{9,25},{17,1},{25,9},{2,18},{10... | collective-permute-start | bytes 638984 | tf_op jit(solution)/shard_map/ppermute | solution.py:690
  161.4 2.1 %copy-start.10 = (f32[8,128]{1,0:T(8,128)}, f32[8,128]{1,0:T(8,128)S(1)}, u32[]{:S(2)}) copy-start(f32[8,128]{1,0:T(8,128)S(1)} %get-tuple-element.123.refs_21_) | copy-start | bytes 12292
  161.4 25.7 %collective-permute-start.7 = (f32[208,256]{1,0:T(8,128)S(1)}, f32[208,256]{1,0:T(8,128)S(1)}, u32[]{:S(2)}, u32[]{:S(2)}) collective-permute-start(f32[208,256]{1,0:T(8,128)S(1)} %get-tuple-element.138.refs_0_), channel_id=1, source_target_pairs={{0,16},{8,24},{16,0},{24,8},{1,17},{9,25},{17,1},{25,9},{2,18},{10... | collective-permute-start | bytes 638984 | tf_op jit(solution)/shard_map/ppermute | solution.py:690
  161.6 2.0 %copy-start.13 = (f32[8,128]{1,0:T(8,128)}, f32[8,128]{1,0:T(8,128)S(1)}, u32[]{:S(2)}) copy-start(f32[8,128]{1,0:T(8,128)S(1)} %get-tuple-element.129.refs_22_) | copy-start | bytes 12292
  161.6 15.1 %collective-permute-start.6 = (f32[224,256]{1,0:T(8,128)S(1)}, f32[224,256]{1,0:T(8,128)S(1)}, u32[]{:S(2)}, u32[]{:S(2)}) collective-permute-start(f32[224,256]{1,0:T(8,128)S(1)} %get-tuple-element.134.refs_0_), channel_id=1, source_target_pairs={{0,8},{8,0},{16,24},{24,16},{1,9},{9,1},{17,25},{25,17},{2,10},{10... | collective-permute-start | bytes 688136 | tf_op jit(solution)/shard_map/ppermute | solution.py:690
  176.7 12.5 %collective-permute-start.8 = (f32[224,256]{1,0:T(8,128)S(1)}, f32[224,256]{1,0:T(8,128)S(1)}, u32[]{:S(2)}, u32[]{:S(2)}) collective-permute-start(f32[224,256]{1,0:T(8,128)S(1)} %get-tuple-element.141.refs_2_), channel_id=1, source_target_pairs={{0,16},{8,24},{16,0},{24,8},{1,17},{9,25},{17,1},{25,9},{2,18},{10... | collective-permute-start | bytes 688136 | tf_op jit(solution)/shard_map/ppermute | solution.py:690
  177.3 11.9 %copy-start = (f32[6,32,256]{2,1,0:T(8,128)S(1)}, f32[6,32,256]{2,1,0:T(8,128)}, u32[]{:S(2)}) copy-start(f32[6,32,256]{2,1,0:T(8,128)} %refs_4_.1) | copy-start | bytes 589828
  177.3 11.9 %copy-start.1 = (f32[6,32]{1,0:T(8,128)S(1)}, f32[6,32]{1,0:T(8,128)}, u32[]{:S(2)}) copy-start(f32[6,32]{1,0:T(8,128)} %refs_5_.1) | copy-start | bytes 2308
  177.3 11.9 %copy-start.2 = (f32[6,32]{1,0:T(8,128)S(1)}, f32[6,32]{1,0:T(8,128)}, u32[]{:S(2)}) copy-start(f32[6,32]{1,0:T(8,128)} %refs_6_.1) | copy-start | bytes 2308
  (10 other events, 6.4 us)

commit v6 on v5

--- a/solution.py
+++ b/solution.py
@@ -97,6 +97,10 @@
     )(*arrays, *after)
 
 
+def used_by(group):
+    return sorted({o for e in group for o, _ in uses(e)})
+
+
 def pack_weights(groups, w_in_ref, w_out_ref, to_ref):
     rows_in, rows_out = w_in_ref.shape[1], w_out_ref.shape[1]
     at = 0
@@ -132,7 +136,7 @@
     )(in_bias, gain, shift, out_bias, task_gate.transpose(0, 2, 1), shared_gate.T, w_in, w_out)
 
 
-def prep_kernel(x_ref, c_ref, valid_ref, w_in_ref, w_out_ref, xh_ref, xl_ref, ct_ref, to_ref, done_ref):
+def prep_kernel(x_ref, c_refs, valid_ref, w_in_ref, w_out_ref, xh_ref, xl_ref, ct_ref, to_ref, done_ref):
     depth = x_ref.shape[1]
 
     @pl.when(pl.program_id(0) == 0)
@@ -145,20 +149,22 @@
     xh_ref[depth:] = jnp.ones((xh_ref.shape[0] - depth, xh_ref.shape[1]), BF16)
     xl_ref[...] = low
     valid = valid_ref[...]
-    for o in range(c_ref.shape[0]):
-        ct_ref[o] = c_ref[o].T * valid
+    for k, c_ref in enumerate(c_refs):
+        ct_ref[k] = c_ref[0].T * valid
 
 
 def prep(features, cotangent, valid, w_in, w_out, pairs):
     rows, depth = features.shape
     packed = sum(len(g) for g in GROUPS[1:]) * (w_in.shape[1] + w_out.shape[1])
-    outs, _, units = cotangent.shape
+    units = cotangent.shape[2]
+    used = used_by(GROUPS[0])
+    outs = len(used)
     return pl.pallas_call(
         prep_kernel,
         grid=(rows // TILE,),
         in_specs=[
             pl.BlockSpec((TILE, depth), lambda i: (i, 0)),
-            pl.BlockSpec((outs, TILE, units), lambda i: (0, i, 0)),
+            [pl.BlockSpec((1, TILE, units), lambda i, o=o: (o, i, 0)) for o in used],
             pl.BlockSpec((1, TILE), lambda i: (0, i)),
             pl.BlockSpec(w_in.shape, lambda i: (0, 0, 0)),
             pl.BlockSpec(w_out.shape, lambda i: (0, 0, 0)),
@@ -178,8 +184,8 @@
             jax.ShapeDtypeStruct(TOKEN, F32),
         ],
         compiler_params=pltpu.CompilerParams(vmem_limit_bytes=VMEM_BYTES),
-        cost_estimate=pl.CostEstimate(flops=0, bytes_accessed=32000000, transcendentals=0),
-    )(features, cotangent, valid, w_in, w_out)
+        cost_estimate=pl.CostEstimate(flops=0, bytes_accessed=26000000, transcendentals=0),
+    )(features, [cotangent] * outs, valid, w_in, w_out)
 
 
 def softmax_rows(v):
@@ -187,10 +193,11 @@
     return e / jnp.sum(e, axis=0, keepdims=True)
 
 
-def expert_kernel(group, first, last, n_after, partial, *refs):
-    used = sorted({o for e in group for o, _ in uses(e)})
+def expert_kernel(group, first, last, n_after, partial, fresh, *refs):
+    used = used_by(group)
     names = ["core", "own", "other"] + ([] if first else ["small"]) + ["xh", "xl"]
-    names += [f"c{o}" for o in used]
+    names += [f"c{o}" for o in used if o not in fresh]
+    names += (["valid"] + [f"cot{o}" for o in fresh]) if fresh else []
     names += [] if first else ["prob"]
     if last:
         names += [f"dp{k}" for k in range(len(GROUPS) - 1)]
@@ -203,7 +210,7 @@
     if first:
         names += ["prob", "small", "gates"]
     names += ["dl"] if last else ["dp"]
-    names += ["done"]
+    names += ["done"] + [f"c{o}" for o in fresh]
     each = ["win_t", "wp", "wp_t", "b_in", "b_out", "acc_w", "acc_g"]
     each += ["h", "u", "a", "xhat", "h2", "g", "ex", "xhh", "xhl", "dzh", "dzl"]
     names += [f"{name}{l}" for name in each for l in range(len(group))]
@@ -389,6 +396,8 @@
         r["acc_w"][l][0:depth] += dot(r["xl"][...], high, NT)
 
     chains = [(l, s) for l in range(count) for s in spans]
+    for o in fresh:
+        r[f"c{o}"][0] = r[f"cot{o}"][0].T * r["valid"][...]
     for stage in ORDER:
         if isinstance(stage, tuple):
             name, k = stage
@@ -420,8 +429,8 @@
             r["dl"][lower:upper] = p * (d - jnp.sum(p * d, axis=0, keepdims=True))
         r["dl"][14:16] = jnp.zeros((2, tile), F32)
         high, low = halves(r["dl"][...])
-        both = dot(r["xh"][0:depth], jnp.concatenate([high, low], 0), NT)
-        r["acc_gate"][:, 0:GATES] += both[:, 0:GATES] + both[:, GATES:] + dot(r["xl"][...], high, NT)
+        both = dot(jnp.concatenate([high, low], 0), r["xh"][0:depth], NT)
+        r["acc_gate"][...] += both[0:GATES] + both[GATES:] + dot(high, r["xl"][...], NT)
 
     @pl.when(step == pl.num_programs(0) - 1)
     def _():
@@ -442,7 +451,7 @@
                 dst[q, base + rows_in : base + rows_all] = r["acc_g"][l][pl.ds(place * rows_out, rows_out)]
                 dst[q, base + rows_all : base + rows_all + 8] = tail
         if last:
-            gate = r["acc_gate"][...].T[0:GATES]
+            gate = r["acc_gate"][...]
             base = count * (rows_all + 8)
             for q in range(pairs):
                 even = gate[:, 2 * q * rows_in : (2 * q + 1) * rows_in]
@@ -451,7 +460,7 @@
                     dst[q, base:, 0:rows_in] = jnp.where(at == 0, even, odd)
 
 
-def expert_call(group, core, own, other, small, xh, xl, ct, prob, dps, last, after, skip, mixed):
+def expert_call(group, core, own, other, small, xh, xl, cts, valid, cotangent, prob, dps, last, after, skip, mixed):
     first = small is None
     pairs, _, units = own.shape
     depth, rows = xl.shape
@@ -460,8 +469,9 @@
     count = len(group)
     whole = lambda shape: pl.BlockSpec(shape, lambda i: (0,) * len(shape))
     along = lambda n: pl.BlockSpec((n, TILE), lambda i: (0, i))
-    used = sorted({o for e in group for o, _ in uses(e)})
-    ins = [core, own, other] + ([] if first else [small]) + [xh, xl] + [ct] * len(used)
+    used = used_by(group)
+    old, fresh = [o for o in used if o in cts], tuple(o for o in used if o not in cts)
+    ins = [core, own, other] + ([] if first else [small]) + [xh, xl] + [cts[o][0] for o in old]
     held = own.shape[1] if first else count * (rows_in + rows_out)
     weights = pl.BlockSpec((pairs, held, units), lambda i: (0, skip, 0))
     in_specs = [
@@ -472,7 +482,11 @@
         along(xh.shape[0]),
         along(depth),
     ]
-    in_specs += [pl.BlockSpec((1, units, TILE), lambda i, o=o: (o, 0, i)) for o in used]
+    in_specs += [pl.BlockSpec((1, units, TILE), lambda i, k=cts[o][1]: (k, 0, i)) for o in old]
+    if fresh:
+        ins += [valid] + [cotangent] * len(fresh)
+        in_specs.append(along(1))
+        in_specs += [pl.BlockSpec((1, TILE, units), lambda i, o=o: (o, i, 0)) for o in fresh]
     if not first:
         ins.append(prob)
         in_specs.append(along(GATES))
@@ -512,6 +526,9 @@
     else:
         outs.append((along(8), shape((8, rows), F32)))
     outs.append((whole(TOKEN), shape(TOKEN, F32)))
+    outs += [
+        (pl.BlockSpec((1, units, TILE), lambda i: (0, 0, i)), shape((1, units, rows), F32)) for _ in fresh
+    ]
     top = units + (GATES if first else 0)
     kinds = [
         ((2 * top, depth), BF16),
@@ -535,10 +552,10 @@
     ]
     scratch = [pltpu.VMEM(*kind) for kind in kinds for _ in group]
     if last:
-        scratch += [pltpu.VMEM((GATES, TILE), F32), pltpu.VMEM((depth, LANES), F32)]
+        scratch += [pltpu.VMEM((GATES, TILE), F32), pltpu.VMEM((GATES, depth), F32)]
         scratch += [pltpu.VMEM((units, TILE), F32)] * len(used)
     return pl.pallas_call(
-        functools.partial(expert_kernel, group, first, last, len(after), tuple(sorted(mixed))),
+        functools.partial(expert_kernel, group, first, last, len(after), tuple(sorted(mixed)), fresh),
         grid=(rows // TILE,),
         in_specs=in_specs,
         out_specs=[o[0] for o in outs],
@@ -706,7 +723,8 @@
         valid = (lax.broadcasted_iota(jnp.int32, (1, rows), 1) < counts[0]) & (keep.reshape(1, rows) > 0)
         me = lax.axis_index("fsdp")
         core = (me % 2).astype(jnp.int32).reshape(1)
-        xh, xl, ct, spread, done = prep(features, cotangent, valid.astype(F32), w_in, w_out, pairs)
+        valid = valid.astype(F32)
+        xh, xl, ct, spread, done = prep(features, cotangent, valid, w_in, w_out, pairs)
         own0 = tie(
             spread_out(
                 pack(pairs, w_in, in_bias, norm_gain, norm_bias, w_out, out_bias, task_gate, shared_gate)
@@ -714,19 +732,22 @@
             [done],
         )
         other0 = lax.ppermute(own0, "fsdp", twin)
+        cts = {o: (ct, k) for k, o in enumerate(used_by(GROUPS[0]))}
+
         def parts_of(got, group):
             n = len(group)
             m = 1 if group == GROUPS[-1] else len({o for e in group for o, _ in uses(e)})
             return got[:n], got[n : 2 * n], got[2 * n : 2 * n + m], got[2 * n + m :]
 
-        got = expert_call(GROUPS[0], core, own0, other0, None, xh, xl, ct, None, [], False, [], 0, {})
+        got = expert_call(GROUPS[0], core, own0, other0, None, xh, xl, cts, valid, cotangent, None, [], False, [], 0, {})
         dah0, dal0, mix0, (wih0, wil0, grads0, prob, small, gates, dp0, done0) = parts_of(got, GROUPS[0])
         own1 = tie(spread_out(spread), [done0])
         other1 = lax.ppermute(own1, "fsdp", twin)
         got = expert_call(
-            GROUPS[1], core, own1, other1, small, xh, xl, ct, prob, [], False, [], 0, {2: mix0[1]}
+            GROUPS[1], core, own1, other1, small, xh, xl, cts, valid, cotangent, prob, [], False, [], 0, {2: mix0[1]}
         )
-        dah1, dal1, mix1, (wih1, wil1, grads1, dp1, done1) = parts_of(got, GROUPS[1])
+        dah1, dal1, mix1, (wih1, wil1, grads1, dp1, done1, *fresh) = parts_of(got, GROUPS[1])
+        cts.update(zip([o for o in used_by(GROUPS[1]) if o not in cts], [(c, 0) for c in fresh]))
         sum0, token0 = total([lax.all_to_all(grads0, "fsdp", 0, 0)], [done1])
         got = expert_call(
             GROUPS[2],
@@ -736,7 +757,9 @@
             small,
             xh,
             xl,
-            ct,
+            cts,
+            valid,
+            cotangent,
             prob,
             [dp0, dp1],
             True,

time: 192 us -> 190 us (0.990)
  Pallas kernels: 144 us -> 142 us
    pallas_call x1, Pallas kernels: 14.2 us -> 11.7 us  [prep(): pl.pallas_call(prep_kernel, grid=(rows // TILE,), in_specs=[pl.BlockSpec(...]
  transfers between devices with their start and end apart: 14 -> 14, of which waited for: 3 -> 4; matrix products, arithmetic and copies ran while one was open for 0% -> 0% of each run, Pallas kernels for 73% -> 73%
where the time goes in v6:
time: 190 us; the launch traced here: 189 us
  Pallas kernels  142 us (75%)
  starting transfers between devices  30.2 us (16%)
  local copies, waits for them, and re-layouts  7.68 us (4%)
  waiting for transfers between devices  6.11 us (3%)
    pallas_call x3, Pallas kernels, expert_call(): pl.pallas_call(functools.partial(expert_kernel, group, first, last, len(a...  95.6 us
    pallas_call x3, Pallas kernels, final_call(): pl.pallas_call(functools.partial(final_kernel, steps), grid=(steps,), in_...  29.3 us
    all_to_all x3, starting transfers between devices, spread_out(): return lax.all_to_all(x, 'fsdp', 0, 0, axis_index_groups=across)  13.7 us
    pallas_call x1, Pallas kernels, prep(): pl.pallas_call(prep_kernel, grid=(rows // TILE,), in_specs=[pl.BlockSpec(...  11.7 us
    unnamed x40, local copies, waits for them, and re-layouts  7.68 us
    ppermute x6, starting transfers between devices, swap(): return lax.ppermute(x, 'dp', [(i, i ^ bit) for i in range(n_dp)])  7.42 us
    all_to_all x1, starting transfers between devices, on_device(): sum1, token1 = total([lax.all_to_all(grads1, 'fsdp', 0, 0)], [done2])  4.21 us
    all_to_all x1, starting transfers between devices, on_device(): sum0, token0 = total([lax.all_to_all(grads0, 'fsdp', 0, 0)], [done1])  4.01 us
  transfers between devices with their start and end apart: 14, of which 4 were waited for; matrix products, arithmetic and copies ran while one was open for 0% of the time, Pallas kernels for 73%

profile of v6, /device:TPU:0, one launch (start us, length us, event | category | flops | bytes accessed | tf_op | source)
XLA Modules:
  0.0 189.3 jit_solution(14445059065948508176)
XLA Ops:
  0.7 2.2 %shard_map.196 = f32[4,232,256]{2,1,0:T(8,128)} custom-call(f32[6,32]{1,0:T(8,128)} %in_bias.1, f32[6,32]{1,0:T(8,128)} %refs_5_.1, f32[6,32]{1,0:T(8,128)} %refs_6_.1, f32[6,32]{1,0:T(8,128)} %out_bias.1, f32[2,4,64]{2,1,0:T(4,128)} %bitcast.11, f32[6,64]{1,0:T(8,128)} %bitcast.12, f32[6,64,256]{2,1,0:T(8,128)} %w_in_ref.3, f32[6,32,256]{2,1,0:T(8,128)} %refs_4_.1), custom_call_target="tpu_custom_call" | custom-call | tf_op jit(solution)/shard_map/pallas_call | solution.py:132
  2.8 5.2 %all-to-all-start.1 = ((f32[4,232,256]{2,1,0:T(8,128)}), f32[4,232,256]{2,1,0:T(8,128)}, u32[]{:S(2)}, u32[]{:S(2)}) async-start(f32[4,232,256]{2,1,0:T(8,128)} %shard_map.196), calls=%async_computation.1 | async-start | bytes 1900544 | tf_op jit(solution)/shard_map/all_to_all | solution.py:704
  9.2 11.7 %shard_map.195 = (bf16[528,3072]{1,0:T(8,128)(2,1)}, bf16[512,3072]{1,0:T(8,128)(2,1)}, f32[2,256,3072]{2,1,0:T(8,128)}, f32[4,384,256]{2,1,0:T(8,128)}, f32[8,128]{1,0:T(8,128)}) custom-call(f32[3072,512]{1,0:T(8,128)} %x_ref.1, f32[3,3072,256]{2,1,0:T(8,128)} %refs_8_.1, f32[3,3072,256]{2,1,0:T(8,128)} %refs_8_.1, f32[1,3072]{1,0:T(1,128)} %bitcast.9, ...), custom_call_target="tpu_custom_call" | custom-call | bytes 26000000 | tf_op jit(solution)/shard_map/pallas_call | solution.py:162
  21.2 4.4 %all-to-all-start = ((f32[4,384,256]{2,1,0:T(8,128)}), f32[4,384,256]{2,1,0:T(8,128)}, u32[]{:S(2)}, u32[]{:S(2)}) async-start(f32[4,384,256]{2,1,0:T(8,128)} %get-tuple-element.81), calls=%async_computation | async-start | bytes 3145728 | tf_op jit(solution)/shard_map/all_to_all | solution.py:704
  25.6 1.0 copy-done.19
  26.6 30.2 %shard_map.198 = (bf16[256,3072]{1,0:T(8,128)(2,1)}, bf16[256,3072]{1,0:T(8,128)(2,1)}, bf16[256,3072]{1,0:T(8,128)(2,1)}, bf16[256,3072]{1,0:T(8,128)(2,1)}, f3...) custom-call(s32[1]{0:T(128)} %bitcast.refs_0_, ...), custom_call_target="tpu_custom_call" | custom-call | flops 20000000000 | bytes 30000000 | tf_op jit(solution)/shard_map/pallas_call | solution.py:557
  57.4 4.0 %all-to-all-start.2 = ((f32[8,208,256]{2,1,0:T(8,128)}), f32[8,208,256]{2,1,0:T(8,128)S(1)}, u32[]{:S(2)}, u32[]{:S(2)}) async-start(f32[8,208,256]{2,1,0:T(8,128)} %get-tuple-element.96), calls=%async_computation.2 | async-start | bytes 3407872 | tf_op jit(solution)/shard_map/all_to_all | solution.py:751
  61.4 1.1 copy-done.18
  62.6 30.6 %shard_map.200 = (bf16[256,3072]{1,0:T(8,128)(2,1)}, bf16[256,3072]{1,0:T(8,128)(2,1)}, bf16[256,3072]{1,0:T(8,128)(2,1)}, bf16[256,3072]{1,0:T(8,128)(2,1)}, f3...) custom-call(s32[1]{0:T(128)} %bitcast.refs_0_, ...), custom_call_target="tpu_custom_call" | custom-call | flops 20000000000 | bytes 30000000 | tf_op jit(solution)/shard_map/pallas_call | solution.py:557
  93.2 4.2 %all-to-all-start.3 = ((f32[8,208,256]{2,1,0:T(8,128)}), f32[8,208,256]{2,1,0:T(8,128)S(1)}, u32[]{:S(2)}, u32[]{:S(2)}) async-start(f32[8,208,256]{2,1,0:T(8,128)} %get-tuple-element.121), calls=%async_computation.3 | async-start | bytes 3407872 | tf_op jit(solution)/shard_map/all_to_all | solution.py:771
  98.1 2.0 %collective-permute-start.3 = (f32[208,256]{1,0:T(8,128)S(1)}, f32[208,256]{1,0:T(8,128)S(1)}, u32[]{:S(2)}, u32[]{:S(2)}) collective-permute-start(f32[208,256]{1,0:T(8,128)S(1)} %get-tuple-element.128.refs_0_), channel_id=1, source_target_pairs={{0,8},{8,0},{16,24},{24,16},{1,9},{9,1},{17,25},{25,17},{2,10},{10... | collective-permute-start | bytes 638984 | tf_op jit(solution)/shard_map/ppermute | solution.py:707
  100.1 34.8 %shard_map.202 = (bf16[256,3072]{1,0:T(8,128)(2,1)}, bf16[256,3072]{1,0:T(8,128)(2,1)}, bf16[256,3072]{1,0:T(8,128)(2,1)}, bf16[256,3072]{1,0:T(8,128)(2,1)}, f3...) custom-call(s32[1]{0:T(128)} %bitcast.refs_0_, ...), custom_call_target="tpu_custom_call" | custom-call | flops 20000000000 | bytes 30000000 | tf_op jit(solution)/shard_map/pallas_call | solution.py:557
  137.8 2.5 %collective-permute-done.4 = f32[4,224,256]{2,1,0:T(8,128)S(1)} collective-permute-done((f32[4,224,256]{2,1,0:T(8,128)}, f32[4,224,256]{2,1,0:T(8,128)S(1)}, u32[]{:S(2)}, u32[]{:S(2)}) %collective-permute-start.4) | collective-permute-done | bytes 917536 | tf_op jit(solution)/shard_map/ppermute | solution.py:773
  140.3 1.0 add.8
  141.3 4.2 %all-to-all-start.4 = ((f32[4,224,256]{2,1,0:T(8,128)}), f32[4,224,256]{2,1,0:T(8,128)S(1)}, u32[]{:S(2)}, u32[]{:S(2)}) async-start(f32[4,224,256]{2,1,0:T(8,128)} %add.8), calls=%async_computation.4 | async-start | bytes 1835008 | tf_op jit(solution)/shard_map/all_to_all | solution.py:704
  145.5 9.8 %shard_map.203 = (f32[3072,512]{1,0:T(8,128)}, f32[8,128]{1,0:T(8,128)}) custom-call(bf16[256,3072]{1,0:T(8,128)(2,1)} %get-tuple-element.100.refs_0_, bf16[256,3072]{1,0:T(8,128)(2,1)} %get-tuple-element.101.refs_1_, bf16[256,3072]{1,0:T(8,128)(2,1)} %get-tuple-element.102.refs_2_, bf16[256,3072]{1,0:T(8,128)(2,1)} %get-tuple-element.103.refs_3_, ...), custom_call_target="tpu_custom_call" | custom-call | flops 5000000000 | bytes 8333333 | tf_op jit(solution)/shard_map/pallas_call | solution.py:608
  155.3 3.1 %collective-permute-start.5 = (f32[208,256]{1,0:T(8,128)S(1)}, f32[208,256]{1,0:T(8,128)S(1)}, u32[]{:S(2)}, u32[]{:S(2)}) collective-permute-start(f32[208,256]{1,0:T(8,128)S(1)} %get-tuple-element.133.refs_0_), channel_id=1, source_target_pairs={{0,16},{8,24},{16,0},{24,8},{1,17},{9,25},{17,1},{25,9},{2,18},{10... | collective-permute-start | bytes 638984 | tf_op jit(solution)/shard_map/ppermute | solution.py:707
  158.4 0.7 copy-done.5
  159.3 2.0 %collective-permute-start.6 = (f32[224,256]{1,0:T(8,128)S(1)}, f32[224,256]{1,0:T(8,128)S(1)}, u32[]{:S(2)}, u32[]{:S(2)}) collective-permute-start(f32[224,256]{1,0:T(8,128)S(1)} %get-tuple-element.136.refs_0_), channel_id=1, source_target_pairs={{0,8},{8,0},{16,24},{24,16},{1,9},{9,1},{17,25},{25,17},{2,10},{10... | collective-permute-start | bytes 688136 | tf_op jit(solution)/shard_map/ppermute | solution.py:707
  161.3 9.8 %shard_map.209 = (f32[3072,512]{1,0:T(8,128)}, f32[8,128]{1,0:T(8,128)}) custom-call(bf16[256,3072]{1,0:T(8,128)(2,1)} %get-tuple-element.100.refs_0_, bf16[256,3072]{1,0:T(8,128)(2,1)} %get-tuple-element.101.refs_1_, bf16[256,3072]{1,0:T(8,128)(2,1)} %get-tuple-element.102.refs_2_, ...), custom_call_target="tpu_custom_call", output_to_operand_aliasing={{0}: (20, {})} | custom-call | flops 5000000000 | bytes 8333333 | tf_op jit(solution)/shard_map/pallas_call | solution.py:608
  171.0 2.6 %collective-permute-done.5.refs_1_ = f32[208,256]{1,0:T(8,128)S(1)} collective-permute-done((f32[208,256]{1,0:T(8,128)S(1)}, f32[208,256]{1,0:T(8,128)S(1)}, u32[]{:S(2)}, u32[]{:S(2)}) %collective-permute-start.5) | collective-permute-done | bytes 213024 | tf_op jit(solution)/shard_map/ppermute | solution.py:707
  175.0 9.8 %shard_map.212 = (f32[3072,512]{1,0:T(8,128)}, f32[8,128]{1,0:T(8,128)}) custom-call(bf16[256,3072]{1,0:T(8,128)(2,1)} %get-tuple-element.100.refs_0_, bf16[256,3072]{1,0:T(8,128)(2,1)} %get-tuple-element.101.refs_1_, bf16[256,3072]{1,0:T(8,128)(2,1)} %get-tuple-element.102.refs_2_, ...), custom_call_target="tpu_custom_call", output_to_operand_aliasing={{0}: (20, {})} | custom-call | flops 5000000000 | bytes 8333333 | tf_op jit(solution)/shard_map/pallas_call | solution.py:608
  186.1 0.8 collective-permute-done.8.refs_3_
  186.9 2.4 %shard_map.214 = (f32[6,64,256]{2,1,0:T(8,128)}, f32[6,32]{1,0:T(8,128)}, f32[6,32]{1,0:T(8,128)}, f32[6,32]{1,0:T(8,128)}, f32[6,32,256]{2,1,0:T(8,128)}, /*ind...) custom-call(s32[1]{0:T(128)} %bitcast.5.me_ref, f32[208,256]{1,0:T(8,128)S(1)} %get-tuple-element.139.refs_0_, ...), custom_call_target="tpu_custom_call" | custom-call | tf_op jit(solution)/shard_map/pallas_call | solution.py:687
  (66 shorter events, 7.8 us)
Async XLA Ops:
  0.6 8.0 %copy-start.17 = (s32[3072]{0:T(1024)S(1)}, s32[3072]{0:T(1024)}, u32[]{:S(2)}) copy-start(s32[3072]{0:T(1024)} %param.15) | copy-start | bytes 36868
  2.8 18.4 %all-to-all-start.1 = ((f32[4,232,256]{2,1,0:T(8,128)}), f32[4,232,256]{2,1,0:T(8,128)}, u32[]{:S(2)}, u32[]{:S(2)}) async-start(f32[4,232,256]{2,1,0:T(8,128)} %shard_map.196), calls=%async_computation.1 | async-start | bytes 1900544 | tf_op jit(solution)/shard_map/all_to_all | solution.py:704
  21.2 4.4 %collective-permute-start = (f32[4,232,256]{2,1,0:T(8,128)}, f32[4,232,256]{2,1,0:T(8,128)S(1)}, u32[]{:S(2)}, u32[]{:S(2)}) collective-permute-start(f32[4,232,256]{2,1,0:T(8,128)} %shard_map.197.refs_1_), channel_id=1, source_target_pairs={{0,1},{1,0},{2,3},{3,2},{4,5},{5,4},{6,7},{7,6},{8,9},{9,8},{10,11... | collective-permute-start | bytes 2850824 | tf_op jit(solution)/shard_map/ppermute | solution.py:734
  21.2 35.6 %all-to-all-start = ((f32[4,384,256]{2,1,0:T(8,128)}), f32[4,384,256]{2,1,0:T(8,128)}, u32[]{:S(2)}, u32[]{:S(2)}) async-start(f32[4,384,256]{2,1,0:T(8,128)} %get-tuple-element.81), calls=%async_computation | async-start | bytes 3145728 | tf_op jit(solution)/shard_map/all_to_all | solution.py:704
  25.6 1.0 copy-start.19
  56.8 4.6 %collective-permute-start.1 = (f32[4,384,256]{2,1,0:T(8,128)}, f32[4,384,256]{2,1,0:T(8,128)S(1)}, u32[]{:S(2)}, u32[]{:S(2)}) collective-permute-start(f32[4,384,256]{2,1,0:T(8,128)} %shard_map.199.refs_1_), channel_id=1, source_target_pairs={{0,1},{1,0},{2,3},{3,2},{4,5},{5,4},{6,7},{7,6},{8,9},{9,8},{10,11... | collective-permute-start | bytes 4718600 | tf_op jit(solution)/shard_map/ppermute | solution.py:745
  57.4 35.8 %all-to-all-start.2 = ((f32[8,208,256]{2,1,0:T(8,128)}), f32[8,208,256]{2,1,0:T(8,128)S(1)}, u32[]{:S(2)}, u32[]{:S(2)}) async-start(f32[8,208,256]{2,1,0:T(8,128)} %get-tuple-element.96), calls=%async_computation.2 | async-start | bytes 3407872 | tf_op jit(solution)/shard_map/all_to_all | solution.py:751
  61.4 1.2 copy-start.18
  93.2 4.2 %copy-start.10 = (f32[8,128]{1,0:T(8,128)S(1)}, f32[8,128]{1,0:T(8,128)}, u32[]{:S(2)}) copy-start(f32[8,128]{1,0:T(8,128)} %get-tuple-element.97.refs_1_) | copy-start | bytes 12292
  93.2 43.1 %all-to-all-start.3 = ((f32[8,208,256]{2,1,0:T(8,128)}), f32[8,208,256]{2,1,0:T(8,128)S(1)}, u32[]{:S(2)}, u32[]{:S(2)}) async-start(f32[8,208,256]{2,1,0:T(8,128)} %get-tuple-element.121), calls=%async_computation.3 | async-start | bytes 3407872 | tf_op jit(solution)/shard_map/all_to_all | solution.py:771
  98.1 36.8 %collective-permute-start.3 = (f32[208,256]{1,0:T(8,128)S(1)}, f32[208,256]{1,0:T(8,128)S(1)}, u32[]{:S(2)}, u32[]{:S(2)}) collective-permute-start(f32[208,256]{1,0:T(8,128)S(1)} %get-tuple-element.128.refs_0_), channel_id=1, source_target_pairs={{0,8},{8,0},{16,24},{24,16},{1,9},{9,1},{17,25},{25,17},{2,10},{10... | collective-permute-start | bytes 638984 | tf_op jit(solution)/shard_map/ppermute | solution.py:707
  136.9 3.4 %copy-start.16 = (f32[4,224,256]{2,1,0:T(8,128)S(1)}, f32[4,224,256]{2,1,0:T(8,128)}, u32[]{:S(2)}) copy-start(f32[4,224,256]{2,1,0:T(8,128)} %get-tuple-element.126) | copy-start | bytes 2752516
  137.6 2.7 %collective-permute-start.4 = (f32[4,224,256]{2,1,0:T(8,128)}, f32[4,224,256]{2,1,0:T(8,128)S(1)}, u32[]{:S(2)}, u32[]{:S(2)}) collective-permute-start(f32[4,224,256]{2,1,0:T(8,128)} %shard_map.207), channel_id=1, source_target_pairs={{0,1},{1,0},{2,3},{3,2},{4,5},{5,4},{6,7},{7,6},{8,9},{9,8},{10,11... | collective-permute-start | bytes 2752520 | tf_op jit(solution)/shard_map/ppermute | solution.py:773
  141.3 17.9 %all-to-all-start.4 = ((f32[4,224,256]{2,1,0:T(8,128)}), f32[4,224,256]{2,1,0:T(8,128)S(1)}, u32[]{:S(2)}, u32[]{:S(2)}) async-start(f32[4,224,256]{2,1,0:T(8,128)} %add.8), calls=%async_computation.4 | async-start | bytes 1835008 | tf_op jit(solution)/shard_map/all_to_all | solution.py:704
  145.5 12.9 %collective-permute-start.2 = (f32[208,256]{1,0:T(8,128)S(1)}, f32[208,256]{1,0:T(8,128)S(1)}, u32[]{:S(2)}, u32[]{:S(2)}) collective-permute-start(f32[208,256]{1,0:T(8,128)S(1)} %get-tuple-element.123.refs_0_), channel_id=1, source_target_pairs={{0,8},{8,0},{16,24},{24,16},{1,9},{9,1},{17,25},{25,17},{2,10},{10... | collective-permute-start | bytes 638984 | tf_op jit(solution)/shard_map/ppermute | solution.py:707
  155.3 18.3 %collective-permute-start.5 = (f32[208,256]{1,0:T(8,128)S(1)}, f32[208,256]{1,0:T(8,128)S(1)}, u32[]{:S(2)}, u32[]{:S(2)}) collective-permute-start(f32[208,256]{1,0:T(8,128)S(1)} %get-tuple-element.133.refs_0_), channel_id=1, source_target_pairs={{0,16},{8,24},{16,0},{24,8},{1,17},{9,25},{17,1},{25,9},{2,18},{10... | collective-permute-start | bytes 638984 | tf_op jit(solution)/shard_map/ppermute | solution.py:707
  159.1 2.1 %copy-start.11 = (f32[8,128]{1,0:T(8,128)}, f32[8,128]{1,0:T(8,128)S(1)}, u32[]{:S(2)}) copy-start(f32[8,128]{1,0:T(8,128)S(1)} %get-tuple-element.125.refs_21_) | copy-start | bytes 12292
  159.1 25.7 %collective-permute-start.7 = (f32[208,256]{1,0:T(8,128)S(1)}, f32[208,256]{1,0:T(8,128)S(1)}, u32[]{:S(2)}, u32[]{:S(2)}) collective-permute-start(f32[208,256]{1,0:T(8,128)S(1)} %get-tuple-element.140.refs_0_), channel_id=1, source_target_pairs={{0,16},{8,24},{16,0},{24,8},{1,17},{9,25},{17,1},{25,9},{2,18},{10... | collective-permute-start | bytes 638984 | tf_op jit(solution)/shard_map/ppermute | solution.py:707
  159.3 2.0 %copy-start.13 = (f32[8,128]{1,0:T(8,128)}, f32[8,128]{1,0:T(8,128)S(1)}, u32[]{:S(2)}) copy-start(f32[8,128]{1,0:T(8,128)S(1)} %get-tuple-element.131.refs_22_) | copy-start | bytes 12292
  159.3 15.1 %collective-permute-start.6 = (f32[224,256]{1,0:T(8,128)S(1)}, f32[224,256]{1,0:T(8,128)S(1)}, u32[]{:S(2)}, u32[]{:S(2)}) collective-permute-start(f32[224,256]{1,0:T(8,128)S(1)} %get-tuple-element.136.refs_0_), channel_id=1, source_target_pairs={{0,8},{8,0},{16,24},{24,16},{1,9},{9,1},{17,25},{25,17},{2,10},{10... | collective-permute-start | bytes 688136 | tf_op jit(solution)/shard_map/ppermute | solution.py:707
  174.4 12.5 %collective-permute-start.8 = (f32[224,256]{1,0:T(8,128)S(1)}, f32[224,256]{1,0:T(8,128)S(1)}, u32[]{:S(2)}, u32[]{:S(2)}) collective-permute-start(f32[224,256]{1,0:T(8,128)S(1)} %get-tuple-element.143.refs_2_), channel_id=1, source_target_pairs={{0,16},{8,24},{16,0},{24,8},{1,17},{9,25},{17,1},{25,9},{2,18},{10... | collective-permute-start | bytes 688136 | tf_op jit(solution)/shard_map/ppermute | solution.py:707
  175.0 11.9 %copy-start = (f32[6,32,256]{2,1,0:T(8,128)S(1)}, f32[6,32,256]{2,1,0:T(8,128)}, u32[]{:S(2)}) copy-start(f32[6,32,256]{2,1,0:T(8,128)} %refs_4_.1) | copy-start | bytes 589828
  175.0 11.9 %copy-start.1 = (f32[6,32]{1,0:T(8,128)S(1)}, f32[6,32]{1,0:T(8,128)}, u32[]{:S(2)}) copy-start(f32[6,32]{1,0:T(8,128)} %refs_5_.1) | copy-start | bytes 2308
  175.0 11.9 %copy-start.2 = (f32[6,32]{1,0:T(8,128)S(1)}, f32[6,32]{1,0:T(8,128)}, u32[]{:S(2)}) copy-start(f32[6,32]{1,0:T(8,128)} %refs_6_.1) | copy-start | bytes 2308
  (10 other events, 6.4 us)

commit v7 on v6

--- a/solution.py
+++ b/solution.py
@@ -67,6 +67,10 @@
     return jnp.concatenate([block] * (width // LANES), axis=1)
 
 
+def pinned(tokens):
+    return [pltpu.with_memory_space_constraint(token, pltpu.HBM) for token in tokens]
+
+
 def tie(x, after):
     return pl.pallas_call(
         lambda *refs: None,
@@ -74,7 +78,7 @@
         out_specs=pl.BlockSpec(memory_space=pl.ANY),
         out_shape=jax.ShapeDtypeStruct(x.shape, x.dtype),
         input_output_aliases={0: 0},
-    )(x, *after)
+    )(x, *pinned(after))
 
 
 def total_kernel(n, *refs):
@@ -83,7 +87,6 @@
         for part in [ref[...]] if len(ref.shape) == 2 else [ref[k] for k in range(ref.shape[0])]:
             value = part if value is None else value + part
     refs[-2][...] = value
-    refs[-1][...] = jnp.zeros_like(refs[-1])
 
 
 def total(arrays, after):
@@ -91,10 +94,10 @@
     return pl.pallas_call(
         functools.partial(total_kernel, len(arrays)),
         in_specs=[vmem] * len(arrays) + [pl.BlockSpec(memory_space=pltpu.HBM)] * len(after),
-        out_specs=[vmem, vmem],
-        out_shape=[jax.ShapeDtypeStruct(arrays[0].shape[-2:], F32), jax.ShapeDtypeStruct(TOKEN, F32)],
+        out_specs=[vmem, pl.BlockSpec(memory_space=pltpu.HBM)],
+        out_shape=[jax.ShapeDtypeStruct(arrays[0].shape[-2:], F32), pltpu.HBM(TOKEN, F32)],
         compiler_params=pltpu.CompilerParams(vmem_limit_bytes=16 << 20),
-    )(*arrays, *after)
+    )(*arrays, *pinned(after))
 
 
 def used_by(group):
@@ -495,7 +498,7 @@
         in_specs += [along(8)] * len(dps)
     ins += [mixed[o] for o in sorted(mixed)]
     in_specs += [along(units)] * len(mixed)
-    ins += after
+    ins += pinned(after)
     in_specs += [pl.BlockSpec(memory_space=pltpu.HBM)] * len(after)
     packed = count * (rows_in + rows_out + 8)
     shape = jax.ShapeDtypeStruct
@@ -603,7 +606,7 @@
     steps, parts = end - skip, PARTS
     whole = lambda a: pl.BlockSpec(a.shape, lambda i: (0,) * a.ndim)
     along = lambda a: pl.BlockSpec((a.shape[0], TILE), lambda i: (0, i + skip))
-    ins = [*dahs, *dals, *wihs, *wils, dl, gates, *before, *after]
+    ins = [*dahs, *dals, *wihs, *wils, dl, gates, *before, *pinned(after)]
     n = 2 * EXPERTS + 2 * len(GROUPS) + 2
     return pl.pallas_call(
         functools.partial(final_kernel, steps),

time: 190 us -> 187 us (0.984)
  local copies, waits for them, and re-layouts: 7.68 us -> 2.1 us
  waiting for transfers between devices: 6.11 us -> 8.46 us
    unnamed x40 -> x14, local copies, waits for them, and re-layouts: 7.68 us -> 2.1 us
    ppermute x6, waiting for transfers between devices: 3.41 us -> 5.76 us  [swap(): return lax.ppermute(x, 'dp', [(i, i ^ bit) for i in range(n_dp)])]
where the time goes in v7:
time: 187 us; the launch traced here: 186 us
  Pallas kernels  142 us (76%)
  starting transfers between devices  31.1 us (17%)
  waiting for transfers between devices  8.46 us (5%)
  local copies, waits for them, and re-layouts  2.1 us (1%)
    pallas_call x3, Pallas kernels, expert_call(): pl.pallas_call(functools.partial(expert_kernel, group, first, last, len(a...  95.6 us
    pallas_call x3, Pallas kernels, final_call(): pl.pallas_call(functools.partial(final_kernel, steps), grid=(steps,), in_...  29.4 us
    all_to_all x3, starting transfers between devices, spread_out(): return lax.all_to_all(x, 'fsdp', 0, 0, axis_index_groups=across)  13.7 us
    pallas_call x1, Pallas kernels, prep(): pl.pallas_call(prep_kernel, grid=(rows // TILE,), in_specs=[pl.BlockSpec(...  11.7 us
    ppermute x6, starting transfers between devices, swap(): return lax.ppermute(x, 'dp', [(i, i ^ bit) for i in range(n_dp)])  8.17 us
    ppermute x6, waiting for transfers between devices, swap(): return lax.ppermute(x, 'dp', [(i, i ^ bit) for i in range(n_dp)])  5.76 us
    all_to_all x1, starting transfers between devices, on_device(): sum1, token1 = total([lax.all_to_all(grads1, 'fsdp', 0, 0)], [done2])  4.21 us
    all_to_all x1, starting transfers between devices, on_device(): sum0, token0 = total([lax.all_to_all(grads0, 'fsdp', 0, 0)], [done1])  4.06 us
  transfers between devices with their start and end apart: 14, of which 4 were waited for; matrix products, arithmetic and copies ran while one was open for 0% of the time, Pallas kernels for 73%

profile of v7, /device:TPU:0, one launch (start us, length us, event | category | flops | bytes accessed | tf_op | source)
XLA Modules:
  0.0 186.3 jit_solution(3518114396672632739)
XLA Ops:
  0.7 2.2 %shard_map.196 = f32[4,232,256]{2,1,0:T(8,128)} custom-call(f32[6,32]{1,0:T(8,128)} %in_bias.1, f32[6,32]{1,0:T(8,128)} %refs_5_.1, f32[6,32]{1,0:T(8,128)} %refs_6_.1, f32[6,32]{1,0:T(8,128)} %out_bias.1, f32[2,4,64]{2,1,0:T(4,128)} %bitcast.11, f32[6,64]{1,0:T(8,128)} %bitcast.12, f32[6,64,256]{2,1,0:T(8,128)} %w_in_ref.3, f32[6,32,256]{2,1,0:T(8,128)} %refs_4_.1), custom_call_target="tpu_custom_call" | custom-call | tf_op jit(solution)/shard_map/pallas_call | solution.py:135
  2.8 5.2 %all-to-all-start.1 = ((f32[4,232,256]{2,1,0:T(8,128)}), f32[4,232,256]{2,1,0:T(8,128)}, u32[]{:S(2)}, u32[]{:S(2)}) async-start(f32[4,232,256]{2,1,0:T(8,128)} %shard_map.196), calls=%async_computation.1 | async-start | bytes 1900544 | tf_op jit(solution)/shard_map/all_to_all | solution.py:707
  9.2 11.7 %shard_map.195 = (bf16[528,3072]{1,0:T(8,128)(2,1)}, bf16[512,3072]{1,0:T(8,128)(2,1)}, f32[2,256,3072]{2,1,0:T(8,128)}, f32[4,384,256]{2,1,0:T(8,128)}, f32[8,128]{1,0:T(8,128)}) custom-call(f32[3072,512]{1,0:T(8,128)} %x_ref.1, f32[3,3072,256]{2,1,0:T(8,128)} %refs_8_.1, f32[3,3072,256]{2,1,0:T(8,128)} %refs_8_.1, f32[1,3072]{1,0:T(1,128)} %bitcast.9, ...), custom_call_target="tpu_custom_call" | custom-call | bytes 26000000 | tf_op jit(solution)/shard_map/pallas_call | solution.py:165
  21.2 4.4 %all-to-all-start = ((f32[4,384,256]{2,1,0:T(8,128)}), f32[4,384,256]{2,1,0:T(8,128)}, u32[]{:S(2)}, u32[]{:S(2)}) async-start(f32[4,384,256]{2,1,0:T(8,128)} %get-tuple-element.81), calls=%async_computation | async-start | bytes 3145728 | tf_op jit(solution)/shard_map/all_to_all | solution.py:707
  25.6 0.9 copy-done.6
  26.6 30.2 %shard_map.198 = (bf16[256,3072]{1,0:T(8,128)(2,1)}, bf16[256,3072]{1,0:T(8,128)(2,1)}, bf16[256,3072]{1,0:T(8,128)(2,1)}, bf16[256,3072]{1,0:T(8,128)(2,1)}, f3...) custom-call(s32[1]{0:T(128)} %bitcast.refs_0_, ...), custom_call_target="tpu_custom_call" | custom-call | flops 20000000000 | bytes 30000000 | tf_op jit(solution)/shard_map/pallas_call | solution.py:560
  57.4 4.1 %all-to-all-start.2 = ((f32[8,208,256]{2,1,0:T(8,128)}), f32[8,208,256]{2,1,0:T(8,128)S(1)}, u32[]{:S(2)}, u32[]{:S(2)}) async-start(f32[8,208,256]{2,1,0:T(8,128)} %get-tuple-element.96), calls=%async_computation.2 | async-start | bytes 3407872 | tf_op jit(solution)/shard_map/all_to_all | solution.py:754
  61.5 1.1 copy-done.5
  62.6 30.6 %shard_map.200 = (bf16[256,3072]{1,0:T(8,128)(2,1)}, bf16[256,3072]{1,0:T(8,128)(2,1)}, bf16[256,3072]{1,0:T(8,128)(2,1)}, bf16[256,3072]{1,0:T(8,128)(2,1)}, f3...) custom-call(s32[1]{0:T(128)} %bitcast.refs_0_, ...), custom_call_target="tpu_custom_call" | custom-call | flops 20000000000 | bytes 30000000 | tf_op jit(solution)/shard_map/pallas_call | solution.py:560
  93.2 4.2 %all-to-all-start.3 = ((f32[8,208,256]{2,1,0:T(8,128)}), f32[8,208,256]{2,1,0:T(8,128)S(1)}, u32[]{:S(2)}, u32[]{:S(2)}) async-start(f32[8,208,256]{2,1,0:T(8,128)} %get-tuple-element.121), calls=%async_computation.3 | async-start | bytes 3407872 | tf_op jit(solution)/shard_map/all_to_all | solution.py:774
  97.5 2.1 %collective-permute-start.3 = (f32[208,256]{1,0:T(8,128)S(1)}, f32[208,256]{1,0:T(8,128)S(1)}, u32[]{:S(2)}, u32[]{:S(2)}) collective-permute-start(f32[208,256]{1,0:T(8,128)S(1)} %get-tuple-element.128.refs_0_), channel_id=1, source_target_pairs={{0,8},{8,0},{16,24},{24,16},{1,9},{9,1},{17,25},{25,17},{2,10},{10... | collective-permute-start | bytes 638984 | tf_op jit(solution)/shard_map/ppermute | solution.py:710
  99.6 34.8 %shard_map.202 = (bf16[256,3072]{1,0:T(8,128)(2,1)}, bf16[256,3072]{1,0:T(8,128)(2,1)}, bf16[256,3072]{1,0:T(8,128)(2,1)}, bf16[256,3072]{1,0:T(8,128)(2,1)}, f3...) custom-call(s32[1]{0:T(128)} %bitcast.refs_0_, ...), custom_call_target="tpu_custom_call" | custom-call | flops 20000000000 | bytes 30000000 | tf_op jit(solution)/shard_map/pallas_call | solution.py:560
  134.8 2.5 %collective-permute-done.4 = f32[4,224,256]{2,1,0:T(8,128)S(1)} collective-permute-done((f32[4,224,256]{2,1,0:T(8,128)}, f32[4,224,256]{2,1,0:T(8,128)S(1)}, u32[]{:S(2)}, u32[]{:S(2)}) %collective-permute-start.4) | collective-permute-done | bytes 917536 | tf_op jit(solution)/shard_map/ppermute | solution.py:776
  137.3 1.1 add.8
  138.3 4.2 %all-to-all-start.4 = ((f32[4,224,256]{2,1,0:T(8,128)}), f32[4,224,256]{2,1,0:T(8,128)S(1)}, u32[]{:S(2)}, u32[]{:S(2)}) async-start(f32[4,224,256]{2,1,0:T(8,128)} %add.8), calls=%async_computation.4 | async-start | bytes 1835008 | tf_op jit(solution)/shard_map/all_to_all | solution.py:707
  142.6 9.8 %shard_map.203 = (f32[3072,512]{1,0:T(8,128)}, f32[8,128]{1,0:T(8,128)}) custom-call(bf16[256,3072]{1,0:T(8,128)(2,1)} %get-tuple-element.100.refs_0_, bf16[256,3072]{1,0:T(8,128)(2,1)} %get-tuple-element.101.refs_1_, bf16[256,3072]{1,0:T(8,128)(2,1)} %get-tuple-element.102.refs_2_, bf16[256,3072]{1,0:T(8,128)(2,1)} %get-tuple-element.103.refs_3_, ...), custom_call_target="tpu_custom_call" | custom-call | flops 5000000000 | bytes 8333333 | tf_op jit(solution)/shard_map/pallas_call | solution.py:611
  152.3 3.1 %collective-permute-start.5 = (f32[208,256]{1,0:T(8,128)S(1)}, f32[208,256]{1,0:T(8,128)S(1)}, u32[]{:S(2)}, u32[]{:S(2)}) collective-permute-start(f32[208,256]{1,0:T(8,128)S(1)} %get-tuple-element.133.refs_0_), channel_id=1, source_target_pairs={{0,16},{8,24},{16,0},{24,8},{1,17},{9,25},{17,1},{25,9},{2,18},{10... | collective-permute-start | bytes 638984 | tf_op jit(solution)/shard_map/ppermute | solution.py:710
  155.6 1.9 %collective-permute-start.6 = (f32[224,256]{1,0:T(8,128)S(1)}, f32[224,256]{1,0:T(8,128)S(1)}, u32[]{:S(2)}, u32[]{:S(2)}) collective-permute-start(f32[224,256]{1,0:T(8,128)S(1)} %get-tuple-element.136.refs_0_), channel_id=1, source_target_pairs={{0,8},{8,0},{16,24},{24,16},{1,9},{9,1},{17,25},{25,17},{2,10},{10... | collective-permute-start | bytes 688136 | tf_op jit(solution)/shard_map/ppermute | solution.py:710
  157.5 9.8 %shard_map.209 = (f32[3072,512]{1,0:T(8,128)}, f32[8,128]{1,0:T(8,128)}) custom-call(bf16[256,3072]{1,0:T(8,128)(2,1)} %get-tuple-element.100.refs_0_, bf16[256,3072]{1,0:T(8,128)(2,1)} %get-tuple-element.101.refs_1_, bf16[256,3072]{1,0:T(8,128)(2,1)} %get-tuple-element.102.refs_2_, ...), custom_call_target="tpu_custom_call", output_to_operand_aliasing={{0}: (20, {})} | custom-call | flops 5000000000 | bytes 8333333 | tf_op jit(solution)/shard_map/pallas_call | solution.py:611
  167.3 3.3 %collective-permute-done.5.refs_1_ = f32[208,256]{1,0:T(8,128)S(1)} collective-permute-done((f32[208,256]{1,0:T(8,128)S(1)}, f32[208,256]{1,0:T(8,128)S(1)}, u32[]{:S(2)}, u32[]{:S(2)}) %collective-permute-start.5) | collective-permute-done | bytes 213024 | tf_op jit(solution)/shard_map/ppermute | solution.py:710
  170.7 0.9 collective-permute-start.8
  171.7 9.8 %shard_map.212 = (f32[3072,512]{1,0:T(8,128)}, f32[8,128]{1,0:T(8,128)}) custom-call(bf16[256,3072]{1,0:T(8,128)(2,1)} %get-tuple-element.100.refs_0_, bf16[256,3072]{1,0:T(8,128)(2,1)} %get-tuple-element.101.refs_1_, bf16[256,3072]{1,0:T(8,128)(2,1)} %get-tuple-element.102.refs_2_, ...), custom_call_target="tpu_custom_call", output_to_operand_aliasing={{0}: (20, {})} | custom-call | flops 5000000000 | bytes 8333333 | tf_op jit(solution)/shard_map/pallas_call | solution.py:611
  181.5 2.4 %collective-permute-done.8.refs_3_ = f32[224,256]{1,0:T(8,128)S(1)} collective-permute-done((f32[224,256]{1,0:T(8,128)S(1)}, f32[224,256]{1,0:T(8,128)S(1)}, u32[]{:S(2)}, u32[]{:S(2)}) %collective-permute-start.8) | collective-permute-done | bytes 229408 | tf_op jit(solution)/shard_map/ppermute | solution.py:710
  183.9 2.4 %shard_map.214 = (f32[6,64,256]{2,1,0:T(8,128)}, f32[6,32]{1,0:T(8,128)}, f32[6,32]{1,0:T(8,128)}, f32[6,32]{1,0:T(8,128)}, f32[6,32,256]{2,1,0:T(8,128)}, /*ind...) custom-call(s32[1]{0:T(128)} %bitcast.5.me_ref, f32[208,256]{1,0:T(8,128)S(1)} %get-tuple-element.139.refs_0_, ...), custom_call_target="tpu_custom_call" | custom-call | tf_op jit(solution)/shard_map/pallas_call | solution.py:690
  (40 shorter events, 2.2 us)
Async XLA Ops:
  0.6 8.0 %copy-start.4 = (s32[3072]{0:T(1024)S(1)}, s32[3072]{0:T(1024)}, u32[]{:S(2)}) copy-start(s32[3072]{0:T(1024)} %param.15) | copy-start | bytes 36868
  2.8 18.4 %all-to-all-start.1 = ((f32[4,232,256]{2,1,0:T(8,128)}), f32[4,232,256]{2,1,0:T(8,128)}, u32[]{:S(2)}, u32[]{:S(2)}) async-start(f32[4,232,256]{2,1,0:T(8,128)} %shard_map.196), calls=%async_computation.1 | async-start | bytes 1900544 | tf_op jit(solution)/shard_map/all_to_all | solution.py:707
  21.2 4.4 %collective-permute-start = (f32[4,232,256]{2,1,0:T(8,128)}, f32[4,232,256]{2,1,0:T(8,128)S(1)}, u32[]{:S(2)}, u32[]{:S(2)}) collective-permute-start(f32[4,232,256]{2,1,0:T(8,128)} %shard_map.197.refs_1_), channel_id=1, source_target_pairs={{0,1},{1,0},{2,3},{3,2},{4,5},{5,4},{6,7},{7,6},{8,9},{9,8},{10,11... | collective-permute-start | bytes 2850824 | tf_op jit(solution)/shard_map/ppermute | solution.py:737
  21.2 35.6 %all-to-all-start = ((f32[4,384,256]{2,1,0:T(8,128)}), f32[4,384,256]{2,1,0:T(8,128)}, u32[]{:S(2)}, u32[]{:S(2)}) async-start(f32[4,384,256]{2,1,0:T(8,128)} %get-tuple-element.81), calls=%async_computation | async-start | bytes 3145728 | tf_op jit(solution)/shard_map/all_to_all | solution.py:707
  25.6 1.0 copy-start.6
  56.8 4.6 %collective-permute-start.1 = (f32[4,384,256]{2,1,0:T(8,128)}, f32[4,384,256]{2,1,0:T(8,128)S(1)}, u32[]{:S(2)}, u32[]{:S(2)}) collective-permute-start(f32[4,384,256]{2,1,0:T(8,128)} %shard_map.199.refs_1_), channel_id=1, source_target_pairs={{0,1},{1,0},{2,3},{3,2},{4,5},{5,4},{6,7},{7,6},{8,9},{9,8},{10,11... | collective-permute-start | bytes 4718600 | tf_op jit(solution)/shard_map/ppermute | solution.py:748
  57.4 35.8 %all-to-all-start.2 = ((f32[8,208,256]{2,1,0:T(8,128)}), f32[8,208,256]{2,1,0:T(8,128)S(1)}, u32[]{:S(2)}, u32[]{:S(2)}) async-start(f32[8,208,256]{2,1,0:T(8,128)} %get-tuple-element.96), calls=%async_computation.2 | async-start | bytes 3407872 | tf_op jit(solution)/shard_map/all_to_all | solution.py:754
  61.4 1.1 copy-start.5
  93.2 41.2 %all-to-all-start.3 = ((f32[8,208,256]{2,1,0:T(8,128)}), f32[8,208,256]{2,1,0:T(8,128)S(1)}, u32[]{:S(2)}, u32[]{:S(2)}) async-start(f32[8,208,256]{2,1,0:T(8,128)} %get-tuple-element.121), calls=%async_computation.3 | async-start | bytes 3407872 | tf_op jit(solution)/shard_map/all_to_all | solution.py:774
  97.5 36.9 %collective-permute-start.3 = (f32[208,256]{1,0:T(8,128)S(1)}, f32[208,256]{1,0:T(8,128)S(1)}, u32[]{:S(2)}, u32[]{:S(2)}) collective-permute-start(f32[208,256]{1,0:T(8,128)S(1)} %get-tuple-element.128.refs_0_), channel_id=1, source_target_pairs={{0,8},{8,0},{16,24},{24,16},{1,9},{9,1},{17,25},{25,17},{2,10},{10... | collective-permute-start | bytes 638984 | tf_op jit(solution)/shard_map/ppermute | solution.py:710
  134.4 2.9 %copy-start.3 = (f32[4,224,256]{2,1,0:T(8,128)S(1)}, f32[4,224,256]{2,1,0:T(8,128)}, u32[]{:S(2)}) copy-start(f32[4,224,256]{2,1,0:T(8,128)} %get-tuple-element.126) | copy-start | bytes 2752516
  134.5 2.7 %collective-permute-start.4 = (f32[4,224,256]{2,1,0:T(8,128)}, f32[4,224,256]{2,1,0:T(8,128)S(1)}, u32[]{:S(2)}, u32[]{:S(2)}) collective-permute-start(f32[4,224,256]{2,1,0:T(8,128)} %shard_map.207), channel_id=1, source_target_pairs={{0,1},{1,0},{2,3},{3,2},{4,5},{5,4},{6,7},{7,6},{8,9},{9,8},{10,11... | collective-permute-start | bytes 2752520 | tf_op jit(solution)/shard_map/ppermute | solution.py:776
  138.3 17.2 %all-to-all-start.4 = ((f32[4,224,256]{2,1,0:T(8,128)}), f32[4,224,256]{2,1,0:T(8,128)S(1)}, u32[]{:S(2)}, u32[]{:S(2)}) async-start(f32[4,224,256]{2,1,0:T(8,128)} %add.8), calls=%async_computation.4 | async-start | bytes 1835008 | tf_op jit(solution)/shard_map/all_to_all | solution.py:707
  142.5 12.9 %collective-permute-start.2 = (f32[208,256]{1,0:T(8,128)S(1)}, f32[208,256]{1,0:T(8,128)S(1)}, u32[]{:S(2)}, u32[]{:S(2)}) collective-permute-start(f32[208,256]{1,0:T(8,128)S(1)} %get-tuple-element.123.refs_0_), channel_id=1, source_target_pairs={{0,8},{8,0},{16,24},{24,16},{1,9},{9,1},{17,25},{25,17},{2,10},{10... | collective-permute-start | bytes 638984 | tf_op jit(solution)/shard_map/ppermute | solution.py:710
  152.3 18.3 %collective-permute-start.5 = (f32[208,256]{1,0:T(8,128)S(1)}, f32[208,256]{1,0:T(8,128)S(1)}, u32[]{:S(2)}, u32[]{:S(2)}) collective-permute-start(f32[208,256]{1,0:T(8,128)S(1)} %get-tuple-element.133.refs_0_), channel_id=1, source_target_pairs={{0,16},{8,24},{16,0},{24,8},{1,17},{9,25},{17,1},{25,9},{2,18},{10... | collective-permute-start | bytes 638984 | tf_op jit(solution)/shard_map/ppermute | solution.py:710
  155.4 26.0 %collective-permute-start.7 = (f32[208,256]{1,0:T(8,128)S(1)}, f32[208,256]{1,0:T(8,128)S(1)}, u32[]{:S(2)}, u32[]{:S(2)}) collective-permute-start(f32[208,256]{1,0:T(8,128)S(1)} %get-tuple-element.140.refs_0_), channel_id=1, source_target_pairs={{0,16},{8,24},{16,0},{24,8},{1,17},{9,25},{17,1},{25,9},{2,18},{10... | collective-permute-start | bytes 638984 | tf_op jit(solution)/shard_map/ppermute | solution.py:710
  155.6 15.1 %collective-permute-start.6 = (f32[224,256]{1,0:T(8,128)S(1)}, f32[224,256]{1,0:T(8,128)S(1)}, u32[]{:S(2)}, u32[]{:S(2)}) collective-permute-start(f32[224,256]{1,0:T(8,128)S(1)} %get-tuple-element.136.refs_0_), channel_id=1, source_target_pairs={{0,8},{8,0},{16,24},{24,16},{1,9},{9,1},{17,25},{25,17},{2,10},{10... | collective-permute-start | bytes 688136 | tf_op jit(solution)/shard_map/ppermute | solution.py:710
  170.7 13.2 %collective-permute-start.8 = (f32[224,256]{1,0:T(8,128)S(1)}, f32[224,256]{1,0:T(8,128)S(1)}, u32[]{:S(2)}, u32[]{:S(2)}) collective-permute-start(f32[224,256]{1,0:T(8,128)S(1)} %get-tuple-element.143.refs_2_), channel_id=1, source_target_pairs={{0,16},{8,24},{16,0},{24,8},{1,17},{9,25},{17,1},{25,9},{2,18},{10... | collective-permute-start | bytes 688136 | tf_op jit(solution)/shard_map/ppermute | solution.py:710
  171.6 12.3 %copy-start = (f32[6,32,256]{2,1,0:T(8,128)S(1)}, f32[6,32,256]{2,1,0:T(8,128)}, u32[]{:S(2)}) copy-start(f32[6,32,256]{2,1,0:T(8,128)} %refs_4_.1) | copy-start | bytes 589828
  171.6 12.3 %copy-start.1 = (f32[6,32]{1,0:T(8,128)S(1)}, f32[6,32]{1,0:T(8,128)}, u32[]{:S(2)}) copy-start(f32[6,32]{1,0:T(8,128)} %refs_5_.1) | copy-start | bytes 2308
  171.6 12.3 %copy-start.2 = (f32[6,32]{1,0:T(8,128)S(1)}, f32[6,32]{1,0:T(8,128)}, u32[]{:S(2)}) copy-start(f32[6,32]{1,0:T(8,128)} %refs_6_.1) | copy-start | bytes 2308

commit v8 on v7

--- a/solution.py
+++ b/solution.py
@@ -714,7 +714,7 @@
             x, token = total([x, swap(x, bit)], beside)
         return x, token
 
-    bits = [1 << k for k in range(n_dp.bit_length() - 1)]
+    bits = [1 << k for k in reversed(range(n_dp.bit_length() - 1))]
 
     def on_device(
         features, cotangent, counts, keep, w_in, in_bias, norm_gain, norm_bias, w_out, out_bias, task_gate, shared_gate

time: 187 us -> 185 us (0.989)
  waiting for transfers between devices: 8.46 us -> 4.12 us
  starting transfers between devices: 31.1 us -> 33.9 us
    ppermute x6, waiting for transfers between devices: 5.76 us -> 1.41 us  [swap(): return lax.ppermute(x, 'dp', [(i, i ^ bit) for i in range(n_dp)])]
    ppermute x6, starting transfers between devices: 8.17 us -> 11 us  [swap(): return lax.ppermute(x, 'dp', [(i, i ^ bit) for i in range(n_dp)])]
  transfers between devices with their start and end apart: 14 -> 14, of which waited for: 4 -> 4; matrix products, arithmetic and copies ran while one was open for 0% -> 0% of each run, Pallas kernels for 73% -> 74%
where the time goes in v8:
time: 185 us
  Pallas kernels  142 us (77%)
  starting transfers between devices  33.9 us (18%)
  waiting for transfers between devices  4.12 us (2%)
  local copies, waits for them, and re-layouts  2.1 us (1%)
    pallas_call x3, Pallas kernels, expert_call(): pl.pallas_call(functools.partial(expert_kernel, group, first, last, len(a...  95.6 us
    pallas_call x3, Pallas kernels, final_call(): pl.pallas_call(functools.partial(final_kernel, steps), grid=(steps,), in_...  29.4 us
    all_to_all x3, starting transfers between devices, spread_out(): return lax.all_to_all(x, 'fsdp', 0, 0, axis_index_groups=across)  13.7 us
    pallas_call x1, Pallas kernels, prep(): pl.pallas_call(prep_kernel, grid=(rows // TILE,), in_specs=[pl.BlockSpec(...  11.7 us
    ppermute x6, starting transfers between devices, swap(): return lax.ppermute(x, 'dp', [(i, i ^ bit) for i in range(n_dp)])  11 us
    all_to_all x1, starting transfers between devices, on_device(): sum1, token1 = total([lax.all_to_all(grads1, 'fsdp', 0, 0)], [done2])  4.21 us
    all_to_all x1, starting transfers between devices, on_device(): sum0, token0 = total([lax.all_to_all(grads0, 'fsdp', 0, 0)], [done1])  4.06 us
  transfers between devices with their start and end apart: 14, of which 4 were waited for; matrix products, arithmetic and copies ran while one was open for 0% of the time, Pallas kernels for 74%

profile of v8, /device:TPU:0, one launch (start us, length us, event | category | flops | bytes accessed | tf_op | source)
XLA Modules:
  0.0 184.9 jit_solution(1937064093355392958)
XLA Ops:
  0.7 2.2 %shard_map.196 = f32[4,232,256]{2,1,0:T(8,128)} custom-call(f32[6,32]{1,0:T(8,128)} %in_bias.1, f32[6,32]{1,0:T(8,128)} %refs_5_.1, f32[6,32]{1,0:T(8,128)} %refs_6_.1, f32[6,32]{1,0:T(8,128)} %out_bias.1, f32[2,4,64]{2,1,0:T(4,128)} %bitcast.11, f32[6,64]{1,0:T(8,128)} %bitcast.12, f32[6,64,256]{2,1,0:T(8,128)} %w_in_ref.3, f32[6,32,256]{2,1,0:T(8,128)} %refs_4_.1), custom_call_target="tpu_custom_call" | custom-call | tf_op jit(solution)/shard_map/pallas_call | solution.py:135
  2.8 5.2 %all-to-all-start.1 = ((f32[4,232,256]{2,1,0:T(8,128)}), f32[4,232,256]{2,1,0:T(8,128)}, u32[]{:S(2)}, u32[]{:S(2)}) async-start(f32[4,232,256]{2,1,0:T(8,128)} %shard_map.196), calls=%async_computation.1 | async-start | bytes 1900544 | tf_op jit(solution)/shard_map/all_to_all | solution.py:707
  9.2 11.7 %shard_map.195 = (bf16[528,3072]{1,0:T(8,128)(2,1)}, bf16[512,3072]{1,0:T(8,128)(2,1)}, f32[2,256,3072]{2,1,0:T(8,128)}, f32[4,384,256]{2,1,0:T(8,128)}, f32[8,128]{1,0:T(8,128)}) custom-call(f32[3072,512]{1,0:T(8,128)} %x_ref.1, f32[3,3072,256]{2,1,0:T(8,128)} %refs_8_.1, f32[3,3072,256]{2,1,0:T(8,128)} %refs_8_.1, f32[1,3072]{1,0:T(1,128)} %bitcast.9, ...), custom_call_target="tpu_custom_call" | custom-call | bytes 26000000 | tf_op jit(solution)/shard_map/pallas_call | solution.py:165
  21.2 4.4 %all-to-all-start = ((f32[4,384,256]{2,1,0:T(8,128)}), f32[4,384,256]{2,1,0:T(8,128)}, u32[]{:S(2)}, u32[]{:S(2)}) async-start(f32[4,384,256]{2,1,0:T(8,128)} %get-tuple-element.81), calls=%async_computation | async-start | bytes 3145728 | tf_op jit(solution)/shard_map/all_to_all | solution.py:707
  25.6 0.9 copy-done.6
  26.6 30.2 %shard_map.198 = (bf16[256,3072]{1,0:T(8,128)(2,1)}, bf16[256,3072]{1,0:T(8,128)(2,1)}, bf16[256,3072]{1,0:T(8,128)(2,1)}, bf16[256,3072]{1,0:T(8,128)(2,1)}, f3...) custom-call(s32[1]{0:T(128)} %bitcast.refs_0_, ...), custom_call_target="tpu_custom_call" | custom-call | flops 20000000000 | bytes 30000000 | tf_op jit(solution)/shard_map/pallas_call | solution.py:560
  57.4 4.1 %all-to-all-start.2 = ((f32[8,208,256]{2,1,0:T(8,128)}), f32[8,208,256]{2,1,0:T(8,128)S(1)}, u32[]{:S(2)}, u32[]{:S(2)}) async-start(f32[8,208,256]{2,1,0:T(8,128)} %get-tuple-element.96), calls=%async_computation.2 | async-start | bytes 3407872 | tf_op jit(solution)/shard_map/all_to_all | solution.py:754
  61.5 1.1 copy-done.5
  62.6 30.6 %shard_map.200 = (bf16[256,3072]{1,0:T(8,128)(2,1)}, bf16[256,3072]{1,0:T(8,128)(2,1)}, bf16[256,3072]{1,0:T(8,128)(2,1)}, bf16[256,3072]{1,0:T(8,128)(2,1)}, f3...) custom-call(s32[1]{0:T(128)} %bitcast.refs_0_, ...), custom_call_target="tpu_custom_call" | custom-call | flops 20000000000 | bytes 30000000 | tf_op jit(solution)/shard_map/pallas_call | solution.py:560
  93.2 4.2 %all-to-all-start.3 = ((f32[8,208,256]{2,1,0:T(8,128)}), f32[8,208,256]{2,1,0:T(8,128)S(1)}, u32[]{:S(2)}, u32[]{:S(2)}) async-start(f32[8,208,256]{2,1,0:T(8,128)} %get-tuple-element.121), calls=%async_computation.3 | async-start | bytes 3407872 | tf_op jit(solution)/shard_map/all_to_all | solution.py:774
  97.5 3.1 %collective-permute-start.3 = (f32[208,256]{1,0:T(8,128)S(1)}, f32[208,256]{1,0:T(8,128)S(1)}, u32[]{:S(2)}, u32[]{:S(2)}) collective-permute-start(f32[208,256]{1,0:T(8,128)S(1)} %get-tuple-element.128.refs_0_), channel_id=1, source_target_pairs={{0,16},{8,24},{16,0},{24,8},{1,17},{9,25},{17,1},{25,9},{2,18},{10... | collective-permute-start | bytes 638984 | tf_op jit(solution)/shard_map/ppermute | solution.py:710
  100.6 34.8 %shard_map.202 = (bf16[256,3072]{1,0:T(8,128)(2,1)}, bf16[256,3072]{1,0:T(8,128)(2,1)}, bf16[256,3072]{1,0:T(8,128)(2,1)}, bf16[256,3072]{1,0:T(8,128)(2,1)}, f3...) custom-call(s32[1]{0:T(128)} %bitcast.refs_0_, ...), custom_call_target="tpu_custom_call" | custom-call | flops 20000000000 | bytes 30000000 | tf_op jit(solution)/shard_map/pallas_call | solution.py:560
  135.8 2.5 %collective-permute-done.4 = f32[4,224,256]{2,1,0:T(8,128)S(1)} collective-permute-done((f32[4,224,256]{2,1,0:T(8,128)}, f32[4,224,256]{2,1,0:T(8,128)S(1)}, u32[]{:S(2)}, u32[]{:S(2)}) %collective-permute-start.4) | collective-permute-done | bytes 917536 | tf_op jit(solution)/shard_map/ppermute | solution.py:776
  138.3 1.1 add.8
  139.3 4.2 %all-to-all-start.4 = ((f32[4,224,256]{2,1,0:T(8,128)}), f32[4,224,256]{2,1,0:T(8,128)S(1)}, u32[]{:S(2)}, u32[]{:S(2)}) async-start(f32[4,224,256]{2,1,0:T(8,128)} %add.8), calls=%async_computation.4 | async-start | bytes 1835008 | tf_op jit(solution)/shard_map/all_to_all | solution.py:707
  143.6 9.8 %shard_map.203 = (f32[3072,512]{1,0:T(8,128)}, f32[8,128]{1,0:T(8,128)}) custom-call(bf16[256,3072]{1,0:T(8,128)(2,1)} %get-tuple-element.100.refs_0_, bf16[256,3072]{1,0:T(8,128)(2,1)} %get-tuple-element.101.refs_1_, bf16[256,3072]{1,0:T(8,128)(2,1)} %get-tuple-element.102.refs_2_, bf16[256,3072]{1,0:T(8,128)(2,1)} %get-tuple-element.103.refs_3_, ...), custom_call_target="tpu_custom_call" | custom-call | flops 5000000000 | bytes 8333333 | tf_op jit(solution)/shard_map/pallas_call | solution.py:611
  153.4 1.9 %collective-permute-start.5 = (f32[208,256]{1,0:T(8,128)S(1)}, f32[208,256]{1,0:T(8,128)S(1)}, u32[]{:S(2)}, u32[]{:S(2)}) collective-permute-start(f32[208,256]{1,0:T(8,128)S(1)} %get-tuple-element.133.refs_0_), channel_id=1, source_target_pairs={{0,8},{8,0},{16,24},{24,16},{1,9},{9,1},{17,25},{25,17},{2,10},{10... | collective-permute-start | bytes 638984 | tf_op jit(solution)/shard_map/ppermute | solution.py:710
  155.3 0.7 collective-permute-done.2.refs_1_
  156.2 2.3 %collective-permute-start.6 = (f32[224,256]{1,0:T(8,128)S(1)}, f32[224,256]{1,0:T(8,128)S(1)}, u32[]{:S(2)}, u32[]{:S(2)}) collective-permute-start(f32[224,256]{1,0:T(8,128)S(1)} %get-tuple-element.136.refs_0_), channel_id=1, source_target_pairs={{0,16},{8,24},{16,0},{24,8},{1,17},{9,25},{17,1},{25,9},{2,18},{10... | collective-permute-start | bytes 688136 | tf_op jit(solution)/shard_map/ppermute | solution.py:710
  158.5 9.8 %shard_map.209 = (f32[3072,512]{1,0:T(8,128)}, f32[8,128]{1,0:T(8,128)}) custom-call(bf16[256,3072]{1,0:T(8,128)(2,1)} %get-tuple-element.100.refs_0_, bf16[256,3072]{1,0:T(8,128)(2,1)} %get-tuple-element.101.refs_1_, bf16[256,3072]{1,0:T(8,128)(2,1)} %get-tuple-element.102.refs_2_, ...), custom_call_target="tpu_custom_call", output_to_operand_aliasing={{0}: (20, {})} | custom-call | flops 5000000000 | bytes 8333333 | tf_op jit(solution)/shard_map/pallas_call | solution.py:611
  168.4 0.7 collective-permute-done.6.refs_1_
  169.1 3.6 %collective-permute-start.8 = (f32[224,256]{1,0:T(8,128)S(1)}, f32[224,256]{1,0:T(8,128)S(1)}, u32[]{:S(2)}, u32[]{:S(2)}) collective-permute-start(f32[224,256]{1,0:T(8,128)S(1)} %get-tuple-element.143.refs_2_), channel_id=1, source_target_pairs={{0,8},{8,0},{16,24},{24,16},{1,9},{9,1},{17,25},{25,17},{2,10},{10... | collective-permute-start | bytes 688136 | tf_op jit(solution)/shard_map/ppermute | solution.py:710
  172.6 9.8 %shard_map.212 = (f32[3072,512]{1,0:T(8,128)}, f32[8,128]{1,0:T(8,128)}) custom-call(bf16[256,3072]{1,0:T(8,128)(2,1)} %get-tuple-element.100.refs_0_, bf16[256,3072]{1,0:T(8,128)(2,1)} %get-tuple-element.101.refs_1_, bf16[256,3072]{1,0:T(8,128)(2,1)} %get-tuple-element.102.refs_2_, ...), custom_call_target="tpu_custom_call", output_to_operand_aliasing={{0}: (20, {})} | custom-call | flops 5000000000 | bytes 8333333 | tf_op jit(solution)/shard_map/pallas_call | solution.py:611
  182.5 2.4 %shard_map.214 = (f32[6,64,256]{2,1,0:T(8,128)}, f32[6,32]{1,0:T(8,128)}, f32[6,32]{1,0:T(8,128)}, f32[6,32]{1,0:T(8,128)}, f32[6,32,256]{2,1,0:T(8,128)}, /*ind...) custom-call(s32[1]{0:T(128)} %bitcast.5.me_ref, f32[208,256]{1,0:T(8,128)S(1)} %get-tuple-element.139.refs_0_, ...), custom_call_target="tpu_custom_call" | custom-call | tf_op jit(solution)/shard_map/pallas_call | solution.py:690
  (40 shorter events, 2.2 us)
Async XLA Ops:
  0.6 8.0 %copy-start.4 = (s32[3072]{0:T(1024)S(1)}, s32[3072]{0:T(1024)}, u32[]{:S(2)}) copy-start(s32[3072]{0:T(1024)} %param.15) | copy-start | bytes 36868
  2.8 18.4 %all-to-all-start.1 = ((f32[4,232,256]{2,1,0:T(8,128)}), f32[4,232,256]{2,1,0:T(8,128)}, u32[]{:S(2)}, u32[]{:S(2)}) async-start(f32[4,232,256]{2,1,0:T(8,128)} %shard_map.196), calls=%async_computation.1 | async-start | bytes 1900544 | tf_op jit(solution)/shard_map/all_to_all | solution.py:707
  21.2 4.4 %collective-permute-start = (f32[4,232,256]{2,1,0:T(8,128)}, f32[4,232,256]{2,1,0:T(8,128)S(1)}, u32[]{:S(2)}, u32[]{:S(2)}) collective-permute-start(f32[4,232,256]{2,1,0:T(8,128)} %shard_map.197.refs_1_), channel_id=1, source_target_pairs={{0,1},{1,0},{2,3},{3,2},{4,5},{5,4},{6,7},{7,6},{8,9},{9,8},{10,11... | collective-permute-start | bytes 2850824 | tf_op jit(solution)/shard_map/ppermute | solution.py:737
  21.2 35.6 %all-to-all-start = ((f32[4,384,256]{2,1,0:T(8,128)}), f32[4,384,256]{2,1,0:T(8,128)}, u32[]{:S(2)}, u32[]{:S(2)}) async-start(f32[4,384,256]{2,1,0:T(8,128)} %get-tuple-element.81), calls=%async_computation | async-start | bytes 3145728 | tf_op jit(solution)/shard_map/all_to_all | solution.py:707
  25.6 1.0 copy-start.6
  56.8 4.6 %collective-permute-start.1 = (f32[4,384,256]{2,1,0:T(8,128)}, f32[4,384,256]{2,1,0:T(8,128)S(1)}, u32[]{:S(2)}, u32[]{:S(2)}) collective-permute-start(f32[4,384,256]{2,1,0:T(8,128)} %shard_map.199.refs_1_), channel_id=1, source_target_pairs={{0,1},{1,0},{2,3},{3,2},{4,5},{5,4},{6,7},{7,6},{8,9},{9,8},{10,11... | collective-permute-start | bytes 4718600 | tf_op jit(solution)/shard_map/ppermute | solution.py:748
  57.4 35.8 %all-to-all-start.2 = ((f32[8,208,256]{2,1,0:T(8,128)}), f32[8,208,256]{2,1,0:T(8,128)S(1)}, u32[]{:S(2)}, u32[]{:S(2)}) async-start(f32[8,208,256]{2,1,0:T(8,128)} %get-tuple-element.96), calls=%async_computation.2 | async-start | bytes 3407872 | tf_op jit(solution)/shard_map/all_to_all | solution.py:754
  61.4 1.1 copy-start.5
  93.2 42.2 %all-to-all-start.3 = ((f32[8,208,256]{2,1,0:T(8,128)}), f32[8,208,256]{2,1,0:T(8,128)S(1)}, u32[]{:S(2)}, u32[]{:S(2)}) async-start(f32[8,208,256]{2,1,0:T(8,128)} %get-tuple-element.121), calls=%async_computation.3 | async-start | bytes 3407872 | tf_op jit(solution)/shard_map/all_to_all | solution.py:774
  97.5 37.9 %collective-permute-start.3 = (f32[208,256]{1,0:T(8,128)S(1)}, f32[208,256]{1,0:T(8,128)S(1)}, u32[]{:S(2)}, u32[]{:S(2)}) collective-permute-start(f32[208,256]{1,0:T(8,128)S(1)} %get-tuple-element.128.refs_0_), channel_id=1, source_target_pairs={{0,16},{8,24},{16,0},{24,8},{1,17},{9,25},{17,1},{25,9},{2,18},{10... | collective-permute-start | bytes 638984 | tf_op jit(solution)/shard_map/ppermute | solution.py:710
  135.4 2.9 %copy-start.3 = (f32[4,224,256]{2,1,0:T(8,128)S(1)}, f32[4,224,256]{2,1,0:T(8,128)}, u32[]{:S(2)}) copy-start(f32[4,224,256]{2,1,0:T(8,128)} %get-tuple-element.126) | copy-start | bytes 2752516
  135.5 2.7 %collective-permute-start.4 = (f32[4,224,256]{2,1,0:T(8,128)}, f32[4,224,256]{2,1,0:T(8,128)S(1)}, u32[]{:S(2)}, u32[]{:S(2)}) collective-permute-start(f32[4,224,256]{2,1,0:T(8,128)} %shard_map.207), channel_id=1, source_target_pairs={{0,1},{1,0},{2,3},{3,2},{4,5},{5,4},{6,7},{7,6},{8,9},{9,8},{10,11... | collective-permute-start | bytes 2752520 | tf_op jit(solution)/shard_map/ppermute | solution.py:776
  139.3 16.8 %all-to-all-start.4 = ((f32[4,224,256]{2,1,0:T(8,128)}), f32[4,224,256]{2,1,0:T(8,128)S(1)}, u32[]{:S(2)}, u32[]{:S(2)}) async-start(f32[4,224,256]{2,1,0:T(8,128)} %add.8), calls=%async_computation.4 | async-start | bytes 1835008 | tf_op jit(solution)/shard_map/all_to_all | solution.py:707
  143.5 12.5 %collective-permute-start.2 = (f32[208,256]{1,0:T(8,128)S(1)}, f32[208,256]{1,0:T(8,128)S(1)}, u32[]{:S(2)}, u32[]{:S(2)}) collective-permute-start(f32[208,256]{1,0:T(8,128)S(1)} %get-tuple-element.123.refs_0_), channel_id=1, source_target_pairs={{0,16},{8,24},{16,0},{24,8},{1,17},{9,25},{17,1},{25,9},{2,18},{10... | collective-permute-start | bytes 638984 | tf_op jit(solution)/shard_map/ppermute | solution.py:710
  153.4 15.0 %collective-permute-start.5 = (f32[208,256]{1,0:T(8,128)S(1)}, f32[208,256]{1,0:T(8,128)S(1)}, u32[]{:S(2)}, u32[]{:S(2)}) collective-permute-start(f32[208,256]{1,0:T(8,128)S(1)} %get-tuple-element.133.refs_0_), channel_id=1, source_target_pairs={{0,8},{8,0},{16,24},{24,16},{1,9},{9,1},{17,25},{25,17},{2,10},{10... | collective-permute-start | bytes 638984 | tf_op jit(solution)/shard_map/ppermute | solution.py:710
  156.1 26.4 %collective-permute-start.7 = (f32[208,256]{1,0:T(8,128)S(1)}, f32[208,256]{1,0:T(8,128)S(1)}, u32[]{:S(2)}, u32[]{:S(2)}) collective-permute-start(f32[208,256]{1,0:T(8,128)S(1)} %get-tuple-element.140.refs_0_), channel_id=1, source_target_pairs={{0,8},{8,0},{16,24},{24,16},{1,9},{9,1},{17,25},{25,17},{2,10},{10... | collective-permute-start | bytes 638984 | tf_op jit(solution)/shard_map/ppermute | solution.py:710
  156.2 12.8 %collective-permute-start.6 = (f32[224,256]{1,0:T(8,128)S(1)}, f32[224,256]{1,0:T(8,128)S(1)}, u32[]{:S(2)}, u32[]{:S(2)}) collective-permute-start(f32[224,256]{1,0:T(8,128)S(1)} %get-tuple-element.136.refs_0_), channel_id=1, source_target_pairs={{0,16},{8,24},{16,0},{24,8},{1,17},{9,25},{17,1},{25,9},{2,18},{10... | collective-permute-start | bytes 688136 | tf_op jit(solution)/shard_map/ppermute | solution.py:710
  169.1 13.4 %collective-permute-start.8 = (f32[224,256]{1,0:T(8,128)S(1)}, f32[224,256]{1,0:T(8,128)S(1)}, u32[]{:S(2)}, u32[]{:S(2)}) collective-permute-start(f32[224,256]{1,0:T(8,128)S(1)} %get-tuple-element.143.refs_2_), channel_id=1, source_target_pairs={{0,8},{8,0},{16,24},{24,16},{1,9},{9,1},{17,25},{25,17},{2,10},{10... | collective-permute-start | bytes 688136 | tf_op jit(solution)/shard_map/ppermute | solution.py:710
  172.6 9.9 %copy-start = (f32[6,32,256]{2,1,0:T(8,128)S(1)}, f32[6,32,256]{2,1,0:T(8,128)}, u32[]{:S(2)}) copy-start(f32[6,32,256]{2,1,0:T(8,128)} %refs_4_.1) | copy-start | bytes 589828
  172.6 9.9 %copy-start.1 = (f32[6,32]{1,0:T(8,128)S(1)}, f32[6,32]{1,0:T(8,128)}, u32[]{:S(2)}) copy-start(f32[6,32]{1,0:T(8,128)} %refs_5_.1) | copy-start | bytes 2308
  172.6 9.9 %copy-start.2 = (f32[6,32]{1,0:T(8,128)S(1)}, f32[6,32]{1,0:T(8,128)}, u32[]{:S(2)}) copy-start(f32[6,32]{1,0:T(8,128)} %refs_6_.1) | copy-start | bytes 2308
